TPU v7x, 32 devices: a whole 2x2x4 slice. The times are simulated.
32 devices in a mesh: dp: 8 (over z, y), feat: 4 (over x, core).
Axes of the slice: x: 2, y: 2, z: 4, core: 2. Of those that a mesh axis runs over, the one named last changes fastest.
Arguments:
- fine_values: float32 [512, 8192], P('feat', 'dp'), may hold values from 0 to 1
- grad: bfloat16 [8192], P('dp'), may hold values from -6 to 6
- hess: bfloat16 [8192], P('dp'), may hold values from 0.0099487305 to 0.25
- slab_rows: int32 [8], replicated, may hold values from 256 to 1024, as said below
- split_feature: int32 [3], replicated, may hold values from 0 to 511
- split_bin: int32 [3], replicated, may hold values from 32 to 223
Outputs:
- gain: float32 [7, 512, 256], P(None, 'feat')
Inputs may be any that keep to these rules, and one draw needn't show every extreme that they name: `slab_rows`: each slab's used rows are its first ones; the fullest slab uses all 1024 slots.
All inputs are finite; a program needn't handle non-finite values.
Results may differ from a plain program's by a relative error of at most 0.0003.
Values sent between devices are 32-bit elements; how exact they have to be, the bound alone decides.
No kernel may reach another device: no remote copies, remote signals or barrier semaphores. Data moves between devices by JAX's collectives and lax.ppermute only.
A program may use at most 64 MiB of HBM per device.

v0:
```python
import math

import jax
import jax.numpy as jnp
from jax import lax
from jax.sharding import PartitionSpec as P

FINE_BINS = 1024
BINS = 256
LEVELS = 3
BLOCK = 512
NODES = 7
INNER = 3


penalty = 1.0


def fine_of(values_now):
    return jnp.clip(jnp.floor(values_now * FINE_BINS), 0, FINE_BINS - 1).astype(jnp.int32)


def quantile_cut(before, total):
    remainder = before
    quotient = jnp.zeros_like(before)
    for step_now in range(BINS.bit_length() - 1):
        remainder = remainder * 2
        bit_now = remainder >= total
        remainder = jnp.where(bit_now, remainder - total, remainder)
        quotient = quotient * 2 + bit_now.astype(jnp.int32)
    return jnp.minimum(BINS - 1, quotient)


def coarse_map(counts):
    whole_counts = (counts * 16384.0).astype(jnp.int32)
    before = jnp.cumsum(whole_counts, axis=1, dtype=jnp.int32) - whole_counts
    total = jnp.sum(whole_counts, axis=1, keepdims=True, dtype=jnp.int32)
    return quantile_cut(before, total)


def gains_of(full_hist):
    totals = jnp.sum(full_hist, axis=3, keepdims=True)
    left_sums = jnp.cumsum(full_hist, axis=3)
    rights = totals - left_sums

    def score_of(sums_part):
        return sums_part[:, 0] ** 2 / (sums_part[:, 1] + penalty)

    return score_of(left_sums) + score_of(rights) - score_of(totals)


def level_nodes(depth_now):
    first_node = 2**depth_now - 1
    node_count = 2**depth_now
    return list(range(first_node, first_node + node_count))


def count_block(fine_block, live_block, hess_block):
    side_len = math.isqrt(FINE_BINS)
    steps_side = jnp.arange(side_len, dtype=jnp.int32)
    upper_part = fine_block // side_len
    lower_part = fine_block % side_len
    upper_hot = (
        (upper_part[:, None, :] == steps_side[None, :, None]) & live_block[None, None, :]
    ).astype(jnp.bfloat16)
    upper_hot = upper_hot * hess_block[None, None, :]
    lower_hot = (lower_part[:, None, :] == steps_side[None, :, None]).astype(jnp.bfloat16)
    count_table = jnp.einsum(
        "fkr,fmr->fkm", upper_hot, lower_hot, preferred_element_type=jnp.float32
    )
    return count_table.reshape(fine_block.shape[0], FINE_BINS)


def lookup_block(fine_block, table_split):
    side_len = math.isqrt(FINE_BINS)
    steps_side = jnp.arange(side_len, dtype=jnp.int32)
    upper_hot = (fine_block[:, None, :] // side_len == steps_side[None, :, None]).astype(
        jnp.bfloat16
    )
    lower_mask = fine_block[:, None, :] % side_len == steps_side[None, :, None]
    middle = jnp.einsum("fum,fur->fmr", table_split, upper_hot, preferred_element_type=jnp.float32)
    return jnp.sum(jnp.where(lower_mask, middle, 0.0), axis=1).astype(jnp.int32)


def grad_block(coarse_block, node_blocks, pair_block, node_lists):
    side_len = math.isqrt(BINS)
    steps_side = jnp.arange(side_len, dtype=jnp.int32)
    feat_dev = coarse_block.shape[0]
    rows_block = coarse_block.shape[1]
    upper_part = coarse_block // side_len
    lower_part = coarse_block % side_len
    member_rows = jnp.stack(
        [
            node_blocks[depth_now] == node_id
            for depth_now in range(len(node_lists))
            for node_id in node_lists[depth_now]
        ]
    )
    width_all = member_rows.shape[0]
    upper_hot = upper_part[:, None, :] == steps_side[None, :, None]
    left_hot = (member_rows[None, :, None, :] & upper_hot[:, None, :, :]).astype(jnp.bfloat16)
    left_hot = left_hot.reshape(feat_dev, width_all * side_len, rows_block)
    lower_hot = (lower_part[:, None, :] == steps_side[None, :, None]).astype(jnp.bfloat16)
    right_side = (lower_hot[:, :, None, :] * pair_block[None, None, :, :]).reshape(
        feat_dev, side_len * 2, rows_block
    )
    table_now = jnp.einsum("fkr,fmr->fkm", left_hot, right_side, preferred_element_type=jnp.float32)
    table_now = table_now.reshape(feat_dev, width_all, side_len, side_len, 2)
    table_now = jnp.transpose(table_now, (1, 4, 0, 2, 3))
    return table_now.reshape(width_all, 2, feat_dev, BINS)


def complete(partials, node_lists):
    position = {}
    flat_nodes = [node_id for nodes_now in node_lists for node_id in nodes_now]
    for index_now in range(len(flat_nodes)):
        position[flat_nodes[index_now]] = index_now
    full_hist = []
    for node_id in range(NODES):
        full_hist.append(partials[position[node_id]])
    return jnp.stack(full_hist)


def shards(fine_values, grad, hess, slab_rows, split_feature, split_bin):
    feat_dev = fine_values.shape[0]
    row_dev = fine_values.shape[1]
    pair_rows = jnp.stack([grad, hess])
    buffers = [(fine_values, pair_rows, jnp.int32(0), slab_rows[lax.axis_index("dp")])]
    buffers = [
        (
            buffer_now[0],
            buffer_now[1],
            jnp.asarray(buffer_now[2], jnp.int32),
            jnp.asarray(buffer_now[3], jnp.int32),
        )
        for buffer_now in buffers
    ]
    row_ids = jnp.arange(row_dev, dtype=jnp.int32)
    fine_list = [fine_of(buffer_now[0]) for buffer_now in buffers]
    counts = jnp.zeros((feat_dev, FINE_BINS), jnp.float32)
    index_now = 0
    buffer_now = buffers[index_now]

    def add_counts(
        block_index,
        running,
        fine_now=fine_list[index_now],
        pairs_now=buffer_now[1],
        start_row=buffer_now[2],
        stop_row=buffer_now[3],
    ):
        first_row = block_index * BLOCK
        fine_block = lax.dynamic_slice_in_dim(fine_now, first_row, BLOCK, 1)
        hess_block = lax.dynamic_slice_in_dim(pairs_now[1], first_row, BLOCK, 0)
        rows_block = first_row + jnp.arange(BLOCK, dtype=jnp.int32)
        live_block = (rows_block >= start_row) & (rows_block < stop_row)
        return running + count_block(fine_block, live_block, hess_block)

    counts = lax.fori_loop(
        buffer_now[2] // BLOCK, (buffer_now[3] + BLOCK - 1) // BLOCK, add_counts, counts
    )
    counts = lax.psum(counts, "dp")
    map_table = coarse_map(counts)
    side_fine = math.isqrt(FINE_BINS)
    table_split = map_table.reshape(feat_dev, side_fine, side_fine).astype(jnp.bfloat16)
    offset = lax.axis_index("feat") * feat_dev
    inner_ids = jnp.arange(INNER, dtype=jnp.int32)
    node_now = [
        jnp.where((row_ids >= buffer_now[2]) & (row_ids < buffer_now[3]), 0, -1).astype(jnp.int32)
        for buffer_now in buffers
    ]
    node_levels = [node_now]
    for depth_now in range(1, LEVELS):
        index_now = 0
        nodes_row = node_now[index_now]
        member = nodes_row[None, :] == inner_ids[:, None]
        chosen = jnp.sum(jnp.where(member, split_feature[:, None], 0), 0) - offset
        bound_row = jnp.sum(jnp.where(member, split_bin[:, None], 0), 0)
        is_owned = (chosen >= 0) & (chosen < feat_dev)
        safe_feature = jnp.clip(chosen, 0, feat_dev - 1)
        picked_fine = jnp.take_along_axis(fine_list[index_now], safe_feature[None, :], 0)[0]
        picked = map_table[safe_feature, picked_fine]
        left_bits = jnp.where(is_owned & (picked <= bound_row), 1, 0).astype(jnp.int32)
        went_left = lax.pmax(left_bits, "feat")
        index_now = 0
        nodes_row = node_now[index_now]
        next_nodes = [jnp.where(nodes_row >= 0, 2 * nodes_row + 2 - went_left, -1)]
        node_now = next_nodes
        node_levels.append(node_now)
    node_lists = [level_nodes(depth_now) for depth_now in range(LEVELS)]
    width_all = sum((len(nodes_now) for nodes_now in node_lists))
    partials = jnp.zeros((width_all, 2, feat_dev, BINS), jnp.float32)
    index_now = 0
    buffer_now = buffers[index_now]
    level_rows = [node_levels[depth_now][index_now] for depth_now in range(LEVELS)]

    def add_hist(
        block_index,
        running,
        fine_now=fine_list[index_now],
        pairs_now=buffer_now[1],
        level_rows=level_rows,
    ):
        first_row = block_index * BLOCK
        fine_block = lax.dynamic_slice_in_dim(fine_now, first_row, BLOCK, 1)
        coarse_block = lookup_block(fine_block, table_split)
        pair_block = lax.dynamic_slice_in_dim(pairs_now, first_row, BLOCK, 1)
        node_blocks = [
            lax.dynamic_slice_in_dim(rows_now, first_row, BLOCK, 0) for rows_now in level_rows
        ]
        return running + grad_block(coarse_block, node_blocks, pair_block, node_lists)

    partials = lax.fori_loop(
        buffer_now[2] // BLOCK, (buffer_now[3] + BLOCK - 1) // BLOCK, add_hist, partials
    )
    summed = lax.psum(partials, "dp")
    return gains_of(complete(summed, node_lists))


def solution(mesh):
    return jax.shard_map(
        shards,
        mesh=mesh,
        in_specs=(P("feat", "dp"), P("dp"), P("dp"), P(), P(), P()),
        out_specs=P(None, "feat", None),
        check_vma=False,
    )
```

profile of v0, /device:TPU:0, one launch (start us, length us, event | category | flops | bytes accessed | tf_op | source)
XLA Modules:
  0.0 357.5 jit_solution(2928200202572735942)
XLA Ops:
  6.5 1.3 dynamic_slice.50
  8.6 1.1 clamp_convert_fusion
  9.7 0.8 max.16.clone
  10.6 14.7 %while.25 = (s32[]{:T(128)}, f32[128,1024]{0,1:T(8,128)}, s32[]{:T(128)}, s32[128,1024]{1,0:T(8,128)S(1)}, s32[]{:T(128)}, /*index=5*/bf16[1024]{0:T(1024)(128)(2,1)}, s32[]{:T(128)}, s32[]{:T(128)}, s32[]{:T(128)}, s32[]{:T(128)}) while((s32[]{:T(128)}, f32[128,1024]{0,1:T(8,128)}, s32[]{:T(128)}, s32[128,1024]{1,0:T(8,128)S(1)}, s32[]{:T(128)}, ...), condition=%wide.region_1.2_spmd, body=%wide.region_0.1_spmd.sunk | while | flops 144377856 | bytes 4853927 | solution.py:159
  10.6 0.7 fusion.92
  11.3 0.8 dynamic_slice.101
  12.4 2.4 fusion.93
  14.8 1.3 copy.62
  16.0 1.9 bitcast_add_fusion.4
  17.9 0.7 fusion.92
  18.6 0.8 dynamic_slice.101
  19.7 2.4 fusion.93
  22.1 1.3 copy.62
  23.4 1.9 bitcast_add_fusion.4
  25.3 2.1 copy.41
  27.4 0.7 fusion.73
  28.1 0.7 stack.68
  29.0 8.6 %gather_fusion.2 = s32[1024]{0:T(1024)S(1)} fusion(s32[128,1024]{1,0:T(8,128)S(1)} %get-tuple-element.541, s32[1024]{0:T(1024)S(1)} %bitcast.77), kind=kCustom, calls=%fused_computation.clone | custom fusion | bytes 16384 | tf_op jit(solution)/shard_map/jit(take_along_axis)/gather | solution.py:181
  37.7 64.9 %all-reduce.3.cloned.1.call-done = f32[128,1024]{1,0:T(8,128)} async-done(((f32[128,1024]{1,0:T(8,128)}), f32[128,1024]{1,0:T(8,128)}) %all-reduce.3.cloned.1.call-update) | async-done | bytes 524304 | tf_op jit(solution)/shard_map/psum | solution.py:162
  102.6 1.1 convert_bitcast_fusion
  103.8 0.3 copy.42
  104.1 23.3 %fusion.79 = s32[128,8,128]{0,1,2:T(8,128)S(1)} fusion(s32[128,8,128]{0,1,2:T(8,128)S(1)} %copy.42), kind=kOutput, calls=%fused_computation.179 | output fusion | flops 16646144 | bytes 1048576 | tf_op jit(solution)/shard_map/reduce-window
  128.0 1.1 fusion.77
  129.2 8.6 %gather_fusion = s32[1024]{0:T(1024)S(1)} fusion(s32[128,1024]{1,0:T(8,128)S(1)} %get-tuple-element.334, s32[1024]{0:T(1024)S(1)} %bitcast.79), kind=kCustom, calls=%fused_computation.2 | custom fusion | bytes 16384 | tf_op jit(solution)/shard_map/gather | solution.py:182
  137.8 4.9 %pmax.14 = s32[1024]{0:T(1024)S(1)} all-reduce(s32[1024]{0:T(1024)S(1)} %and_select_fusion.3), channel_id=1, replica_groups=mesh['dp'=8,'feat'=4] {'feat'}, use_global_device_ids=true, to_apply=%region_8.10 | all-reduce | flops 1024 | bytes 8192 | tf_op jit(solution)/shard_map/pmax | solution.py:184
  142.7 0.7 subtract_select_fusion.8
  143.6 8.6 %gather_fusion.3 = s32[1024]{0:T(1024)S(1)} fusion(s32[128,1024]{1,0:T(8,128)S(1)} %get-tuple-element.541, s32[1024]{0:T(1024)S(1)} %bitcast.78), kind=kCustom, calls=%fused_computation.1.clone | custom fusion | bytes 16384 | tf_op jit(solution)/shard_map/jit(take_along_axis)/gather | solution.py:181
  152.3 8.6 %gather_fusion.1 = s32[1024]{0:T(1024)S(1)} fusion(s32[128,1024]{1,0:T(8,128)S(1)} %get-tuple-element.334, s32[1024]{0:T(1024)S(1)} %bitcast.80), kind=kCustom, calls=%fused_computation.3 | custom fusion | bytes 16384 | tf_op jit(solution)/shard_map/gather | solution.py:182
  160.9 4.3 %pmax.15 = s32[1024]{0:T(1024)S(1)} all-reduce(s32[1024]{0:T(1024)S(1)} %and_select_fusion.2), channel_id=1, replica_groups=mesh['dp'=8,'feat'=4] {'feat'}, use_global_device_ids=true, to_apply=%region_11.13 | all-reduce | flops 1024 | bytes 8192 | tf_op jit(solution)/shard_map/pmax | solution.py:184
  165.2 0.7 subtract_select_fusion.7
  165.9 1.6 copy.46
  167.5 1.4 broadcast_in_dim.92
  168.9 79.4 %while.26 = (s32[]{:T(128)}, f32[7,2,128,256]{2,3,1,0:T(8,128)}, s32[]{:T(128)}, s32[1024]{0:T(1024)S(1)}, s32[1024]{0:T(1024)S(1)}, /*index=5*/s32[1024]{0:T(10...) while((s32[]{:T(128)}, f32[7,2,128,256]{2,3,1,0:T(8,128)}, ...), condition=%wide.region_14.16_spmd, body=%wide.region_12.15_spmd.sunk | while | flops 628297216 | bytes 70927608 | solution.py:213
  169.6 3.0 fusion.97
  172.6 0.2 add_select_fusion.15
  172.9 1.3 iota_compare_fusion.18
  174.2 4.2 %mul.375 = bf16[128,16,2,512]{3,2,1,0:T(2,128)(2,1)} broadcast(bf16[128,16,512]{2,1,0:T(8,128)(2,1)S(1)} %get-tuple-element.469), dimensions={0,1,3} | broadcast | bytes 6291456 | tf_op jit(solution)/shard_map/while/body/mul | solution.py:104
  178.4 7.2 %mul.376 = bf16[128,32,512]{2,1,0:T(8,128)(2,1)} reshape(bf16[128,16,2,512]{3,2,1,0:T(2,128)(2,1)} %mul.375) | data formatting | bytes 8388608 | tf_op jit(solution)/shard_map/while/body/mul | solution.py:104
  185.7 6.7 %bitcast_and_fusion.2 = pred[128,112,512]{2,1,0:T(8,128)(4,1)} fusion(pred[128,16,512]{2,1,0:T(8,128)(4,1)S(1)} %get-tuple-element.461, pred[112,512]{1,0:T(8,128)(4,1)S(1)} %bitcast.83), kind=kLoop, calls=%fused_computation.29.clone.1 | loop fusion | flops 7340032 | bytes 8445952 | tf_op jit(solution)/shard_map/while/body/and | solution.py:101
  192.4 11.1 %fusion.98 = f32[128,112,32]{1,2,0:T(8,128)} fusion(pred[128,112,512]{2,1,0:T(8,128)(4,1)} %bitcast_and_fusion.2, bf16[128,32,512]{2,1,0:T(8,128)(2,1)} %mul.376, bf16[32,512]{1,0:T(8,128)(2,1)S(1)} %mul.378), kind=kOutput, calls=%fused_computation.35.clone.1 | convolution fusion | flops 471859200 | bytes 13402112 | tf_op jit(solution)/shard_map/while/body/fkr,fmr->fkm/dot_general | solution.py:107
  203.4 2.1 copy.63
  205.5 1.1 copy.64
  206.6 0.4 copy-done
  207.0 0.4 bitcast_add_fusion.5
  207.4 1.2 copy-done.1
  209.3 3.0 fusion.97
  212.3 0.2 add_select_fusion.15
  212.6 1.3 iota_compare_fusion.18
  213.9 4.2 %mul.375 = bf16[128,16,2,512]{3,2,1,0:T(2,128)(2,1)} broadcast(bf16[128,16,512]{2,1,0:T(8,128)(2,1)S(1)} %get-tuple-element.469), dimensions={0,1,3} | broadcast | bytes 6291456 | tf_op jit(solution)/shard_map/while/body/mul | solution.py:104
  218.1 7.2 %mul.376 = bf16[128,32,512]{2,1,0:T(8,128)(2,1)} reshape(bf16[128,16,2,512]{3,2,1,0:T(2,128)(2,1)} %mul.375) | data formatting | bytes 8388608 | tf_op jit(solution)/shard_map/while/body/mul | solution.py:104
  225.4 6.7 %bitcast_and_fusion.2 = pred[128,112,512]{2,1,0:T(8,128)(4,1)} fusion(pred[128,16,512]{2,1,0:T(8,128)(4,1)S(1)} %get-tuple-element.461, pred[112,512]{1,0:T(8,128)(4,1)S(1)} %bitcast.83), kind=kLoop, calls=%fused_computation.29.clone.1 | loop fusion | flops 7340032 | bytes 8445952 | tf_op jit(solution)/shard_map/while/body/and | solution.py:101
  232.1 11.1 %fusion.98 = f32[128,112,32]{1,2,0:T(8,128)} fusion(pred[128,112,512]{2,1,0:T(8,128)(4,1)} %bitcast_and_fusion.2, bf16[128,32,512]{2,1,0:T(8,128)(2,1)} %mul.376, bf16[32,512]{1,0:T(8,128)(2,1)S(1)} %mul.378), kind=kOutput, calls=%fused_computation.35.clone.1 | convolution fusion | flops 471859200 | bytes 13402112 | tf_op jit(solution)/shard_map/while/body/fkr,fmr->fkm/dot_general | solution.py:107
  243.1 2.1 copy.63
  245.2 1.1 copy.64
  246.3 0.4 copy-done
  246.7 0.4 bitcast_add_fusion.5
  247.1 1.2 copy-done.1
  248.4 94.9 %all-reduce.5.cloned.1.call-done = f32[7,2,128,256]{2,3,1,0:T(8,128)} async-done(((f32[7,2,128,256]{2,3,1,0:T(8,128)}), f32[7,2,128,256]{2,3,1,0:T(8,128)}) %all-reduce.5.cloned.1.call-update) | async-done | bytes 1835024 | tf_op jit(solution)/shard_map/psum | solution.py:216
  343.2 1.6 reduce_sum.72
  344.9 2.9 fusion.26
  347.9 0.8 broadcast_add_fusion
  348.7 0.2 copy.48
  349.1 0.3 fusion.31
  349.4 1.2 copy.49
  (84 shorter events, 3.4 us)
Async XLA Ops:
  6.5 96.0 %all-reduce.3.cloned.1.call-start = ((), (), s32[]{:S(2)}) async-start(), calls=%async_computation | async-start | bytes 1048576 | tf_op jit(solution)/shard_map/psum | solution.py:162
  10.6 18.2 %copy-start.3 = (bf16[1024]{0:T(1024)(128)(2,1)S(1)}, bf16[1024]{0:T(1024)(128)(2,1)}, u32[]{:S(2)}) copy-start(bf16[1024]{0:T(1024)(128)(2,1)} %param.13) | copy-start | bytes 6148
  10.6 18.2 %copy-start.4 = (s32[3]{0:T(128)S(1)}, s32[3]{0:T(128)}, u32[]{:S(2)}) copy-start(s32[3]{0:T(128)} %param.17) | copy-start | bytes 40
  10.6 18.3 %copy-start.5 = (s32[3]{0:T(128)S(1)}, s32[3]{0:T(128)}, u32[]{:S(2)}) copy-start(s32[3]{0:T(128)} %param.16) | copy-start | bytes 40
  27.3 315.9 %all-reduce.5.cloned.1.call-start = ((), (), s32[]{:S(2)}) async-start(), calls=%async_computation.1 | async-start | bytes 3670016 | tf_op jit(solution)/shard_map/psum | solution.py:216
  104.1 23.7 %copy-start.2 = (f32[128,1024]{1,0:T(8,128)S(1)}, f32[128,1024]{1,0:T(8,128)}, u32[]{:S(2)}) copy-start(f32[128,1024]{1,0:T(8,128)} %all-reduce.3.cloned.1.call-done) | copy-start | bytes 1572868
  205.5 1.5 copy-start
  207.4 1.2 copy-start.1
  245.2 1.5 copy-start
  247.1 1.2 copy-start.1
Sparse Core Ops, SparseCore 0:
  27.5 75.0 all-reduce.2
  248.5 94.7 all-reduce.4
where the time goes:
time: 358 us; the launch traced here: 357 us
  waiting for transfers between devices  160 us (45%)
  local copies, waits for them, and re-layouts  81.6 us (23%)
  other arithmetic  59.1 us (17%)
  matrix products  33 us (9%)
  between operations  14.5 us (4%)
  blocking collectives  9.22 us (3%)
    psum x1, waiting for transfers between devices, shards(): summed = lax.psum(partials, 'dp')  94.9 us
    psum x1, waiting for transfers between devices, shards(): counts = lax.psum(counts, 'dp')  64.9 us
    another operation x6, other arithmetic  27.1 us
    mul x8, local copies, waits for them, and re-layouts, grad_block(): lower_hot[:, :, None, :] * pair_block[None, None, :, :]  23 us
    dot_general x2, matrix products, grad_block(): jnp.einsum('fkr,fmr->fkm', left_hot, right_side, preferred_element_type=j...  22.2 us
    gather x2, local copies, waits for them, and re-layouts, shards(): jnp.take_along_axis(fine_list[index_now], safe_feature[None, :], 0)[0]  17.3 us
    gather x2, local copies, waits for them, and re-layouts, shards(): picked = map_table[safe_feature, picked_fine]  17.2 us
    and x2, other arithmetic, grad_block(): member_rows[None, :, None, :] & upper_hot[:, None, :, :]  13.4 us
  transfers between devices with their start and end apart: 2, of which 2 were waited for; matrix products, arithmetic and copies ran while one was open for 3% of the time, Pallas kernels for 0%

commit v1 on v0

v1 whole, which is shorter than its diff:
```python
import jax
import jax.numpy as jnp
from jax import lax
from jax.experimental import pallas as pl
from jax.experimental.pallas import tpu as pltpu
from jax.sharding import PartitionSpec as P

FINE_BINS=1024; BINS=256; HI=8; LO=128; CHUNK=256
f32=jnp.float32; bf16=jnp.bfloat16; i32=jnp.int32

def dot_nt(a,b):
    return lax.dot_general(a,b,(((1,),(1,)),((),())),preferred_element_type=f32)

def running_sum(whole):
    n=whole.shape[0]
    lane=lax.broadcasted_iota(i32,(n,LO),1)
    sub=lax.broadcasted_iota(i32,(n,LO),0)%HI
    x=whole
    for s in (1,2,4,8,16,32,64):
        x=x+jnp.where(lane>=s,pltpu.roll(x,s,1),0)
    tot=jnp.broadcast_to(x[:,LO-1:LO],(n,LO))
    y=tot
    for s in (1,2,4):
        y=y+jnp.where(sub>=s,pltpu.roll(y,s,0),0)
    return x+(y-tot), y

def coarse_of(whole):
    n=whole.shape[0]
    incl,rows=running_sum(whole)
    before=incl-whole
    g=rows.reshape(n//HI,HI,LO)
    total=jnp.broadcast_to(g[:,HI-1:HI,:],(n//HI,HI,LO)).reshape(n,LO)
    rem=before; quo=jnp.zeros_like(before)
    for _ in range(8):
        rem=rem*2
        bit=rem>=total
        rem=jnp.where(bit,rem-total,rem)
        quo=quo*2+bit.astype(i32)
    return jnp.minimum(BINS-1,quo)

def parts_of(v):
    t=jnp.clip(jnp.floor(v*FINE_BINS),0,FINE_BINS-1)
    hi=jnp.floor(t*(1.0/LO))
    return t,hi,t-hi*LO

def make_kernel(n_dp,feats,row_dev):
  def kernel(slab_rows,split_bin,order,x_ref,s_ref,o_ref,acc_ref,cum_ref):
    sub16=lax.broadcasted_iota(i32,(16,CHUNK),0)
    k16=(sub16%HI).astype(f32).astype(bf16)
    m16=[(sub16+16*j).astype(f32).astype(bf16) for j in range(LO//16)]
    one=jnp.ones((16,CHUNK),bf16); zero=jnp.zeros((16,CHUNK),bf16)
    def lower_hot(lo_row):
        lb=jnp.broadcast_to(lo_row,(16,CHUNK)).astype(bf16)
        return jnp.concatenate([jnp.where(lb==m,one,zero) for m in m16],0)
    def chunks(s):
        return (slab_rows[s]+CHUNK-1)//CHUNK
    cnt=tuple(jnp.zeros((HI,LO),f32) for _ in range(3))
    for s in range(n_dp):
        def body(q,cnt,s=s):
            r0=pl.multiple_of(q*CHUNK,CHUNK)
            rows=s_ref[order[s],:,pl.ds(r0,CHUNK)]
            live=lax.broadcasted_iota(i32,(1,CHUNK),1)+r0<slab_rows[s]
            h=jnp.where(live,rows[1:2],0.0)
            hb=jnp.broadcast_to(h,(16,CHUNK)).astype(bf16)
            t,hi,lo=parts_of(rows)
            out=[]
            for n in range(3):
                kb=jnp.broadcast_to(hi[2+n:3+n],(16,CHUNK)).astype(bf16)
                a=jnp.where(kb==k16,hb,zero)
                out.append(cnt[n]+dot_nt(a,lower_hot(lo[2+n:3+n]))[:HI])
            return tuple(out)
        cnt=lax.fori_loop(0,chunks(s),body,cnt)
    whole=(jnp.concatenate(cnt,0)*16384.0).astype(i32)
    cut=coarse_of(whole)
    thr=[]
    for n in range(3):
        left=(cut[n*HI:(n+1)*HI]<=split_bin[n]).astype(f32)
        thr.append(jnp.sum(jnp.sum(left,axis=0,keepdims=True),axis=1,keepdims=True))
    acc_ref[...]=jnp.zeros_like(acc_ref)
    sub8=lax.broadcasted_iota(i32,(8,CHUNK),0)
    for s in range(n_dp):
        def body(q,_,s=s):
            r0=pl.multiple_of(q*CHUNK,CHUNK)
            rows=s_ref[order[s],:,pl.ds(r0,CHUNK)]
            live=lax.broadcasted_iota(i32,(1,CHUNK),1)+r0<slab_rows[s]
            g=jnp.where(live,rows[0:1],0.0); h=jnp.where(live,rows[1:2],0.0)
            t,_,_=parts_of(rows)
            l0=t[2:3]<thr[0]; l1=t[3:4]<thr[1]; l2=t[4:5]<thr[2]
            leaf=jnp.where(l0,jnp.where(l1,0,1),jnp.where(l2,2,3))
            gh=jnp.where(sub8<4,jnp.broadcast_to(g,(8,CHUNK)),jnp.broadcast_to(h,(8,CHUNK)))
            ch=jnp.where((sub8%4)==jnp.broadcast_to(leaf,(8,CHUNK)),gh,0.0)
            ch2=jnp.concatenate([ch,ch],0).astype(bf16)
            x=x_ref[s,:,pl.ds(r0,CHUNK)]
            _,hi,lo=parts_of(x)
            kk=[(sub16//8+2*j).astype(f32).astype(bf16) for j in range(4)]
            for f in range(feats):
                hb=jnp.broadcast_to(hi[f:f+1],(16,CHUNK)).astype(bf16)
                a=jnp.concatenate([jnp.where(hb==kk[j],ch2,zero) for j in range(4)],0)
                acc_ref[f]+=dot_nt(a,lower_hot(lo[f:f+1]))
            return 0
        lax.fori_loop(0,chunks(s),body,0)
    acc=acc_ref[...].reshape(feats*HI,8,LO)
    is_h=lax.broadcasted_iota(i32,(feats*HI,8,LO),1)>=4
    cnts=jnp.sum(jnp.where(is_h,acc,0.0),axis=1)
    cut=coarse_of((cnts*16384.0).astype(i32)).astype(f32)
    b16=lax.broadcasted_iota(i32,(16,LO),0)
    one2=jnp.ones((16,LO),bf16); zero2=jnp.zeros((16,LO),bf16)
    bs=[(b16+16*j).astype(f32).astype(bf16) for j in range(BINS//16)]
    for f in range(feats):
        left=[];right=[]
        for k in range(HI):
            fk=acc_ref[f,k*8:(k+1)*8,:]
            p0=fk.astype(bf16); r1=fk-p0.astype(f32); p1=r1.astype(bf16); p2=(r1-p1.astype(f32)).astype(bf16)
            left.append(jnp.concatenate([p0.astype(f32),p1.astype(f32),p2.astype(f32),jnp.zeros((8,LO),f32)],0).astype(bf16))
            cb=jnp.broadcast_to(cut[f*HI+k:f*HI+k+1],(16,LO)).astype(bf16)
            right.append(jnp.concatenate([jnp.where(cb<=b,one2,zero2) for b in bs],0))
        r=dot_nt(jnp.concatenate(left,1),jnp.concatenate(right,1))
        gl=(r[0:8]+r[8:16])+r[16:24]
        for c in range(8):
            cum_ref[c,f:f+1,:]=gl[c:c+1]
    def score(g,h):
        return g*g/(h+1.0)
    gs=[cum_ref[c] for c in range(4)]; hs=[cum_ref[4+c] for c in range(4)]
    def nodes(l):
        a=l[0]+l[1]; b=l[2]+l[3]
        return [a+b,a,b]+l
    for n,(gl,hl) in enumerate(zip(nodes(gs),nodes(hs))):
        gt=gl[:,BINS-1:BINS]; ht=hl[:,BINS-1:BINS]
        o_ref[n]=score(gl,hl)+score(gt-gl,ht-hl)-score(gt,ht)
  return kernel

def histogram_gains(x,s,slab_rows,split_bin,order):
    n_dp,feats,row_dev=x.shape
    smem=pl.BlockSpec(memory_space=pltpu.SMEM); vm=pl.BlockSpec(memory_space=pltpu.VMEM)
    return pl.pallas_call(make_kernel(n_dp,feats,row_dev),
      out_shape=jax.ShapeDtypeStruct((7,feats,BINS),f32),
      in_specs=[smem,smem,smem,vm,vm],out_specs=vm,
      scratch_shapes=[pltpu.VMEM((feats,64,LO),f32),pltpu.VMEM((8,feats,BINS),f32)],
      compiler_params=pltpu.CompilerParams(vmem_limit_bytes=32*2**20),
      name="gains")(slab_rows,split_bin,order,x,s)


def swap(value, axis, size, step):
    return lax.ppermute(value, axis, [(s, s ^ step) for s in range(size)])


def make_shards(n_dp, n_feat):
    def shards(fine_values, grad, hess, slab_rows, split_feature, split_bin):
        feat_dev, row_dev = fine_values.shape
        feats = feat_dev // n_dp
        me = lax.axis_index("dp")
        local = split_feature - lax.axis_index("feat") * feat_dev
        owned = (local >= 0) & (local < feat_dev)
        at = jnp.clip(local, 0, feat_dev - 1)
        picked = jnp.concatenate([lax.dynamic_slice_in_dim(fine_values, at[n], 1, 0) for n in range(3)])
        picked = jnp.where(owned[:, None], picked, 0.0)
        step = 1
        while step < n_feat:
            picked = picked + swap(picked, "feat", n_feat, step)
            step *= 2
        rows = jnp.concatenate([grad.astype(f32)[None], hess.astype(f32)[None], picked, jnp.zeros((3, row_dev), f32)])[None]
        step = 1
        while step < n_dp:
            rows = jnp.concatenate([rows, swap(rows, "dp", n_dp, step)])
            step *= 2
        blocks = lax.all_to_all(fine_values.reshape(n_dp, feats, row_dev), "dp", 0, 0)
        order = jnp.arange(n_dp, dtype=i32) ^ me
        gains = histogram_gains(blocks, rows, slab_rows, split_bin, order)
        whole = jnp.zeros((7, feat_dev, BINS), f32)
        for d in range(n_dp):
            piece = gains if d == 0 else swap(gains, "dp", n_dp, d)
            whole = lax.dynamic_update_slice_in_dim(whole, piece, (me ^ d) * feats, 1)
        return whole

    return shards


def solution(mesh):
    return jax.shard_map(
        make_shards(mesh.shape["dp"], mesh.shape["feat"]),
        mesh=mesh,
        in_specs=(P("feat", "dp"), P("dp"), P("dp"), P(), P(), P()),
        out_specs=P(None, "feat", None),
        check_vma=False,
    )
```

time: 358 us -> 87.2 us (0.24)
  waiting for transfers between devices: 160 us -> 25.6 us
  local copies, waits for them, and re-layouts: 81.6 us -> 4.57 us
  other arithmetic: 59.1 us -> 0.3 us
  matrix products: 33 us -> 0 us
  starting transfers between devices: 0.04 us -> 26 us
  Pallas kernels: 0 us -> 23.7 us
  blocking collectives: 9.22 us -> 0 us
  between operations: 14.5 us -> 5.89 us
    psum x2 -> x0, waiting for transfers between devices: 160 us -> none  [the longest x1 94.9 us: shards(): summed = lax.psum(partials, 'dp')]
    gather x4 -> x0, local copies, waits for them, and re-layouts: 34.5 us -> none  [the longest x2 17.3 us: shards(): jnp.take_along_axis(fine_list[index_now], safe_feature[None, :], 0)[0]]
    dot_general x6 -> x0, matrix products: 33 us -> none  [the longest x2 22.2 us: grad_block(): jnp.einsum('fkr,fmr->fkm', left_hot, right_side, preferred_element_type=j...]
    another operation x7 -> x0, other arithmetic: 27.1 us -> none
    ppermute x0 -> x12, waiting for transfers between devices: none -> 25.6 us  [swap(): return lax.ppermute(value, axis, [(s, s ^ step) for s in range(size)])]
    pallas_call x0 -> x1, Pallas kernels: none -> 23.7 us  [histogram_gains(): pl.pallas_call(make_kernel(n_dp, feats, row_dev), out_shape=jax.ShapeDtyp...]
    mul x8 -> x0, local copies, waits for them, and re-layouts: 23 us -> none  [grad_block(): lower_hot[:, :, None, :] * pair_block[None, None, :, :]]
    ppermute x0 -> x12, starting transfers between devices: none -> 20 us  [swap(): return lax.ppermute(value, axis, [(s, s ^ step) for s in range(size)])]
  transfers between devices with their start and end apart: 2 -> 13, of which waited for: 2 -> 6; matrix products, arithmetic and copies ran while one was open for 3% -> 0% of each run, Pallas kernels for 0% -> 0%
where the time goes in v1:
time: 87.2 us; the launch traced here: 86.1 us
  starting transfers between devices  26 us (30%)
  waiting for transfers between devices  25.6 us (29%)
  Pallas kernels  23.7 us (27%)
  between operations  5.89 us (7%)
  local copies, waits for them, and re-layouts  4.57 us (5%)
    ppermute x12, waiting for transfers between devices, swap(): return lax.ppermute(value, axis, [(s, s ^ step) for s in range(size)])  25.6 us
    pallas_call x1, Pallas kernels, histogram_gains(): pl.pallas_call(make_kernel(n_dp, feats, row_dev), out_shape=jax.ShapeDtyp...  23.7 us
    ppermute x12, starting transfers between devices, swap(): return lax.ppermute(value, axis, [(s, s ^ step) for s in range(size)])  20 us
    all_to_all x1, starting transfers between devices, shards(): lax.all_to_all(fine_values.reshape(n_dp, feats, row_dev), 'dp', 0, 0)  5.97 us
    unnamed x12, local copies, waits for them, and re-layouts  2.24 us
  transfers between devices with their start and end apart: 13, of which 6 were waited for; matrix products, arithmetic and copies ran while one was open for 0% of the time, Pallas kernels for 0%

profile of v1, /device:TPU:0, one launch (start us, length us, event | category | flops | bytes accessed | tf_op | source)
XLA Modules:
  0.0 86.1 jit_solution(4619065328604232243)
XLA Ops:
  0.0 0.0 copy-start.5
  0.0 0.7 copy-done.5
  0.7 0.6 fusion.1
  7.0 0.9 %constant_dynamic-slice_fusion.2 = (f32[1,1024]{1,0:T(1,128)S(1)}, f32[1,1024]{1,0:T(1,128)S(1)}, f32[1,1024]{1,0:T(1,128)S(1)}) fusion(f32[128,1024]{1,0:T(8,128)} %param.6, s32[]{:T(128)S(6)} %select_n.37, s32[]{:T(128)S(6)} %select_n.39, s32[]{:T(128)S(6)} %select_n.38), kind=kLoop, calls=%fused_computation.15 | loop fusion | bytes 24588 | tf_op jit(solution)/shard_map/dynamic_slice | solution.py:155
  7.9 0.1 maximum_select_fusion
  8.0 0.4 collective-permute-start
  8.4 0.8 collective-permute-done
  9.2 0.1 fusion
  9.3 2.8 %collective-permute-start.1 = (f32[3,1024]{1,0:T(4,128)S(1)}, f32[3,1024]{1,0:T(4,128)S(1)}, u32[]{:S(2)}, u32[]{:S(2)}) collective-permute-start(f32[3,1024]{1,0:T(4,128)S(1)} %fusion), channel_id=1, source_target_pairs={{0,2},{1,3},{2,0},{3,1},{4,6},{5,7},{6,4},{7,5},{8,10},{9,11},{10,... | collective-permute-start | bytes 36872 | tf_op jit(solution)/shard_map/ppermute | solution.py:144
  12.1 0.0 copy-start.3
  12.1 6.0 %all-to-all-start = ((f32[8,16,1024]{2,1,0:T(8,128)}), f32[8,16,1024]{2,1,0:T(8,128)S(1)}, u32[]{:S(2)}, u32[]{:S(2)}) async-start(f32[8,16,1024]{2,1,0:T(8,128)} %bitcast.8), calls=%async_computation | async-start | bytes 1048576 | tf_op jit(solution)/shard_map/all_to_all | solution.py:166
  18.1 0.0 copy-done.3
  18.1 0.0 copy-start.4
  18.1 0.7 copy-done.4
  18.8 0.0 collective-permute-done.1
  18.8 0.1 fusion.2
  18.9 2.1 %collective-permute-start.2 = (f32[1,8,1024]{2,1,0:T(8,128)S(1)}, f32[1,8,1024]{2,1,0:T(8,128)S(1)}, u32[]{:S(2)}, u32[]{:S(2)}) collective-permute-start(f32[1,8,1024]{2,1,0:T(8,128)S(1)} %maximum_bitcast_fusion), channel_id=1, source_target_pairs={{0,4},{4,0},{8,12},{12,8},{16,20},{20,16},{24,28},{28,24},{1,5},{5... | collective-permute-start | bytes 98312 | tf_op jit(solution)/shard_map/ppermute | solution.py:144
  21.0 3.8 %collective-permute-done.2 = f32[1,8,1024]{2,1,0:T(8,128)S(1)} collective-permute-done((f32[1,8,1024]{2,1,0:T(8,128)S(1)}, f32[1,8,1024]{2,1,0:T(8,128)S(1)}, u32[]{:S(2)}, u32[]{:S(2)}) %collective-permute-start.2) | collective-permute-done | bytes 32800 | tf_op jit(solution)/shard_map/ppermute | solution.py:144
  24.8 0.3 collective-permute-start.3
  25.1 4.6 %collective-permute-done.3 = f32[2,8,1024]{2,1,0:T(8,128)S(1)} collective-permute-done((f32[2,8,1024]{2,1,0:T(8,128)S(1)}, f32[2,8,1024]{2,1,0:T(8,128)S(1)}, u32[]{:S(2)}, u32[]{:S(2)}) %collective-permute-start.3) | collective-permute-done | bytes 65568 | tf_op jit(solution)/shard_map/ppermute | solution.py:144
  29.7 3.1 %collective-permute-start.4 = (f32[4,8,1024]{2,1,0:T(8,128)S(1)}, f32[4,8,1024]{2,1,0:T(8,128)S(1)}, u32[]{:S(2)}, u32[]{:S(2)}) collective-permute-start(f32[4,8,1024]{2,1,0:T(8,128)S(1)} %pad_maximum_fusion.1), channel_id=1, source_target_pairs={{0,16},{4,20},{8,24},{12,28},{16,0},{20,4},{24,8},{28,12},{1,17},{... | collective-permute-start | bytes 393224 | tf_op jit(solution)/shard_map/ppermute | solution.py:144
  32.8 0.0 copy-start
  32.8 0.0 copy-start.1
  32.8 5.4 %collective-permute-done.4 = f32[4,8,1024]{2,1,0:T(8,128)S(1)} collective-permute-done((f32[4,8,1024]{2,1,0:T(8,128)S(1)}, f32[4,8,1024]{2,1,0:T(8,128)S(1)}, u32[]{:S(2)}, u32[]{:S(2)}) %collective-permute-start.4) | collective-permute-done | bytes 131104 | tf_op jit(solution)/shard_map/ppermute | solution.py:144
  38.3 0.0 all-to-all-done.x_ref
  38.3 0.0 copy-done
  38.3 0.0 copy-done.1
  38.3 23.7 %gains.1 = f32[7,16,256]{2,1,0:T(8,128)S(1)} custom-call(s32[8]{0:T(128)S(1)} %copy-done, s32[3]{0:T(128)S(1)} %copy-done.1, s32[8]{0:T(128)S(1)} %iota_xor_fusion.order, f32[8,16,1024]{2,1,0:T(8,128)S(1)} %all-to-all-done.x_ref, f32[8,8,1024]{2,1,0:T(8,128)S(1)} %pad_maximum_fusion.s_ref), custom_call_target="tpu_custom_call" | custom-call | tf_op jit(solution)/shard_map/gains/pallas_call | solution.py:135
  62.0 1.5 %collective-permute-start.5 = (f32[7,16,256]{2,1,0:T(8,128)S(1)}, f32[7,16,256]{2,1,0:T(8,128)S(1)}, u32[]{:S(2)}, u32[]{:S(2)}) collective-permute-start(f32[7,16,256]{2,1,0:T(8,128)S(1)} %gains.1), channel_id=1, source_target_pairs={{0,4},{4,0},{8,12},{12,8},{16,20},{20,16},{24,28},{28,24},{1,5},{5... | collective-permute-start | bytes 344072 | tf_op jit(solution)/shard_map/ppermute | solution.py:144
  63.5 0.0 collective-permute-start.6
  63.5 2.0 %collective-permute-start.7 = (f32[7,16,256]{2,1,0:T(8,128)S(1)}, f32[7,16,256]{2,1,0:T(8,128)S(1)}, u32[]{:S(2)}, u32[]{:S(2)}) collective-permute-start(f32[7,16,256]{2,1,0:T(8,128)S(1)} %gains.1), channel_id=1, source_target_pairs={{0,12},{4,8},{8,4},{12,0},{16,28},{20,24},{24,20},{28,16},{1,13},{... | collective-permute-start | bytes 344072 | tf_op jit(solution)/shard_map/ppermute | solution.py:144
  65.5 1.3 %collective-permute-start.8 = (f32[7,16,256]{2,1,0:T(8,128)S(1)}, f32[7,16,256]{2,1,0:T(8,128)S(1)}, u32[]{:S(2)}, u32[]{:S(2)}) collective-permute-start(f32[7,16,256]{2,1,0:T(8,128)S(1)} %gains.1), channel_id=1, source_target_pairs={{0,16},{4,20},{8,24},{12,28},{16,0},{20,4},{24,8},{28,12},{1,17},{... | collective-permute-start | bytes 344072 | tf_op jit(solution)/shard_map/ppermute | solution.py:144
  66.8 2.5 %collective-permute-start.9 = (f32[7,16,256]{2,1,0:T(8,128)S(1)}, f32[7,16,256]{2,1,0:T(8,128)S(1)}, u32[]{:S(2)}, u32[]{:S(2)}) collective-permute-start(f32[7,16,256]{2,1,0:T(8,128)S(1)} %gains.1), channel_id=1, source_target_pairs={{0,20},{4,16},{8,28},{12,24},{16,4},{20,0},{24,12},{28,8},{1,21},{... | collective-permute-start | bytes 344072 | tf_op jit(solution)/shard_map/ppermute | solution.py:144
  69.4 0.1 broadcast_in_dim.32
  69.5 0.0 collective-permute-done.5
  69.5 1.7 %collective-permute-start.10 = (f32[7,16,256]{2,1,0:T(8,128)S(1)}, f32[7,16,256]{2,1,0:T(8,128)S(1)}, u32[]{:S(2)}, u32[]{:S(2)}) collective-permute-start(f32[7,16,256]{2,1,0:T(8,128)S(1)} %gains.1), channel_id=1, source_target_pairs={{0,24},{4,28},{8,16},{12,20},{16,8},{20,12},{24,0},{28,4},{1,25},{... | collective-permute-start | bytes 344072 | tf_op jit(solution)/shard_map/ppermute | solution.py:144
  71.2 0.0 collective-permute-done.6
  71.3 2.2 %collective-permute-start.11 = (f32[7,16,256]{2,1,0:T(8,128)S(1)}, f32[7,16,256]{2,1,0:T(8,128)S(1)}, u32[]{:S(2)}, u32[]{:S(2)}) collective-permute-start(f32[7,16,256]{2,1,0:T(8,128)S(1)} %gains.1), channel_id=1, source_target_pairs={{0,28},{4,24},{8,20},{12,16},{16,12},{20,8},{24,4},{28,0},{1,29},{... | collective-permute-start | bytes 344072 | tf_op jit(solution)/shard_map/ppermute | solution.py:144
  73.5 0.0 collective-permute-done.7
  73.5 7.3 %collective-permute-done.8 = f32[7,16,256]{2,1,0:T(8,128)S(1)} collective-permute-done((f32[7,16,256]{2,1,0:T(8,128)S(1)}, f32[7,16,256]{2,1,0:T(8,128)S(1)}, u32[]{:S(2)}, u32[]{:S(2)}) %collective-permute-start.8) | collective-permute-done | bytes 114720 | tf_op jit(solution)/shard_map/ppermute | solution.py:144
  80.8 3.6 %collective-permute-done.9 = f32[7,16,256]{2,1,0:T(8,128)S(1)} collective-permute-done((f32[7,16,256]{2,1,0:T(8,128)S(1)}, f32[7,16,256]{2,1,0:T(8,128)S(1)}, u32[]{:S(2)}, u32[]{:S(2)}) %collective-permute-start.9) | collective-permute-done | bytes 114720 | tf_op jit(solution)/shard_map/ppermute | solution.py:144
  84.5 0.0 collective-permute-done.10
  84.5 0.0 copy-start.2
  84.5 0.0 collective-permute-done.11
  84.5 0.9 %copy-done.2 = f32[7,128,256]{2,1,0:T(8,128)} copy-done((f32[7,128,256]{2,1,0:T(8,128)}, f32[7,128,256]{2,1,0:T(8,128)S(1)}, u32[]{:S(2)}) %copy-start.2) | copy-done | bytes 917528
  85.4 0.7 constant_dynamic-update-slice_fusion
  (17 shorter events, 0.2 us)
Async XLA Ops:
  0.0 0.7 copy-start.5
  8.0 1.3 %collective-permute-start = (f32[3,1024]{1,0:T(4,128)S(1)}, f32[3,1024]{1,0:T(4,128)S(1)}, u32[]{:S(2)}, u32[]{:S(2)}) collective-permute-start(f32[3,1024]{1,0:T(4,128)S(1)} %maximum_select_fusion), channel_id=1, source_target_pairs={{0,1},{1,0},{2,3},{3,2},{4,5},{5,4},{6,7},{7,6},{8,9},{9,8},{10,11... | collective-permute-start | bytes 36872 | tf_op jit(solution)/shard_map/ppermute | solution.py:144
  9.3 9.5 %collective-permute-start.1 = (f32[3,1024]{1,0:T(4,128)S(1)}, f32[3,1024]{1,0:T(4,128)S(1)}, u32[]{:S(2)}, u32[]{:S(2)}) collective-permute-start(f32[3,1024]{1,0:T(4,128)S(1)} %fusion), channel_id=1, source_target_pairs={{0,2},{1,3},{2,0},{3,1},{4,6},{5,7},{6,4},{7,5},{8,10},{9,11},{10,... | collective-permute-start | bytes 36872 | tf_op jit(solution)/shard_map/ppermute | solution.py:144
  12.1 6.0 %copy-start.3 = (bf16[1024]{0:T(1024)(128)(2,1)S(1)}, bf16[1024]{0:T(1024)(128)(2,1)}, u32[]{:S(2)}) copy-start(bf16[1024]{0:T(1024)(128)(2,1)} %param.7) | copy-start | bytes 6148
  12.1 26.1 %all-to-all-start = ((f32[8,16,1024]{2,1,0:T(8,128)}), f32[8,16,1024]{2,1,0:T(8,128)S(1)}, u32[]{:S(2)}, u32[]{:S(2)}) async-start(f32[8,16,1024]{2,1,0:T(8,128)} %bitcast.8), calls=%async_computation | async-start | bytes 1048576 | tf_op jit(solution)/shard_map/all_to_all | solution.py:166
  18.1 0.7 copy-start.4
  18.9 5.9 %collective-permute-start.2 = (f32[1,8,1024]{2,1,0:T(8,128)S(1)}, f32[1,8,1024]{2,1,0:T(8,128)S(1)}, u32[]{:S(2)}, u32[]{:S(2)}) collective-permute-start(f32[1,8,1024]{2,1,0:T(8,128)S(1)} %maximum_bitcast_fusion), channel_id=1, source_target_pairs={{0,4},{4,0},{8,12},{12,8},{16,20},{20,16},{24,28},{28,24},{1,5},{5... | collective-permute-start | bytes 98312 | tf_op jit(solution)/shard_map/ppermute | solution.py:144
  24.8 4.8 %collective-permute-start.3 = (f32[2,8,1024]{2,1,0:T(8,128)S(1)}, f32[2,8,1024]{2,1,0:T(8,128)S(1)}, u32[]{:S(2)}, u32[]{:S(2)}) collective-permute-start(f32[2,8,1024]{2,1,0:T(8,128)S(1)} %pad_maximum_fusion.2), channel_id=1, source_target_pairs={{0,8},{4,12},{8,0},{12,4},{16,24},{20,28},{24,16},{28,20},{1,9},{5... | collective-permute-start | bytes 196616 | tf_op jit(solution)/shard_map/ppermute | solution.py:144
  29.7 8.6 %collective-permute-start.4 = (f32[4,8,1024]{2,1,0:T(8,128)S(1)}, f32[4,8,1024]{2,1,0:T(8,128)S(1)}, u32[]{:S(2)}, u32[]{:S(2)}) collective-permute-start(f32[4,8,1024]{2,1,0:T(8,128)S(1)} %pad_maximum_fusion.1), channel_id=1, source_target_pairs={{0,16},{4,20},{8,24},{12,28},{16,0},{20,4},{24,8},{28,12},{1,17},{... | collective-permute-start | bytes 393224 | tf_op jit(solution)/shard_map/ppermute | solution.py:144
  32.8 5.5 %copy-start = (s32[8]{0:T(128)S(1)}, s32[8]{0:T(128)}, u32[]{:S(2)}) copy-start(s32[8]{0:T(128)} %slab_rows.1) | copy-start | bytes 100
  32.8 5.5 %copy-start.1 = (s32[3]{0:T(128)S(1)}, s32[3]{0:T(128)}, u32[]{:S(2)}) copy-start(s32[3]{0:T(128)} %split_bin.1) | copy-start | bytes 40
  62.0 7.5 %collective-permute-start.5 = (f32[7,16,256]{2,1,0:T(8,128)S(1)}, f32[7,16,256]{2,1,0:T(8,128)S(1)}, u32[]{:S(2)}, u32[]{:S(2)}) collective-permute-start(f32[7,16,256]{2,1,0:T(8,128)S(1)} %gains.1), channel_id=1, source_target_pairs={{0,4},{4,0},{8,12},{12,8},{16,20},{20,16},{24,28},{28,24},{1,5},{5... | collective-permute-start | bytes 344072 | tf_op jit(solution)/shard_map/ppermute | solution.py:144
  63.5 7.7 %collective-permute-start.6 = (f32[7,16,256]{2,1,0:T(8,128)S(1)}, f32[7,16,256]{2,1,0:T(8,128)S(1)}, u32[]{:S(2)}, u32[]{:S(2)}) collective-permute-start(f32[7,16,256]{2,1,0:T(8,128)S(1)} %gains.1), channel_id=1, source_target_pairs={{0,8},{4,12},{8,0},{12,4},{16,24},{20,28},{24,16},{28,20},{1,9},{5... | collective-permute-start | bytes 344072 | tf_op jit(solution)/shard_map/ppermute | solution.py:144
  63.5 10.0 %collective-permute-start.7 = (f32[7,16,256]{2,1,0:T(8,128)S(1)}, f32[7,16,256]{2,1,0:T(8,128)S(1)}, u32[]{:S(2)}, u32[]{:S(2)}) collective-permute-start(f32[7,16,256]{2,1,0:T(8,128)S(1)} %gains.1), channel_id=1, source_target_pairs={{0,12},{4,8},{8,4},{12,0},{16,28},{20,24},{24,20},{28,16},{1,13},{... | collective-permute-start | bytes 344072 | tf_op jit(solution)/shard_map/ppermute | solution.py:144
  65.5 15.2 %collective-permute-start.8 = (f32[7,16,256]{2,1,0:T(8,128)S(1)}, f32[7,16,256]{2,1,0:T(8,128)S(1)}, u32[]{:S(2)}, u32[]{:S(2)}) collective-permute-start(f32[7,16,256]{2,1,0:T(8,128)S(1)} %gains.1), channel_id=1, source_target_pairs={{0,16},{4,20},{8,24},{12,28},{16,0},{20,4},{24,8},{28,12},{1,17},{... | collective-permute-start | bytes 344072 | tf_op jit(solution)/shard_map/ppermute | solution.py:144
  66.8 17.6 %collective-permute-start.9 = (f32[7,16,256]{2,1,0:T(8,128)S(1)}, f32[7,16,256]{2,1,0:T(8,128)S(1)}, u32[]{:S(2)}, u32[]{:S(2)}) collective-permute-start(f32[7,16,256]{2,1,0:T(8,128)S(1)} %gains.1), channel_id=1, source_target_pairs={{0,20},{4,16},{8,28},{12,24},{16,4},{20,0},{24,12},{28,8},{1,21},{... | collective-permute-start | bytes 344072 | tf_op jit(solution)/shard_map/ppermute | solution.py:144
  69.5 15.0 %collective-permute-start.10 = (f32[7,16,256]{2,1,0:T(8,128)S(1)}, f32[7,16,256]{2,1,0:T(8,128)S(1)}, u32[]{:S(2)}, u32[]{:S(2)}) collective-permute-start(f32[7,16,256]{2,1,0:T(8,128)S(1)} %gains.1), channel_id=1, source_target_pairs={{0,24},{4,28},{8,16},{12,20},{16,8},{20,12},{24,0},{28,4},{1,25},{... | collective-permute-start | bytes 344072 | tf_op jit(solution)/shard_map/ppermute | solution.py:144
  71.3 13.3 %collective-permute-start.11 = (f32[7,16,256]{2,1,0:T(8,128)S(1)}, f32[7,16,256]{2,1,0:T(8,128)S(1)}, u32[]{:S(2)}, u32[]{:S(2)}) collective-permute-start(f32[7,16,256]{2,1,0:T(8,128)S(1)} %gains.1), channel_id=1, source_target_pairs={{0,28},{4,24},{8,20},{12,16},{16,12},{20,8},{24,4},{28,0},{1,29},{... | collective-permute-start | bytes 344072 | tf_op jit(solution)/shard_map/ppermute | solution.py:144
  84.5 0.9 %copy-start.2 = (f32[7,128,256]{2,1,0:T(8,128)}, f32[7,128,256]{2,1,0:T(8,128)S(1)}, u32[]{:S(2)}) copy-start(f32[7,128,256]{2,1,0:T(8,128)S(1)} %constant_dynamic-update-slice_fusion.1) | copy-start | bytes 2752516

commit v2 on v1

v2 whole, which is shorter than its diff:
```python
import jax
import jax.numpy as jnp
from jax import lax
from jax.experimental import pallas as pl
from jax.experimental.pallas import tpu as pltpu
from jax.sharding import PartitionSpec as P

FINE_BINS = 1024
BINS = 256
HI = 8
LO = 128
CHUNK = 256
GROUP = 4
f32 = jnp.float32
bf16 = jnp.bfloat16
i32 = jnp.int32


def dot_nt(a, b):
    return lax.dot_general(a, b, (((1,), (1,)), ((), ())), preferred_element_type=f32)


def dot_nn(a, b):
    return jnp.dot(a, b, preferred_element_type=f32)


def iota(shape, axis):
    return lax.broadcasted_iota(i32, shape, axis)


def to_bf16(x):
    return x.astype(f32).astype(bf16)


def bytes_of(x, axis):
    return jnp.concatenate([to_bf16((x >> (8 * i)) & 255) for i in range(4)], axis)


def coarse_of(whole, group):
    n = whole.shape[0]
    r, c = iota((LO, 2 * LO), 0), iota((LO, 2 * LO), 1)
    in_row = dot_nn(bytes_of(whole, 0), to_bf16((r < c) | (c >= LO)))
    in_row = in_row.astype(i32)
    in_row = sum(in_row[i * n : (i + 1) * n] << (8 * i) for i in range(4))
    before, row_total = in_row[:, :LO], in_row[:, LO:]
    r, c = iota((2 * n, n), 0), iota((2 * n, n), 1)
    same = (r % n) // group == c // group
    over = dot_nn(to_bf16(same & ((c < r) | (r >= n))), bytes_of(row_total, 1)).astype(i32)
    over = sum(over[:, i * LO : (i + 1) * LO] << (8 * i) for i in range(4))
    total = over[n:]
    remainder = before + over[:n]
    quotient = jnp.zeros_like(remainder)
    for _ in range(BINS.bit_length() - 1):
        remainder = remainder * 2
        bit = remainder >= total
        remainder = jnp.where(bit, remainder - total, remainder)
        quotient = quotient * 2 + bit.astype(i32)
    return jnp.minimum(BINS - 1, quotient)


def fine_of(v):
    return jnp.clip(jnp.floor(v * FINE_BINS), 0, FINE_BINS - 1)


def hi_lo(t):
    hi = jnp.floor(t * (1.0 / LO))
    return hi, t - hi * LO


def hot(row, rows, width):
    b = jnp.broadcast_to(row, (16, width)).astype(bf16)
    at = iota((16, width), 0)
    one, zero = jnp.ones((16, width), bf16), jnp.zeros((16, width), bf16)
    return jnp.concatenate([jnp.where(b == to_bf16(at + 16 * j), one, zero) for j in range(rows // 16)], 0)


def make_route(n_dp, row_dev):
    tiles = row_dev // LO
    side = 32

    def kernel(slab_rows, split_bin, *refs):
        blocks, ch_ref, t_ref = refs[: n_dp // 2], refs[n_dp // 2], refs[n_dp // 2 + 1]
        me = lax.axis_index("dp")
        at16 = iota((16, LO), 0)
        steps = [to_bf16(at16), to_bf16(at16 + 16)]
        one, zero = jnp.ones((16, LO), bf16), jnp.zeros((16, LO), bf16)
        counts = [jnp.zeros((side, side), f32) for _ in range(3)]
        for j in range(n_dp):
            block = blocks[j // 2]
            row = iota((tiles, LO), 0) * LO + iota((tiles, LO), 1)
            live = row < slab_rows[me ^ j]
            t_ref[j, 3] = jnp.where(live, block[j % 2, 3 * tiles : 4 * tiles], 0.0)
            h = jnp.where(live, block[j % 2, 4 * tiles :], 0.0)
            t_ref[j, 4] = h
            hs = [jnp.broadcast_to(h[i : i + 1], (16, LO)).astype(bf16) for i in range(tiles)]
            for n in range(3):
                t = fine_of(block[j % 2, n * tiles : (n + 1) * tiles])
                t_ref[j, n] = t
                hi = jnp.floor(t * (1.0 / side))
                lo = t - hi * side
                left, right = [], []
                for i in range(tiles):
                    hb = jnp.broadcast_to(hi[i : i + 1], (16, LO)).astype(bf16)
                    lb = jnp.broadcast_to(lo[i : i + 1], (16, LO)).astype(bf16)
                    left.append(jnp.concatenate([jnp.where(hb == k, hs[i], zero) for k in steps], 0))
                    right.append(jnp.concatenate([jnp.where(lb == k, one, zero) for k in steps], 0))
                counts[n] += dot_nt(jnp.concatenate(left, 1), jnp.concatenate(right, 1))
        whole = (jnp.concatenate(counts, 0) * 16384.0).astype(i32)
        cut = coarse_of(jnp.concatenate([whole, jnp.zeros((3 * side, LO - side), i32)], 1), side)
        cuts = []
        for n in range(3):
            below = (cut[n * side : (n + 1) * side] <= split_bin[n]) & (iota((side, LO), 1) < side)
            below = jnp.where(below, 1.0, 0.0)
            cuts.append(jnp.sum(jnp.sum(below, axis=0, keepdims=True), axis=1, keepdims=True))
        ch_ref[n_dp] = jnp.zeros((8, row_dev), f32)
        at = iota((8, LO), 0)
        for j in range(n_dp):
            s = me ^ j
            l0, l1, l2 = [t_ref[j, n] < cuts[n] for n in range(3)]
            leaf = jnp.where(l0, jnp.where(l1, 0, 1), jnp.where(l2, 2, 3))
            g, h = t_ref[j, 3], t_ref[j, 4]
            for i in range(tiles):
                gh = jnp.where(at < 4, jnp.broadcast_to(g[i : i + 1], (8, LO)), jnp.broadcast_to(h[i : i + 1], (8, LO)))
                here = at % 4 == jnp.broadcast_to(leaf[i : i + 1], (8, LO))
                ch_ref[s, :, i * LO : (i + 1) * LO] = jnp.where(here, gh, 0.0)

    return kernel


def route_rows(blocks, slab_rows, split_bin, n_dp, row_dev):
    smem = pl.BlockSpec(memory_space=pltpu.SMEM)
    vmem = pl.BlockSpec(memory_space=pltpu.VMEM)
    return pl.pallas_call(
        make_route(n_dp, row_dev),
        out_shape=jax.ShapeDtypeStruct((n_dp + 1, 8, row_dev), f32),
        in_specs=[smem, smem] + [vmem] * len(blocks),
        out_specs=vmem,
        scratch_shapes=[pltpu.VMEM((n_dp, 5, row_dev // LO, LO), f32)],
        compiler_params=pltpu.CompilerParams(vmem_limit_bytes=32 * 2**20),
        cost_estimate=pl.CostEstimate(flops=2 * 96 * 256 * n_dp * row_dev, bytes_accessed=2**18, transcendentals=0),
        name="route",
    )(slab_rows, split_bin, *blocks)


def make_gains(n_dp, feats, row_dev):
    pairs = feats // 2
    per = row_dev // CHUNK
    width = GROUP * CHUNK

    def kernel(slab_rows, x_ref, ch_ref, o_ref, list_ref, acc_ref, cum_ref):
        def note(i, n):
            list_ref[n] = i
            return n + (i % per * CHUNK < slab_rows[i // per]).astype(i32)

        used = lax.fori_loop(0, n_dp * per, note, 0)
        for i in range(GROUP - 1):
            list_ref[used + i] = n_dp * per
        acc_ref[...] = jnp.zeros_like(acc_ref)
        kk = [to_bf16(iota((16, width), 0) // 8 + 2 * j) for j in range(HI // 2)]
        zero = jnp.zeros((16, width), bf16)
        in_first = iota((LO, LO), 1) < 64

        def add(q, _):
            xs, chs = [], []
            for i in range(GROUP):
                at = list_ref[q * GROUP + i]
                s = at // per
                col = pl.ds(pl.multiple_of((at % per) * CHUNK, CHUNK), CHUNK)
                xs.append(x_ref[jnp.minimum(s, n_dp - 1), :, col])
                chs.append(ch_ref[s, :, col])
            ch = jnp.concatenate(chs, 1)
            ch = jnp.concatenate([ch, ch], 0).astype(bf16)
            hi, lo = hi_lo(fine_of(jnp.concatenate(xs, 1)))

            def spread(f):
                hb = jnp.broadcast_to(hi[f : f + 1], (16, width)).astype(bf16)
                return [jnp.where(hb == k, ch, zero) for k in kk]

            for p in range(pairs):
                f = 2 * p
                w = jnp.concatenate(spread(f) + spread(f + 1), 0)
                a = dot_nt(hot(lo[f : f + 1], LO, width), w)
                b = dot_nt(hot(lo[f + 1 : f + 2], LO, width), w)
                acc_ref[p] += jnp.where(in_first, a, b)
            return 0

        lax.fori_loop(0, (used + GROUP - 1) // GROUP, add, 0)
        n = feats * HI
        acc = jnp.concatenate([jnp.transpose(acc_ref[p]) for p in range(pairs)], 0)
        p0 = acc.astype(bf16)
        r1 = acc - p0.astype(f32)
        p1 = r1.astype(bf16)
        r2 = r1 - p1.astype(f32)
        r, c = iota((n, n * 8), 0), iota((n, n * 8), 1)
        pick = to_bf16((c // 8 == r) & (c % 8 >= 4))
        counts = (dot_nn(pick, p0) + dot_nn(pick, p1)) + dot_nn(pick, r2.astype(bf16))
        cut = coarse_of((counts * 16384.0).astype(i32), HI).astype(f32)
        edges = [to_bf16(iota((16, LO), 0) + 16 * j) for j in range(BINS // 16)]
        one, none = jnp.ones((16, LO), bf16), jnp.zeros((16, LO), bf16)
        q0, q1 = p0.astype(f32), p1.astype(f32)
        sums = []
        for f in range(feats):
            left, right = [], []
            for k in range(HI):
                at = f * HI + k
                cb = jnp.broadcast_to(cut[at : at + 1], (16, LO)).astype(bf16)
                left.append(jnp.concatenate([jnp.where(cb <= e, one, none) for e in edges], 0))
                right.append(jnp.concatenate([q0[at * 8 : at * 8 + 8], q1[at * 8 : at * 8 + 8]], 0).astype(bf16))
            sums.append(dot_nt(jnp.concatenate(left, 1), jnp.concatenate(right, 1)))
        per_tile = LO // 16
        for f0 in range(0, feats, per_tile):
            tile = jnp.concatenate(sums[f0 : f0 + per_tile], 1)
            if tile.shape[1] < LO:
                tile = jnp.concatenate([tile, jnp.zeros((BINS, LO - tile.shape[1]), f32)], 1)
            tile = jnp.transpose(tile)
            for f in range(f0, min(f0 + per_tile, feats)):
                at = (f - f0) * 16
                gl = tile[at : at + 8] + tile[at + 8 : at + 16]
                for c in range(8):
                    cum_ref[c, f : f + 1, :] = gl[c : c + 1]

        def score(g, h):
            return g * g / (h + 1.0)

        def nodes(first):
            leaves = [cum_ref[first + c] for c in range(4)]
            a, b = leaves[0] + leaves[1], leaves[2] + leaves[3]
            return [a + b, a, b] + leaves

        for i, (gl, hl) in enumerate(zip(nodes(0), nodes(4))):
            g, h = gl[:, BINS - 1 :], hl[:, BINS - 1 :]
            o_ref[i] = score(gl, hl) + score(g - gl, h - hl) - score(g, h)

    return kernel


def gains_of(x, ch, slab_rows):
    n_dp, feats, row_dev = x.shape
    smem = pl.BlockSpec(memory_space=pltpu.SMEM)
    vmem = pl.BlockSpec(memory_space=pltpu.VMEM)
    return pl.pallas_call(
        make_gains(n_dp, feats, row_dev),
        out_shape=jax.ShapeDtypeStruct((7, feats, BINS), f32),
        in_specs=[smem, vmem, vmem],
        out_specs=vmem,
        scratch_shapes=[
            pltpu.SMEM((n_dp * (row_dev // CHUNK) + GROUP,), i32),
            pltpu.VMEM((feats // 2, LO, LO), f32),
            pltpu.VMEM((8, feats, BINS), f32),
        ],
        compiler_params=pltpu.CompilerParams(vmem_limit_bytes=40 * 2**20),
        cost_estimate=pl.CostEstimate(flops=2 * 128 * 256 * n_dp * row_dev * feats, bytes_accessed=2**20, transcendentals=0),
        name="gains",
    )(slab_rows, x, ch)


def make_pick(feat_dev, row_dev):
    tiles = row_dev // LO

    def kernel(split_feature, x_ref, o_ref, rows_ref, sems):
        me = lax.axis_index("feat")
        work = []
        for n in range(3):
            local = split_feature[n] - me * feat_dev
            owned = (local >= 0) & (local < feat_dev)
            at = jnp.clip(local, 0, feat_dev - 1)
            first = pl.multiple_of(at // 8 * 8, 8)
            copy = pltpu.make_async_copy(x_ref.at[pl.ds(first, 8), :], rows_ref.at[n], sems.at[n])
            copy.start()
            work.append((copy, at % 8, jnp.where(owned, 1.0, 0.0)))
        for n, (copy, at, scale) in enumerate(work):
            copy.wait()
            row = jnp.where(iota((8, row_dev), 0) == at, rows_ref[n], 0.0)
            row = jnp.sum(row, axis=0, keepdims=True) * scale
            for i in range(tiles):
                o_ref[n * tiles + i : n * tiles + i + 1, :] = row[:, i * LO : (i + 1) * LO]

    return kernel


def pick_rows(fine_values, split_feature):
    feat_dev, row_dev = fine_values.shape
    return pl.pallas_call(
        make_pick(feat_dev, row_dev),
        out_shape=jax.ShapeDtypeStruct((3 * row_dev // LO, LO), f32),
        in_specs=[pl.BlockSpec(memory_space=pltpu.SMEM), pl.BlockSpec(memory_space=pl.ANY)],
        out_specs=pl.BlockSpec(memory_space=pltpu.VMEM),
        scratch_shapes=[pltpu.VMEM((3, 8, row_dev), f32), pltpu.SemaphoreType.DMA((3,))],
        name="pick",
    )(split_feature, fine_values)


def swap(value, axis, size, step):
    return lax.ppermute(value, axis, [(s, s ^ step) for s in range(size)])


def make_shards(n_dp, n_feat):
    def shards(fine_values, grad, hess, slab_rows, split_feature, split_bin):
        feat_dev, row_dev = fine_values.shape
        feats = feat_dev // n_dp
        me = lax.axis_index("dp")
        both = ("dp", "feat")
        share = pick_rows(fine_values, split_feature)
        share = share + swap(share, "feat", n_feat, 1)
        gh = jnp.concatenate([grad.astype(f32).reshape(-1, LO), hess.astype(f32).reshape(-1, LO)])
        block = jnp.concatenate([share, gh])
        mine, other = share, swap(block, "dp", n_dp, 1)
        v, other_gh = other[: share.shape[0]], other[share.shape[0] :]
        for x in range(2, n_feat, 2):
            mine = mine + swap(share, "feat", n_feat, x)
            v = v + swap(share, both, n_dp * n_feat, n_feat + x)
        pair = jnp.stack([jnp.concatenate([mine, gh]), jnp.concatenate([v, other_gh])])
        pairs = [pair] + [swap(pair, "dp", n_dp, d) for d in range(2, n_dp, 2)]
        blocks = lax.all_to_all(fine_values.reshape(n_dp, feats, row_dev), "dp", 0, 0)
        ch = route_rows(pairs, slab_rows, split_bin, n_dp, row_dev)
        gains = gains_of(blocks, ch, slab_rows)
        whole = jnp.zeros((7, feat_dev, BINS), f32)
        for d in range(n_dp):
            piece = gains if d == 0 else swap(gains, "dp", n_dp, d)
            whole = lax.dynamic_update_slice_in_dim(whole, piece, (me ^ d) * feats, 1)
        return whole

    return shards


def solution(mesh):
    return jax.shard_map(
        make_shards(mesh.shape["dp"], mesh.shape["feat"]),
        mesh=mesh,
        in_specs=(P("feat", "dp"), P("dp"), P("dp"), P(), P(), P()),
        out_specs=P(None, "feat", None),
        check_vma=False,
    )
```

time: 87.2 us -> 68.5 us (0.79)
  Pallas kernels: 23.7 us -> 16.4 us
  between operations: 5.89 us -> 0.17 us
  waiting for transfers between devices: 25.6 us -> 20.8 us
  local copies, waits for them, and re-layouts: 4.57 us -> 1.74 us
  starting transfers between devices: 26 us -> 27.6 us
    pallas_call x1 -> x3, Pallas kernels: 23.7 us -> 16.4 us  [the longest x1 12.4 us: gains_of(): pl.pallas_call(make_gains(n_dp, feats, row_dev), out_shape=jax.ShapeDtype...]
    ppermute x12 -> x14, waiting for transfers between devices: 25.6 us -> 20.8 us  [swap(): return lax.ppermute(value, axis, [(s, s ^ step) for s in range(size)])]
    all_to_all x1, starting transfers between devices: 5.97 us -> 7.28 us  [shards(): lax.all_to_all(fine_values.reshape(n_dp, feats, row_dev), 'dp', 0, 0)]
    unnamed x12 -> x10, local copies, waits for them, and re-layouts: 2.24 us -> 0.93 us
    dynamic_slice x1 -> x0, local copies, waits for them, and re-layouts: 0.89 us -> none  [shards(): lax.dynamic_slice_in_dim(fine_values, at[n], 1, 0)]
    ppermute x12 -> x14, starting transfers between devices: 20 us -> 20.3 us  [swap(): return lax.ppermute(value, axis, [(s, s ^ step) for s in range(size)])]
  transfers between devices with their start and end apart: 13 -> 15, of which waited for: 6 -> 8; matrix products, arithmetic and copies ran while one was open for 0% -> 1% of each run, Pallas kernels for 0% -> 6%
where the time goes in v2:
time: 68.5 us; the launch traced here: 67.5 us
  starting transfers between devices  27.6 us (40%)
  waiting for transfers between devices  20.8 us (30%)
  Pallas kernels  16.4 us (24%)
  local copies, waits for them, and re-layouts  1.74 us (3%)
  other arithmetic  0.74 us (1%)
    ppermute x14, waiting for transfers between devices, swap(): return lax.ppermute(value, axis, [(s, s ^ step) for s in range(size)])  20.8 us
    ppermute x14, starting transfers between devices, swap(): return lax.ppermute(value, axis, [(s, s ^ step) for s in range(size)])  20.3 us
    pallas_call x1, Pallas kernels, gains_of(): pl.pallas_call(make_gains(n_dp, feats, row_dev), out_shape=jax.ShapeDtype...  12.4 us
    all_to_all x1, starting transfers between devices, shards(): lax.all_to_all(fine_values.reshape(n_dp, feats, row_dev), 'dp', 0, 0)  7.28 us
    pallas_call x1, Pallas kernels, pick_rows(): pl.pallas_call(make_pick(feat_dev, row_dev), out_shape=jax.ShapeDtypeStru...  2.18 us
    pallas_call x1, Pallas kernels, route_rows(): pl.pallas_call(make_route(n_dp, row_dev), out_shape=jax.ShapeDtypeStruct(...  1.89 us
  transfers between devices with their start and end apart: 15, of which 8 were waited for; matrix products, arithmetic and copies ran while one was open for 1% of the time, Pallas kernels for 6%

profile of v2, /device:TPU:0, one launch (start us, length us, event | category | flops | bytes accessed | tf_op | source)
XLA Modules:
  0.0 67.5 jit_solution(6250613930601794022)
XLA Ops:
  0.0 7.3 %all-to-all-start = ((f32[8,16,1024]{2,1,0:T(8,128)}), f32[8,16,1024]{2,1,0:T(8,128)S(1)}, u32[]{:S(2)}, u32[]{:S(2)}) async-start(f32[8,16,1024]{2,1,0:T(8,128)} %bitcast.11), calls=%async_computation | async-start | bytes 1048576 | tf_op jit(solution)/shard_map/all_to_all | solution.py:314
  7.3 2.2 %pick.1 = f32[24,128]{1,0:T(8,128)} custom-call(s32[3]{0:T(128)} %split_feature.1, f32[128,1024]{1,0:T(8,128)} %x_ref.1), custom_call_target="tpu_custom_call" | custom-call | tf_op jit(solution)/shard_map/pick/pallas_call | solution.py:283
  9.5 0.0 copy-start.3
  9.5 0.0 copy-start.4
  9.5 0.1 collective-permute-start
  9.6 1.4 %collective-permute-done = f32[24,128]{1,0:T(8,128)S(1)} collective-permute-done((f32[24,128]{1,0:T(8,128)}, f32[24,128]{1,0:T(8,128)S(1)}, u32[]{:S(2)}, u32[]{:S(2)}) %collective-permute-start) | collective-permute-done | bytes 12320 | tf_op jit(solution)/shard_map/ppermute | solution.py:294
  11.0 0.7 %add.33 = f32[24,128]{1,0:T(8,128)S(1)} add(f32[24,128]{1,0:T(8,128)} %pick.1, f32[24,128]{1,0:T(8,128)S(1)} %collective-permute-done) | non-fusion elementwise | flops 3072 | bytes 36864 | tf_op jit(solution)/shard_map/add | solution.py:304
  11.7 1.4 %collective-permute-start.1 = (f32[24,128]{1,0:T(8,128)S(1)}, f32[24,128]{1,0:T(8,128)S(1)}, u32[]{:S(2)}, u32[]{:S(2)}) collective-permute-start(f32[24,128]{1,0:T(8,128)S(1)} %add.33), channel_id=1, source_target_pairs={{0,2},{1,3},{2,0},{3,1},{4,6},{5,7},{6,4},{7,5},{8,10},{9,11},{10,... | collective-permute-start | bytes 36872 | tf_op jit(solution)/shard_map/ppermute | solution.py:294
  13.1 0.0 copy-done.3
  13.1 0.0 copy-done.4
  13.1 2.3 %collective-permute-done.1 = f32[24,128]{1,0:T(8,128)S(1)} collective-permute-done((f32[24,128]{1,0:T(8,128)S(1)}, f32[24,128]{1,0:T(8,128)S(1)}, u32[]{:S(2)}, u32[]{:S(2)}) %collective-permute-start.1) | collective-permute-done | bytes 12320 | tf_op jit(solution)/shard_map/ppermute | solution.py:294
  15.4 2.1 %collective-permute-start.2 = (f32[40,128]{1,0:T(8,128)S(1)}, f32[40,128]{1,0:T(8,128)S(1)}, u32[]{:S(2)}, u32[]{:S(2)}) collective-permute-start(f32[40,128]{1,0:T(8,128)S(1)} %get-tuple-element.6), channel_id=1, source_target_pairs={{0,4},{4,0},{8,12},{12,8},{16,20},{20,16},{24,28},{28,24},{1,5},{5... | collective-permute-start | bytes 61448 | tf_op jit(solution)/shard_map/ppermute | solution.py:294
  17.5 0.9 %collective-permute-start.3 = (f32[24,128]{1,0:T(8,128)S(1)}, f32[24,128]{1,0:T(8,128)S(1)}, u32[]{:S(2)}, u32[]{:S(2)}) collective-permute-start(f32[24,128]{1,0:T(8,128)S(1)} %add.33), channel_id=1, source_target_pairs={{0,6},{1,7},{2,4},{3,5},{4,2},{5,3},{6,0},{7,1},{8,14},{9,15},{10,... | collective-permute-start | bytes 36872 | tf_op jit(solution)/shard_map/ppermute | solution.py:294
  18.4 0.8 %collective-permute-done.2 = f32[40,128]{1,0:T(8,128)S(1)} collective-permute-done((f32[40,128]{1,0:T(8,128)S(1)}, f32[40,128]{1,0:T(8,128)S(1)}, u32[]{:S(2)}, u32[]{:S(2)}) %collective-permute-start.2) | collective-permute-done | bytes 20512 | tf_op jit(solution)/shard_map/ppermute | solution.py:294
  19.2 2.8 %collective-permute-done.3 = f32[24,128]{1,0:T(8,128)S(1)} collective-permute-done((f32[24,128]{1,0:T(8,128)S(1)}, f32[24,128]{1,0:T(8,128)S(1)}, u32[]{:S(2)}, u32[]{:S(2)}) %collective-permute-start.3) | collective-permute-done | bytes 12320 | tf_op jit(solution)/shard_map/ppermute | solution.py:294
  22.1 1.5 %collective-permute-start.4 = (f32[2,40,128]{2,1,0:T(8,128)S(1)}, f32[2,40,128]{2,1,0:T(8,128)S(1)}, u32[]{:S(2)}, u32[]{:S(2)}) collective-permute-start(f32[2,40,128]{2,1,0:T(8,128)S(1)} %pad_maximum_fusion.refs_0_), channel_id=1, source_target_pairs={{0,8},{4,12},{8,0},{12,4},{16,24},{20,28},{24,16},{28,20},{1,9},{5... | collective-permute-start | bytes 122888 | tf_op jit(solution)/shard_map/ppermute | solution.py:294
  23.6 2.4 %collective-permute-start.5 = (f32[2,40,128]{2,1,0:T(8,128)S(1)}, f32[2,40,128]{2,1,0:T(8,128)S(1)}, u32[]{:S(2)}, u32[]{:S(2)}) collective-permute-start(f32[2,40,128]{2,1,0:T(8,128)S(1)} %pad_maximum_fusion.refs_0_), channel_id=1, source_target_pairs={{0,16},{4,20},{8,24},{12,28},{16,0},{20,4},{24,8},{28,12},{1,17},{... | collective-permute-start | bytes 122888 | tf_op jit(solution)/shard_map/ppermute | solution.py:294
  26.0 0.6 collective-permute-start.6
  26.5 0.0 copy-start
  26.5 0.0 copy-start.1
  26.5 0.0 collective-permute-done.4.refs_1_
  26.5 2.6 %collective-permute-done.5.refs_2_ = f32[2,40,128]{2,1,0:T(8,128)S(1)} collective-permute-done((f32[2,40,128]{2,1,0:T(8,128)S(1)}, f32[2,40,128]{2,1,0:T(8,128)S(1)}, u32[]{:S(2)}, u32[]{:S(2)}) %collective-permute-start.5) | collective-permute-done | bytes 40992 | tf_op jit(solution)/shard_map/ppermute | solution.py:294
  29.1 2.6 %collective-permute-done.6.refs_3_ = f32[2,40,128]{2,1,0:T(8,128)S(1)} collective-permute-done((f32[2,40,128]{2,1,0:T(8,128)S(1)}, f32[2,40,128]{2,1,0:T(8,128)S(1)}, u32[]{:S(2)}, u32[]{:S(2)}) %collective-permute-start.6) | collective-permute-done | bytes 40992 | tf_op jit(solution)/shard_map/ppermute | solution.py:294
  31.8 0.0 copy-done
  31.8 0.0 copy-done.1
  31.8 1.9 %route.1.ch_ref = f32[9,8,1024]{2,1,0:T(8,128)S(1)} custom-call(s32[8]{0:T(128)S(1)} %copy-done.1, s32[3]{0:T(128)S(1)} %copy-done, f32[2,40,128]{2,1,0:T(8,128)S(1)} %pad_maximum_fusion.refs_0_, f32[2,40,128]{2,1,0:T(8,128)S(1)} %collective-permute-done.4.refs_1_, f32[2,40,128]{2,1,0:T(8,128)S(1)} %collective-permute-done.5.refs_2_, ...), custom_call_target="tpu_custom_call" | custom-call | flops 402653184 | bytes 262144 | tf_op jit(solution)/shard_map/route/pallas_call | solution.py:133
  33.7 0.0 all-to-all-done.x_ref
  33.7 12.4 %gains.1 = f32[7,16,256]{2,1,0:T(8,128)S(1)} custom-call(s32[8]{0:T(128)S(1)} %copy-done.1, f32[8,16,1024]{2,1,0:T(8,128)S(1)} %all-to-all-done.x_ref, f32[9,8,1024]{2,1,0:T(8,128)S(1)} %route.1.ch_ref), custom_call_target="tpu_custom_call" | custom-call | flops 8589934592 | bytes 1048576 | tf_op jit(solution)/shard_map/gains/pallas_call | solution.py:241
  46.1 0.6 collective-permute-start.7
  46.6 0.0 collective-permute-start.8
  46.6 3.0 %collective-permute-start.9 = (f32[7,16,256]{2,1,0:T(8,128)S(1)}, f32[7,16,256]{2,1,0:T(8,128)S(1)}, u32[]{:S(2)}, u32[]{:S(2)}) collective-permute-start(f32[7,16,256]{2,1,0:T(8,128)S(1)} %gains.1), channel_id=1, source_target_pairs={{0,12},{4,8},{8,4},{12,0},{16,28},{20,24},{24,20},{28,16},{1,13},{... | collective-permute-start | bytes 344072 | tf_op jit(solution)/shard_map/ppermute | solution.py:294
  49.6 0.0 collective-permute-start.10
  49.6 2.9 %collective-permute-start.11 = (f32[7,16,256]{2,1,0:T(8,128)S(1)}, f32[7,16,256]{2,1,0:T(8,128)S(1)}, u32[]{:S(2)}, u32[]{:S(2)}) collective-permute-start(f32[7,16,256]{2,1,0:T(8,128)S(1)} %gains.1), channel_id=1, source_target_pairs={{0,20},{4,16},{8,28},{12,24},{16,4},{20,0},{24,12},{28,8},{1,21},{... | collective-permute-start | bytes 344072 | tf_op jit(solution)/shard_map/ppermute | solution.py:294
  52.5 0.1 broadcast_in_dim.3
  52.6 0.0 collective-permute-done.7
  52.6 0.6 collective-permute-start.12
  53.2 0.0 collective-permute-done.8
  53.2 4.3 %collective-permute-start.13 = (f32[7,16,256]{2,1,0:T(8,128)S(1)}, f32[7,16,256]{2,1,0:T(8,128)S(1)}, u32[]{:S(2)}, u32[]{:S(2)}) collective-permute-start(f32[7,16,256]{2,1,0:T(8,128)S(1)} %gains.1), channel_id=1, source_target_pairs={{0,28},{4,24},{8,20},{12,16},{16,12},{20,8},{24,4},{28,0},{1,29},{... | collective-permute-start | bytes 344072 | tf_op jit(solution)/shard_map/ppermute | solution.py:294
  57.5 0.0 collective-permute-done.9
  57.6 5.7 %collective-permute-done.10 = f32[7,16,256]{2,1,0:T(8,128)S(1)} collective-permute-done((f32[7,16,256]{2,1,0:T(8,128)S(1)}, f32[7,16,256]{2,1,0:T(8,128)S(1)}, u32[]{:S(2)}, u32[]{:S(2)}) %collective-permute-start.10) | collective-permute-done | bytes 114720 | tf_op jit(solution)/shard_map/ppermute | solution.py:294
  63.3 2.6 %collective-permute-done.11 = f32[7,16,256]{2,1,0:T(8,128)S(1)} collective-permute-done((f32[7,16,256]{2,1,0:T(8,128)S(1)}, f32[7,16,256]{2,1,0:T(8,128)S(1)}, u32[]{:S(2)}, u32[]{:S(2)}) %collective-permute-start.11) | collective-permute-done | bytes 114720 | tf_op jit(solution)/shard_map/ppermute | solution.py:294
  65.9 0.0 collective-permute-done.12
  65.9 0.0 copy-start.2
  65.9 0.0 collective-permute-done.13
  65.9 0.9 %copy-done.2 = f32[7,128,256]{2,1,0:T(8,128)} copy-done((f32[7,128,256]{2,1,0:T(8,128)}, f32[7,128,256]{2,1,0:T(8,128)S(1)}, u32[]{:S(2)}) %copy-start.2) | copy-done | bytes 917528
  66.8 0.7 constant_dynamic-update-slice_fusion
  (14 shorter events, 0.1 us)
Async XLA Ops:
  0.0 33.7 %all-to-all-start = ((f32[8,16,1024]{2,1,0:T(8,128)}), f32[8,16,1024]{2,1,0:T(8,128)S(1)}, u32[]{:S(2)}, u32[]{:S(2)}) async-start(f32[8,16,1024]{2,1,0:T(8,128)} %bitcast.11), calls=%async_computation | async-start | bytes 1048576 | tf_op jit(solution)/shard_map/all_to_all | solution.py:314
  9.5 3.6 %copy-start.3 = (bf16[1024]{0:T(1024)(128)(2,1)S(1)}, bf16[1024]{0:T(1024)(128)(2,1)}, u32[]{:S(2)}) copy-start(bf16[1024]{0:T(1024)(128)(2,1)} %param.8) | copy-start | bytes 6148
  9.5 3.6 %copy-start.4 = (bf16[1024]{0:T(1024)(128)(2,1)S(1)}, bf16[1024]{0:T(1024)(128)(2,1)}, u32[]{:S(2)}) copy-start(bf16[1024]{0:T(1024)(128)(2,1)} %param.7) | copy-start | bytes 6148
  9.5 1.5 %collective-permute-start = (f32[24,128]{1,0:T(8,128)}, f32[24,128]{1,0:T(8,128)S(1)}, u32[]{:S(2)}, u32[]{:S(2)}) collective-permute-start(f32[24,128]{1,0:T(8,128)} %pick.1), channel_id=1, source_target_pairs={{0,1},{1,0},{2,3},{3,2},{4,5},{5,4},{6,7},{7,6},{8,9},{9,8},{10,11... | collective-permute-start | bytes 36872 | tf_op jit(solution)/shard_map/ppermute | solution.py:294
  11.7 3.7 %collective-permute-start.1 = (f32[24,128]{1,0:T(8,128)S(1)}, f32[24,128]{1,0:T(8,128)S(1)}, u32[]{:S(2)}, u32[]{:S(2)}) collective-permute-start(f32[24,128]{1,0:T(8,128)S(1)} %add.33), channel_id=1, source_target_pairs={{0,2},{1,3},{2,0},{3,1},{4,6},{5,7},{6,4},{7,5},{8,10},{9,11},{10,... | collective-permute-start | bytes 36872 | tf_op jit(solution)/shard_map/ppermute | solution.py:294
  15.4 3.8 %collective-permute-start.2 = (f32[40,128]{1,0:T(8,128)S(1)}, f32[40,128]{1,0:T(8,128)S(1)}, u32[]{:S(2)}, u32[]{:S(2)}) collective-permute-start(f32[40,128]{1,0:T(8,128)S(1)} %get-tuple-element.6), channel_id=1, source_target_pairs={{0,4},{4,0},{8,12},{12,8},{16,20},{20,16},{24,28},{28,24},{1,5},{5... | collective-permute-start | bytes 61448 | tf_op jit(solution)/shard_map/ppermute | solution.py:294
  17.5 4.6 %collective-permute-start.3 = (f32[24,128]{1,0:T(8,128)S(1)}, f32[24,128]{1,0:T(8,128)S(1)}, u32[]{:S(2)}, u32[]{:S(2)}) collective-permute-start(f32[24,128]{1,0:T(8,128)S(1)} %add.33), channel_id=1, source_target_pairs={{0,6},{1,7},{2,4},{3,5},{4,2},{5,3},{6,0},{7,1},{8,14},{9,15},{10,... | collective-permute-start | bytes 36872 | tf_op jit(solution)/shard_map/ppermute | solution.py:294
  22.1 4.5 %collective-permute-start.4 = (f32[2,40,128]{2,1,0:T(8,128)S(1)}, f32[2,40,128]{2,1,0:T(8,128)S(1)}, u32[]{:S(2)}, u32[]{:S(2)}) collective-permute-start(f32[2,40,128]{2,1,0:T(8,128)S(1)} %pad_maximum_fusion.refs_0_), channel_id=1, source_target_pairs={{0,8},{4,12},{8,0},{12,4},{16,24},{20,28},{24,16},{28,20},{1,9},{5... | collective-permute-start | bytes 122888 | tf_op jit(solution)/shard_map/ppermute | solution.py:294
  23.6 5.5 %collective-permute-start.5 = (f32[2,40,128]{2,1,0:T(8,128)S(1)}, f32[2,40,128]{2,1,0:T(8,128)S(1)}, u32[]{:S(2)}, u32[]{:S(2)}) collective-permute-start(f32[2,40,128]{2,1,0:T(8,128)S(1)} %pad_maximum_fusion.refs_0_), channel_id=1, source_target_pairs={{0,16},{4,20},{8,24},{12,28},{16,0},{20,4},{24,8},{28,12},{1,17},{... | collective-permute-start | bytes 122888 | tf_op jit(solution)/shard_map/ppermute | solution.py:294
  26.0 5.8 %collective-permute-start.6 = (f32[2,40,128]{2,1,0:T(8,128)S(1)}, f32[2,40,128]{2,1,0:T(8,128)S(1)}, u32[]{:S(2)}, u32[]{:S(2)}) collective-permute-start(f32[2,40,128]{2,1,0:T(8,128)S(1)} %pad_maximum_fusion.refs_0_), channel_id=1, source_target_pairs={{0,24},{4,28},{8,16},{12,20},{16,8},{20,12},{24,0},{28,4},{1,25},{... | collective-permute-start | bytes 122888 | tf_op jit(solution)/shard_map/ppermute | solution.py:294
  26.5 5.2 %copy-start = (s32[3]{0:T(128)S(1)}, s32[3]{0:T(128)}, u32[]{:S(2)}) copy-start(s32[3]{0:T(128)} %split_bin.1) | copy-start | bytes 40
  26.5 5.2 %copy-start.1 = (s32[8]{0:T(128)S(1)}, s32[8]{0:T(128)}, u32[]{:S(2)}) copy-start(s32[8]{0:T(128)} %slab_rows.3) | copy-start | bytes 100
  46.1 6.5 %collective-permute-start.7 = (f32[7,16,256]{2,1,0:T(8,128)S(1)}, f32[7,16,256]{2,1,0:T(8,128)S(1)}, u32[]{:S(2)}, u32[]{:S(2)}) collective-permute-start(f32[7,16,256]{2,1,0:T(8,128)S(1)} %gains.1), channel_id=1, source_target_pairs={{0,4},{4,0},{8,12},{12,8},{16,20},{20,16},{24,28},{28,24},{1,5},{5... | collective-permute-start | bytes 344072 | tf_op jit(solution)/shard_map/ppermute | solution.py:294
  46.6 6.6 %collective-permute-start.8 = (f32[7,16,256]{2,1,0:T(8,128)S(1)}, f32[7,16,256]{2,1,0:T(8,128)S(1)}, u32[]{:S(2)}, u32[]{:S(2)}) collective-permute-start(f32[7,16,256]{2,1,0:T(8,128)S(1)} %gains.1), channel_id=1, source_target_pairs={{0,8},{4,12},{8,0},{12,4},{16,24},{20,28},{24,16},{28,20},{1,9},{5... | collective-permute-start | bytes 344072 | tf_op jit(solution)/shard_map/ppermute | solution.py:294
  46.6 10.9 %collective-permute-start.9 = (f32[7,16,256]{2,1,0:T(8,128)S(1)}, f32[7,16,256]{2,1,0:T(8,128)S(1)}, u32[]{:S(2)}, u32[]{:S(2)}) collective-permute-start(f32[7,16,256]{2,1,0:T(8,128)S(1)} %gains.1), channel_id=1, source_target_pairs={{0,12},{4,8},{8,4},{12,0},{16,28},{20,24},{24,20},{28,16},{1,13},{... | collective-permute-start | bytes 344072 | tf_op jit(solution)/shard_map/ppermute | solution.py:294
  49.6 13.7 %collective-permute-start.10 = (f32[7,16,256]{2,1,0:T(8,128)S(1)}, f32[7,16,256]{2,1,0:T(8,128)S(1)}, u32[]{:S(2)}, u32[]{:S(2)}) collective-permute-start(f32[7,16,256]{2,1,0:T(8,128)S(1)} %gains.1), channel_id=1, source_target_pairs={{0,16},{4,20},{8,24},{12,28},{16,0},{20,4},{24,8},{28,12},{1,17},{... | collective-permute-start | bytes 344072 | tf_op jit(solution)/shard_map/ppermute | solution.py:294
  49.6 16.3 %collective-permute-start.11 = (f32[7,16,256]{2,1,0:T(8,128)S(1)}, f32[7,16,256]{2,1,0:T(8,128)S(1)}, u32[]{:S(2)}, u32[]{:S(2)}) collective-permute-start(f32[7,16,256]{2,1,0:T(8,128)S(1)} %gains.1), channel_id=1, source_target_pairs={{0,20},{4,16},{8,28},{12,24},{16,4},{20,0},{24,12},{28,8},{1,21},{... | collective-permute-start | bytes 344072 | tf_op jit(solution)/shard_map/ppermute | solution.py:294
  52.6 13.3 %collective-permute-start.12 = (f32[7,16,256]{2,1,0:T(8,128)S(1)}, f32[7,16,256]{2,1,0:T(8,128)S(1)}, u32[]{:S(2)}, u32[]{:S(2)}) collective-permute-start(f32[7,16,256]{2,1,0:T(8,128)S(1)} %gains.1), channel_id=1, source_target_pairs={{0,24},{4,28},{8,16},{12,20},{16,8},{20,12},{24,0},{28,4},{1,25},{... | collective-permute-start | bytes 344072 | tf_op jit(solution)/shard_map/ppermute | solution.py:294
  53.2 12.7 %collective-permute-start.13 = (f32[7,16,256]{2,1,0:T(8,128)S(1)}, f32[7,16,256]{2,1,0:T(8,128)S(1)}, u32[]{:S(2)}, u32[]{:S(2)}) collective-permute-start(f32[7,16,256]{2,1,0:T(8,128)S(1)} %gains.1), channel_id=1, source_target_pairs={{0,28},{4,24},{8,20},{12,16},{16,12},{20,8},{24,4},{28,0},{1,29},{... | collective-permute-start | bytes 344072 | tf_op jit(solution)/shard_map/ppermute | solution.py:294
  65.9 0.9 %copy-start.2 = (f32[7,128,256]{2,1,0:T(8,128)}, f32[7,128,256]{2,1,0:T(8,128)S(1)}, u32[]{:S(2)}) copy-start(f32[7,128,256]{2,1,0:T(8,128)S(1)} %constant_dynamic-update-slice_fusion.1) | copy-start | bytes 2752516

commit v3 on v2

--- a/solution.py
+++ b/solution.py
@@ -303,21 +303,28 @@
         share = pick_rows(fine_values, split_feature)
         share = share + swap(share, "feat", n_feat, 1)
         gh = jnp.concatenate([grad.astype(f32).reshape(-1, LO), hess.astype(f32).reshape(-1, LO)])
-        block = jnp.concatenate([share, gh])
-        mine, other = share, swap(block, "dp", n_dp, 1)
-        v, other_gh = other[: share.shape[0]], other[share.shape[0] :]
+        share, gh, block = lax.optimization_barrier((share, gh, jnp.concatenate([share, gh])))
+        got = [swap(block, "dp", n_dp, 1)]
         for x in range(2, n_feat, 2):
-            mine = mine + swap(share, "feat", n_feat, x)
-            v = v + swap(share, both, n_dp * n_feat, n_feat + x)
+            got.append(swap(share, "feat", n_feat, x))
+            got.append(swap(share, both, n_dp * n_feat, n_feat + x))
+        got = lax.optimization_barrier(got)
+        mine, v, other_gh = share, got[0][: share.shape[0]], got[0][share.shape[0] :]
+        for i in range(1, len(got), 2):
+            mine, v = mine + got[i], v + got[i + 1]
         pair = jnp.stack([jnp.concatenate([mine, gh]), jnp.concatenate([v, other_gh])])
         pairs = [pair] + [swap(pair, "dp", n_dp, d) for d in range(2, n_dp, 2)]
         blocks = lax.all_to_all(fine_values.reshape(n_dp, feats, row_dev), "dp", 0, 0)
         ch = route_rows(pairs, slab_rows, split_bin, n_dp, row_dev)
         gains = gains_of(blocks, ch, slab_rows)
+        pieces = [gains] + [None] * (n_dp - 1)
+        for d in [*range(n_dp - 2, 0, -2), 1]:
+            pieces[d] = swap(gains, "dp", n_dp, d)
+        for d in range(3, n_dp, 2):
+            pieces[d] = swap(pieces[d - 1], "dp", n_dp, 1)
         whole = jnp.zeros((7, feat_dev, BINS), f32)
         for d in range(n_dp):
-            piece = gains if d == 0 else swap(gains, "dp", n_dp, d)
-            whole = lax.dynamic_update_slice_in_dim(whole, piece, (me ^ d) * feats, 1)
+            whole = lax.dynamic_update_slice_in_dim(whole, pieces[d], (me ^ d) * feats, 1)
         return whole
 
     return shards

time: 68.5 us -> 63 us (0.920)
  starting transfers between devices: 27.6 us -> 23.4 us
  other arithmetic: 0.74 us -> 0.04 us
    ppermute x14, starting transfers between devices: 20.3 us -> 16.5 us  [swap(): return lax.ppermute(value, axis, [(s, s ^ step) for s in range(size)])]
    add x1, other arithmetic: 0.71 us -> 0.01 us  [shards(): share = share + swap(share, 'feat', n_feat, 1)]
  transfers between devices with their start and end apart: 15 -> 15, of which waited for: 8 -> 8; matrix products, arithmetic and copies ran while one was open for 1% -> 0% of each run, Pallas kernels for 6% -> 3%
where the time goes in v3:
time: 63 us; the launch traced here: 62.1 us
  starting transfers between devices  23.4 us (37%)
  waiting for transfers between devices  20.5 us (33%)
  Pallas kernels  16.3 us (26%)
  local copies, waits for them, and re-layouts  1.53 us (2%)
    ppermute x14, waiting for transfers between devices, swap(): return lax.ppermute(value, axis, [(s, s ^ step) for s in range(size)])  20.5 us
    ppermute x14, starting transfers between devices, swap(): return lax.ppermute(value, axis, [(s, s ^ step) for s in range(size)])  16.5 us
    pallas_call x1, Pallas kernels, gains_of(): pl.pallas_call(make_gains(n_dp, feats, row_dev), out_shape=jax.ShapeDtype...  12.3 us
    all_to_all x1, starting transfers between devices, shards(): lax.all_to_all(fine_values.reshape(n_dp, feats, row_dev), 'dp', 0, 0)  6.92 us
    pallas_call x1, Pallas kernels, pick_rows(): pl.pallas_call(make_pick(feat_dev, row_dev), out_shape=jax.ShapeDtypeStru...  2.15 us
    pallas_call x1, Pallas kernels, route_rows(): pl.pallas_call(make_route(n_dp, row_dev), out_shape=jax.ShapeDtypeStruct(...  1.88 us
  transfers between devices with their start and end apart: 15, of which 8 were waited for; matrix products, arithmetic and copies ran while one was open for 0% of the time, Pallas kernels for 3%

profile of v3, /device:TPU:0, one launch (start us, length us, event | category | flops | bytes accessed | tf_op | source)
XLA Modules:
  0.0 62.1 jit_solution(8401146191891278639)
XLA Ops:
  0.0 2.1 %pick.1 = f32[24,128]{1,0:T(8,128)} custom-call(s32[3]{0:T(128)} %split_feature.1, f32[128,1024]{1,0:T(8,128)} %x_ref.1), custom_call_target="tpu_custom_call" | custom-call | tf_op jit(solution)/shard_map/pick/pallas_call | solution.py:283
  2.2 0.5 collective-permute-start
  2.6 0.0 copy-start.4
  2.6 0.0 copy-start.5
  2.6 6.9 %all-to-all-start = ((f32[8,16,1024]{2,1,0:T(8,128)}), f32[8,16,1024]{2,1,0:T(8,128)S(1)}, u32[]{:S(2)}, u32[]{:S(2)}) async-start(f32[8,16,1024]{2,1,0:T(8,128)} %bitcast), calls=%async_computation | async-start | bytes 1048576 | tf_op jit(solution)/shard_map/all_to_all | solution.py:317
  9.6 0.0 copy-done.4
  9.6 0.0 copy-done.5
  9.6 0.0 copy-start.3
  9.6 0.0 collective-permute-done
  9.6 0.7 %copy-done.3 = f32[24,128]{1,0:T(8,128)S(1)} copy-done((f32[24,128]{1,0:T(8,128)S(1)}, f32[24,128]{1,0:T(8,128)}, u32[]{:S(2)}) %copy-start.3) | copy-done | bytes 12312
  10.3 2.0 %collective-permute-start.1 = (f32[40,128]{1,0:T(8,128)S(1)}, f32[40,128]{1,0:T(8,128)S(1)}, u32[]{:S(2)}, u32[]{:S(2)}) collective-permute-start(f32[40,128]{1,0:T(8,128)S(1)} %pad_maximum_fusion.1), channel_id=1, source_target_pairs={{0,4},{4,0},{8,12},{12,8},{16,20},{20,16},{24,28},{28,24},{1,5},{5... | collective-permute-start | bytes 61448 | tf_op jit(solution)/shard_map/ppermute | solution.py:294
  12.3 1.5 %collective-permute-start.2 = (f32[24,128]{1,0:T(8,128)S(1)}, f32[24,128]{1,0:T(8,128)S(1)}, u32[]{:S(2)}, u32[]{:S(2)}) collective-permute-start(f32[24,128]{1,0:T(8,128)S(1)} %add.33), channel_id=1, source_target_pairs={{0,2},{1,3},{2,0},{3,1},{4,6},{5,7},{6,4},{7,5},{8,10},{9,11},{10,... | collective-permute-start | bytes 36872 | tf_op jit(solution)/shard_map/ppermute | solution.py:294
  13.8 0.0 collective-permute-start.3
  13.8 2.2 %collective-permute-done.2 = f32[24,128]{1,0:T(8,128)S(1)} collective-permute-done((f32[24,128]{1,0:T(8,128)S(1)}, f32[24,128]{1,0:T(8,128)S(1)}, u32[]{:S(2)}, u32[]{:S(2)}) %collective-permute-start.2) | collective-permute-done | bytes 12320 | tf_op jit(solution)/shard_map/ppermute | solution.py:294
  16.0 2.4 %collective-permute-done.3 = f32[24,128]{1,0:T(8,128)S(1)} collective-permute-done((f32[24,128]{1,0:T(8,128)S(1)}, f32[24,128]{1,0:T(8,128)S(1)}, u32[]{:S(2)}, u32[]{:S(2)}) %collective-permute-start.3) | collective-permute-done | bytes 12320 | tf_op jit(solution)/shard_map/ppermute | solution.py:294
  18.4 0.0 collective-permute-done.1
  18.5 1.6 %collective-permute-start.4 = (f32[2,40,128]{2,1,0:T(8,128)S(1)}, f32[2,40,128]{2,1,0:T(8,128)S(1)}, u32[]{:S(2)}, u32[]{:S(2)}) collective-permute-start(f32[2,40,128]{2,1,0:T(8,128)S(1)} %pad_maximum_fusion.refs_0_), channel_id=1, source_target_pairs={{0,8},{4,12},{8,0},{12,4},{16,24},{20,28},{24,16},{28,20},{1,9},{5... | collective-permute-start | bytes 122888 | tf_op jit(solution)/shard_map/ppermute | solution.py:294
  20.1 2.4 %collective-permute-start.5 = (f32[2,40,128]{2,1,0:T(8,128)S(1)}, f32[2,40,128]{2,1,0:T(8,128)S(1)}, u32[]{:S(2)}, u32[]{:S(2)}) collective-permute-start(f32[2,40,128]{2,1,0:T(8,128)S(1)} %pad_maximum_fusion.refs_0_), channel_id=1, source_target_pairs={{0,16},{4,20},{8,24},{12,28},{16,0},{20,4},{24,8},{28,12},{1,17},{... | collective-permute-start | bytes 122888 | tf_op jit(solution)/shard_map/ppermute | solution.py:294
  22.5 0.5 collective-permute-start.6
  22.9 0.0 copy-start
  22.9 0.0 copy-start.1
  22.9 0.0 collective-permute-done.4.refs_1_
  22.9 4.5 %collective-permute-done.5.refs_2_ = f32[2,40,128]{2,1,0:T(8,128)S(1)} collective-permute-done((f32[2,40,128]{2,1,0:T(8,128)S(1)}, f32[2,40,128]{2,1,0:T(8,128)S(1)}, u32[]{:S(2)}, u32[]{:S(2)}) %collective-permute-start.5) | collective-permute-done | bytes 40992 | tf_op jit(solution)/shard_map/ppermute | solution.py:294
  27.4 0.9 %collective-permute-done.6.refs_3_ = f32[2,40,128]{2,1,0:T(8,128)S(1)} collective-permute-done((f32[2,40,128]{2,1,0:T(8,128)S(1)}, f32[2,40,128]{2,1,0:T(8,128)S(1)}, u32[]{:S(2)}, u32[]{:S(2)}) %collective-permute-start.6) | collective-permute-done | bytes 40992 | tf_op jit(solution)/shard_map/ppermute | solution.py:294
  28.3 0.0 copy-done
  28.3 0.0 copy-done.1
  28.3 1.9 %route.1.ch_ref = f32[9,8,1024]{2,1,0:T(8,128)S(1)} custom-call(s32[8]{0:T(128)S(1)} %copy-done.1, s32[3]{0:T(128)S(1)} %copy-done, f32[2,40,128]{2,1,0:T(8,128)S(1)} %pad_maximum_fusion.refs_0_, f32[2,40,128]{2,1,0:T(8,128)S(1)} %collective-permute-done.4.refs_1_, f32[2,40,128]{2,1,0:T(8,128)S(1)} %collective-permute-done.5.refs_2_, ...), custom_call_target="tpu_custom_call" | custom-call | flops 402653184 | bytes 262144 | tf_op jit(solution)/shard_map/route/pallas_call | solution.py:133
  30.2 0.0 all-to-all-done.x_ref
  30.2 12.3 %gains.1 = f32[7,16,256]{2,1,0:T(8,128)S(1)} custom-call(s32[8]{0:T(128)S(1)} %copy-done.1, f32[8,16,1024]{2,1,0:T(8,128)S(1)} %all-to-all-done.x_ref, f32[9,8,1024]{2,1,0:T(8,128)S(1)} %route.1.ch_ref), custom_call_target="tpu_custom_call" | custom-call | flops 8589934592 | bytes 1048576 | tf_op jit(solution)/shard_map/gains/pallas_call | solution.py:241
  42.5 1.2 %collective-permute-start.7 = (f32[7,16,256]{2,1,0:T(8,128)S(1)}, f32[7,16,256]{2,1,0:T(8,128)S(1)}, u32[]{:S(2)}, u32[]{:S(2)}) collective-permute-start(f32[7,16,256]{2,1,0:T(8,128)S(1)} %gains.1), channel_id=1, source_target_pairs={{0,4},{4,0},{8,12},{12,8},{16,20},{20,16},{24,28},{28,24},{1,5},{5... | collective-permute-start | bytes 344072 | tf_op jit(solution)/shard_map/ppermute | solution.py:294
  43.7 0.9 %collective-permute-start.8 = (f32[7,16,256]{2,1,0:T(8,128)S(1)}, f32[7,16,256]{2,1,0:T(8,128)S(1)}, u32[]{:S(2)}, u32[]{:S(2)}) collective-permute-start(f32[7,16,256]{2,1,0:T(8,128)S(1)} %gains.1), channel_id=1, source_target_pairs={{0,8},{4,12},{8,0},{12,4},{16,24},{20,28},{24,16},{28,20},{1,9},{5... | collective-permute-start | bytes 344072 | tf_op jit(solution)/shard_map/ppermute | solution.py:294
  44.6 0.6 %collective-permute-start.10 = (f32[7,16,256]{2,1,0:T(8,128)S(1)}, f32[7,16,256]{2,1,0:T(8,128)S(1)}, u32[]{:S(2)}, u32[]{:S(2)}) collective-permute-start(f32[7,16,256]{2,1,0:T(8,128)S(1)} %gains.1), channel_id=1, source_target_pairs={{0,16},{4,20},{8,24},{12,28},{16,0},{20,4},{24,8},{28,12},{1,17},{... | collective-permute-start | bytes 344072 | tf_op jit(solution)/shard_map/ppermute | solution.py:294
  45.3 2.8 %collective-permute-start.12 = (f32[7,16,256]{2,1,0:T(8,128)S(1)}, f32[7,16,256]{2,1,0:T(8,128)S(1)}, u32[]{:S(2)}, u32[]{:S(2)}) collective-permute-start(f32[7,16,256]{2,1,0:T(8,128)S(1)} %gains.1), channel_id=1, source_target_pairs={{0,24},{4,28},{8,16},{12,20},{16,8},{20,12},{24,0},{28,4},{1,25},{... | collective-permute-start | bytes 344072 | tf_op jit(solution)/shard_map/ppermute | solution.py:294
  48.1 0.1 broadcast_in_dim.3
  48.2 1.0 %collective-permute-done.8 = f32[7,16,256]{2,1,0:T(8,128)S(1)} collective-permute-done((f32[7,16,256]{2,1,0:T(8,128)S(1)}, f32[7,16,256]{2,1,0:T(8,128)S(1)}, u32[]{:S(2)}, u32[]{:S(2)}) %collective-permute-start.8) | collective-permute-done | bytes 114720 | tf_op jit(solution)/shard_map/ppermute | solution.py:294
  49.2 0.5 collective-permute-start.9
  49.7 5.7 %collective-permute-done.10 = f32[7,16,256]{2,1,0:T(8,128)S(1)} collective-permute-done((f32[7,16,256]{2,1,0:T(8,128)S(1)}, f32[7,16,256]{2,1,0:T(8,128)S(1)}, u32[]{:S(2)}, u32[]{:S(2)}) %collective-permute-start.10) | collective-permute-done | bytes 114720 | tf_op jit(solution)/shard_map/ppermute | solution.py:294
  55.4 0.4 collective-permute-start.11
  55.7 0.0 collective-permute-done.12
  55.7 1.7 %collective-permute-start.13 = (f32[7,16,256]{2,1,0:T(8,128)S(1)}, f32[7,16,256]{2,1,0:T(8,128)S(1)}, u32[]{:S(2)}, u32[]{:S(2)}) collective-permute-start(f32[7,16,256]{2,1,0:T(8,128)S(1)} %collective-permute-done.12), channel_id=1, source_target_pairs={{0,4},{4,0},{8,12},{12,8},{16,20},{20,16},{24,28},{28,24},{1,5},{5... | collective-permute-start | bytes 344072 | tf_op jit(solution)/shard_map/ppermute | solution.py:294
  57.4 0.0 collective-permute-done.7
  57.4 0.0 collective-permute-done.9
  57.5 2.7 %collective-permute-done.11 = f32[7,16,256]{2,1,0:T(8,128)S(1)} collective-permute-done((f32[7,16,256]{2,1,0:T(8,128)S(1)}, f32[7,16,256]{2,1,0:T(8,128)S(1)}, u32[]{:S(2)}, u32[]{:S(2)}) %collective-permute-start.11) | collective-permute-done | bytes 114720 | tf_op jit(solution)/shard_map/ppermute | solution.py:294
  60.2 0.0 copy-start.2
  60.2 1.2 %collective-permute-done.13 = f32[7,16,256]{2,1,0:T(8,128)S(1)} collective-permute-done((f32[7,16,256]{2,1,0:T(8,128)S(1)}, f32[7,16,256]{2,1,0:T(8,128)S(1)}, u32[]{:S(2)}, u32[]{:S(2)}) %collective-permute-start.13) | collective-permute-done | bytes 114720 | tf_op jit(solution)/shard_map/ppermute | solution.py:294
  61.4 0.0 copy-done.2
  61.4 0.7 %constant_dynamic-update-slice_fusion = f32[7,128,256]{2,1,0:T(8,128)} fusion(f32[7,128,256]{2,1,0:T(8,128)} %copy-done.2, f32[7,16,256]{2,1,0:T(8,128)S(1)} %collective-permute-done.13, s32[]{:T(128)S(6)} %select_n.31), kind=kLoop, calls=%fused_computation.8 | loop fusion | bytes 229380 | tf_op jit(solution)/shard_map/dynamic_update_slice | solution.py:327
  (17 shorter events, 0.1 us)
Async XLA Ops:
  2.2 7.5 %collective-permute-start = (f32[24,128]{1,0:T(8,128)}, f32[24,128]{1,0:T(8,128)S(1)}, u32[]{:S(2)}, u32[]{:S(2)}) collective-permute-start(f32[24,128]{1,0:T(8,128)} %pick.1), channel_id=1, source_target_pairs={{0,1},{1,0},{2,3},{3,2},{4,5},{5,4},{6,7},{7,6},{8,9},{9,8},{10,11... | collective-permute-start | bytes 36872 | tf_op jit(solution)/shard_map/ppermute | solution.py:294
  2.6 6.9 %copy-start.4 = (bf16[1024]{0:T(1024)(128)(2,1)S(1)}, bf16[1024]{0:T(1024)(128)(2,1)}, u32[]{:S(2)}) copy-start(bf16[1024]{0:T(1024)(128)(2,1)} %param.8) | copy-start | bytes 6148
  2.6 6.9 %copy-start.5 = (bf16[1024]{0:T(1024)(128)(2,1)S(1)}, bf16[1024]{0:T(1024)(128)(2,1)}, u32[]{:S(2)}) copy-start(bf16[1024]{0:T(1024)(128)(2,1)} %param.7) | copy-start | bytes 6148
  2.6 27.6 %all-to-all-start = ((f32[8,16,1024]{2,1,0:T(8,128)}), f32[8,16,1024]{2,1,0:T(8,128)S(1)}, u32[]{:S(2)}, u32[]{:S(2)}) async-start(f32[8,16,1024]{2,1,0:T(8,128)} %bitcast), calls=%async_computation | async-start | bytes 1048576 | tf_op jit(solution)/shard_map/all_to_all | solution.py:317
  9.6 0.7 %copy-start.3 = (f32[24,128]{1,0:T(8,128)S(1)}, f32[24,128]{1,0:T(8,128)}, u32[]{:S(2)}) copy-start(f32[24,128]{1,0:T(8,128)} %pick.1) | copy-start | bytes 36868
  10.3 8.1 %collective-permute-start.1 = (f32[40,128]{1,0:T(8,128)S(1)}, f32[40,128]{1,0:T(8,128)S(1)}, u32[]{:S(2)}, u32[]{:S(2)}) collective-permute-start(f32[40,128]{1,0:T(8,128)S(1)} %pad_maximum_fusion.1), channel_id=1, source_target_pairs={{0,4},{4,0},{8,12},{12,8},{16,20},{20,16},{24,28},{28,24},{1,5},{5... | collective-permute-start | bytes 61448 | tf_op jit(solution)/shard_map/ppermute | solution.py:294
  12.3 3.7 %collective-permute-start.2 = (f32[24,128]{1,0:T(8,128)S(1)}, f32[24,128]{1,0:T(8,128)S(1)}, u32[]{:S(2)}, u32[]{:S(2)}) collective-permute-start(f32[24,128]{1,0:T(8,128)S(1)} %add.33), channel_id=1, source_target_pairs={{0,2},{1,3},{2,0},{3,1},{4,6},{5,7},{6,4},{7,5},{8,10},{9,11},{10,... | collective-permute-start | bytes 36872 | tf_op jit(solution)/shard_map/ppermute | solution.py:294
  13.8 4.6 %collective-permute-start.3 = (f32[24,128]{1,0:T(8,128)S(1)}, f32[24,128]{1,0:T(8,128)S(1)}, u32[]{:S(2)}, u32[]{:S(2)}) collective-permute-start(f32[24,128]{1,0:T(8,128)S(1)} %add.33), channel_id=1, source_target_pairs={{0,6},{1,7},{2,4},{3,5},{4,2},{5,3},{6,0},{7,1},{8,14},{9,15},{10,... | collective-permute-start | bytes 36872 | tf_op jit(solution)/shard_map/ppermute | solution.py:294
  18.5 4.5 %collective-permute-start.4 = (f32[2,40,128]{2,1,0:T(8,128)S(1)}, f32[2,40,128]{2,1,0:T(8,128)S(1)}, u32[]{:S(2)}, u32[]{:S(2)}) collective-permute-start(f32[2,40,128]{2,1,0:T(8,128)S(1)} %pad_maximum_fusion.refs_0_), channel_id=1, source_target_pairs={{0,8},{4,12},{8,0},{12,4},{16,24},{20,28},{24,16},{28,20},{1,9},{5... | collective-permute-start | bytes 122888 | tf_op jit(solution)/shard_map/ppermute | solution.py:294
  20.1 7.3 %collective-permute-start.5 = (f32[2,40,128]{2,1,0:T(8,128)S(1)}, f32[2,40,128]{2,1,0:T(8,128)S(1)}, u32[]{:S(2)}, u32[]{:S(2)}) collective-permute-start(f32[2,40,128]{2,1,0:T(8,128)S(1)} %pad_maximum_fusion.refs_0_), channel_id=1, source_target_pairs={{0,16},{4,20},{8,24},{12,28},{16,0},{20,4},{24,8},{28,12},{1,17},{... | collective-permute-start | bytes 122888 | tf_op jit(solution)/shard_map/ppermute | solution.py:294
  22.5 5.8 %collective-permute-start.6 = (f32[2,40,128]{2,1,0:T(8,128)S(1)}, f32[2,40,128]{2,1,0:T(8,128)S(1)}, u32[]{:S(2)}, u32[]{:S(2)}) collective-permute-start(f32[2,40,128]{2,1,0:T(8,128)S(1)} %pad_maximum_fusion.refs_0_), channel_id=1, source_target_pairs={{0,24},{4,28},{8,16},{12,20},{16,8},{20,12},{24,0},{28,4},{1,25},{... | collective-permute-start | bytes 122888 | tf_op jit(solution)/shard_map/ppermute | solution.py:294
  22.9 5.4 %copy-start = (s32[3]{0:T(128)S(1)}, s32[3]{0:T(128)}, u32[]{:S(2)}) copy-start(s32[3]{0:T(128)} %split_bin.1) | copy-start | bytes 40
  22.9 5.4 %copy-start.1 = (s32[8]{0:T(128)S(1)}, s32[8]{0:T(128)}, u32[]{:S(2)}) copy-start(s32[8]{0:T(128)} %slab_rows.3) | copy-start | bytes 100
  42.5 14.9 %collective-permute-start.7 = (f32[7,16,256]{2,1,0:T(8,128)S(1)}, f32[7,16,256]{2,1,0:T(8,128)S(1)}, u32[]{:S(2)}, u32[]{:S(2)}) collective-permute-start(f32[7,16,256]{2,1,0:T(8,128)S(1)} %gains.1), channel_id=1, source_target_pairs={{0,4},{4,0},{8,12},{12,8},{16,20},{20,16},{24,28},{28,24},{1,5},{5... | collective-permute-start | bytes 344072 | tf_op jit(solution)/shard_map/ppermute | solution.py:294
  43.7 5.5 %collective-permute-start.8 = (f32[7,16,256]{2,1,0:T(8,128)S(1)}, f32[7,16,256]{2,1,0:T(8,128)S(1)}, u32[]{:S(2)}, u32[]{:S(2)}) collective-permute-start(f32[7,16,256]{2,1,0:T(8,128)S(1)} %gains.1), channel_id=1, source_target_pairs={{0,8},{4,12},{8,0},{12,4},{16,24},{20,28},{24,16},{28,20},{1,9},{5... | collective-permute-start | bytes 344072 | tf_op jit(solution)/shard_map/ppermute | solution.py:294
  44.6 10.7 %collective-permute-start.10 = (f32[7,16,256]{2,1,0:T(8,128)S(1)}, f32[7,16,256]{2,1,0:T(8,128)S(1)}, u32[]{:S(2)}, u32[]{:S(2)}) collective-permute-start(f32[7,16,256]{2,1,0:T(8,128)S(1)} %gains.1), channel_id=1, source_target_pairs={{0,16},{4,20},{8,24},{12,28},{16,0},{20,4},{24,8},{28,12},{1,17},{... | collective-permute-start | bytes 344072 | tf_op jit(solution)/shard_map/ppermute | solution.py:294
  45.3 10.5 %collective-permute-start.12 = (f32[7,16,256]{2,1,0:T(8,128)S(1)}, f32[7,16,256]{2,1,0:T(8,128)S(1)}, u32[]{:S(2)}, u32[]{:S(2)}) collective-permute-start(f32[7,16,256]{2,1,0:T(8,128)S(1)} %gains.1), channel_id=1, source_target_pairs={{0,24},{4,28},{8,16},{12,20},{16,8},{20,12},{24,0},{28,4},{1,25},{... | collective-permute-start | bytes 344072 | tf_op jit(solution)/shard_map/ppermute | solution.py:294
  49.2 8.2 %collective-permute-start.9 = (f32[7,16,256]{2,1,0:T(8,128)S(1)}, f32[7,16,256]{2,1,0:T(8,128)S(1)}, u32[]{:S(2)}, u32[]{:S(2)}) collective-permute-start(f32[7,16,256]{2,1,0:T(8,128)S(1)} %collective-permute-done.8), channel_id=1, source_target_pairs={{0,4},{4,0},{8,12},{12,8},{16,20},{20,16},{24,28},{28,24},{1,5},{5... | collective-permute-start | bytes 344072 | tf_op jit(solution)/shard_map/ppermute | solution.py:294
  55.4 4.8 %collective-permute-start.11 = (f32[7,16,256]{2,1,0:T(8,128)S(1)}, f32[7,16,256]{2,1,0:T(8,128)S(1)}, u32[]{:S(2)}, u32[]{:S(2)}) collective-permute-start(f32[7,16,256]{2,1,0:T(8,128)S(1)} %collective-permute-done.10), channel_id=1, source_target_pairs={{0,4},{4,0},{8,12},{12,8},{16,20},{20,16},{24,28},{28,24},{1,5},{5... | collective-permute-start | bytes 344072 | tf_op jit(solution)/shard_map/ppermute | solution.py:294
  55.7 5.7 %collective-permute-start.13 = (f32[7,16,256]{2,1,0:T(8,128)S(1)}, f32[7,16,256]{2,1,0:T(8,128)S(1)}, u32[]{:S(2)}, u32[]{:S(2)}) collective-permute-start(f32[7,16,256]{2,1,0:T(8,128)S(1)} %collective-permute-done.12), channel_id=1, source_target_pairs={{0,4},{4,0},{8,12},{12,8},{16,20},{20,16},{24,28},{28,24},{1,5},{5... | collective-permute-start | bytes 344072 | tf_op jit(solution)/shard_map/ppermute | solution.py:294
  60.2 1.2 %copy-start.2 = (f32[7,128,256]{2,1,0:T(8,128)}, f32[7,128,256]{2,1,0:T(8,128)S(1)}, u32[]{:S(2)}) copy-start(f32[7,128,256]{2,1,0:T(8,128)S(1)} %constant_dynamic-update-slice_fusion.1) | copy-start | bytes 2752516

commit v4 on v3

v4 whole, which is shorter than its diff:
```python
import jax
import jax.numpy as jnp
from jax import lax
from jax.experimental import pallas as pl
from jax.experimental.pallas import tpu as pltpu
from jax.sharding import PartitionSpec as P

FINE_BINS = 1024
BINS = 256
LO = 128
SIDE = 32
GROUP = 16
f32 = jnp.float32
bf16 = jnp.bfloat16
i32 = jnp.int32


def dot_nt(a, b):
    return lax.dot_general(a, b, (((1,), (1,)), ((), ())), preferred_element_type=f32)


def dot_nn(a, b):
    return jnp.dot(a, b, preferred_element_type=f32)


def iota(shape, axis):
    return lax.broadcasted_iota(i32, shape, axis)


def to_bf16(x):
    return x.astype(f32).astype(bf16)


def bytes_of(x, axis):
    return jnp.concatenate([to_bf16((x >> (8 * i)) & 255) for i in range(4)], axis)


def coarse_of(whole):
    n = whole.shape[0]
    r, c = iota((LO, 2 * LO), 0), iota((LO, 2 * LO), 1)
    same = r // SIDE == (c % LO) // SIDE
    in_row = dot_nn(bytes_of(whole, 0), to_bf16(same & ((r < c) | (c >= LO)))).astype(i32)
    in_row = sum(in_row[i * n : (i + 1) * n] << (8 * i) for i in range(4))
    before, row_total = in_row[:, :LO], in_row[:, LO:]
    r, c = iota((2 * n, n), 0), iota((2 * n, n), 1)
    same = (r % n) // SIDE == c // SIDE
    over = dot_nn(to_bf16(same & ((c < r) | (r >= n))), bytes_of(row_total, 1)).astype(i32)
    over = sum(over[:, i * LO : (i + 1) * LO] << (8 * i) for i in range(4))
    total = over[n:]
    remainder = before + over[:n]
    quotient = jnp.zeros_like(remainder)
    for _ in range(BINS.bit_length() - 1):
        remainder = remainder * 2
        bit = remainder >= total
        remainder = jnp.where(bit, remainder - total, remainder)
        quotient = quotient * 2 + bit.astype(i32)
    return jnp.minimum(BINS - 1, quotient)


def fine_of(v):
    return jnp.clip(jnp.floor(v * FINE_BINS), 0, FINE_BINS - 1)


def split_by(t, side):
    upper = jnp.floor(t * (1.0 / side))
    return upper, t - upper * side


def spread(rows, f):
    return jnp.broadcast_to(rows[f : f + 1], (16, rows.shape[1])).astype(bf16)


def hot(row, count, value, zero):
    at = iota(row.shape, 0)
    return [jnp.where(row == to_bf16(at + 16 * j), value, zero) for j in range(count // 16)]


def list_blocks(slab_rows, list_ref, n_dp, tiles):
    used = 0
    for s in range(n_dp):
        for i in range(tiles):
            list_ref[used + i] = s * tiles + i
        used = used + (slab_rows[s] + LO - 1) // LO
    for i in range(GROUP - 1):
        list_ref[used + i] = n_dp * tiles
    return used


def list_shape(n_dp, tiles):
    return pltpu.SMEM((n_dp * tiles + GROUP,), i32)


def params():
    return pltpu.CompilerParams(vmem_limit_bytes=40 * 2**20)


def cost(flops):
    return pl.CostEstimate(flops=flops, bytes_accessed=2**20, transcendentals=0)


def make_bins(n_dp, groups, tiles):
    blocks = n_dp * tiles
    feats = groups * 8
    quads = feats // 4
    width = GROUP * LO

    def kernel(slab_rows, x_ref, o_ref, list_ref, h_ref, cnt_ref, cut_ref, map_ref):
        used = list_blocks(slab_rows, list_ref, n_dp, tiles)
        row = iota((tiles, LO), 0) * LO + iota((tiles, LO), 1)
        for s in range(n_dp):
            h = jnp.where(row < slab_rows[s], x_ref[s, groups * tiles + 1], 0.0)
            for i in range(tiles):
                h_ref[s * tiles + i] = jnp.broadcast_to(h[i : i + 1], (8, LO))
        h_ref[blocks] = jnp.zeros((8, LO), f32)
        cnt_ref[...] = jnp.zeros_like(cnt_ref)
        one, zero = jnp.ones((16, width), bf16), jnp.zeros((16, width), bf16)

        def fine_block(at):
            s, i = jnp.minimum(at // tiles, n_dp - 1), at % tiles
            return fine_of(jnp.concatenate([x_ref[s, g * tiles + i] for g in range(groups)], 0))

        def count(q, _):
            ts, hs = [], []
            for i in range(GROUP):
                at = list_ref[q * GROUP + i]
                ts.append(fine_block(at))
                hs.append(h_ref[at])
            h = jnp.concatenate(hs, 1)
            h = jnp.concatenate([h, h], 0).astype(bf16)
            upper, lower = split_by(jnp.concatenate(ts, 1), SIDE)
            for quad in range(quads):
                left, right = [], []
                for f in range(quad * 4, quad * 4 + 4):
                    left += hot(spread(upper, f), SIDE, h, zero)
                    right += hot(spread(lower, f), SIDE, one, zero)
                cnt_ref[quad] += dot_nt(jnp.concatenate(left, 0), jnp.concatenate(right, 0))
            return 0

        rounds = (used + GROUP - 1) // GROUP
        lax.fori_loop(0, rounds, count, 0)
        counts = []
        for quad in range(quads):
            lane = iota((SIDE, LO), 1) // SIDE
            mine = cnt_ref[quad, :SIDE]
            for i in range(1, 4):
                mine = jnp.where(lane == i, cnt_ref[quad, i * SIDE : (i + 1) * SIDE], mine)
            counts.append(mine)
        counts = jnp.concatenate(counts, 0)
        cut_ref[...] = coarse_of((counts * 16384.0).astype(i32)).astype(f32)
        lane = iota((quads * 8, LO), 1) // SIDE
        sub = iota((8, LO), 0)
        rows = [cut_ref[pl.ds(i, quads * 8, 4), :] for i in range(4)]
        words = [jnp.zeros((8, LO), i32) for _ in range(quads)]
        for q in range(4):
            table = jnp.zeros((quads * 8, LO), f32)
            for i in range(4):
                shift = (i - q) * SIDE % LO
                moved = pltpu.roll(rows[i], shift, 1) if shift else rows[i]
                table = jnp.where(lane == i, moved, table)
            for quad in range(quads):
                word = table[quad * 8 : quad * 8 + 8].astype(i32) << (sub % 4 * 8)
                word = word + pltpu.roll(word, 7, 0)
                word = word + pltpu.roll(word, 6, 0)
                word = pltpu.roll(word, q, 0) if q else word
                words[quad] = jnp.where(sub % 4 == q, word, words[quad])
        for quad in range(quads):
            map_ref[quad] = words[quad]
        upper_half = sub >= 4

        def look_up(q, _):
            for i in range(GROUP):
                at = list_ref[q * GROUP + i]
                fine = fine_block(at).astype(i32)
                for g in range(groups):
                    here = fine[g * 8 : g * 8 + 8]
                    turned = pltpu.roll(here, 4, 0)
                    found = []
                    for half in range(2):
                        t = jnp.where(upper_half, turned, here) if half == 0 else jnp.where(upper_half, here, turned)
                        word = jnp.take_along_axis(map_ref[g * 2 + half], t & (LO - 1), axis=1, mode="promise_in_bounds")
                        value = (word >> ((t >> 4) & 24)) & 255
                        value = jnp.where((t >= FINE_BINS // 2) == upper_half, value, 0)
                        found.append(value + pltpu.roll(value, 4, 0))
                    o_ref[at, g * 8 : g * 8 + 8, :] = jnp.where(upper_half, found[1], found[0]).astype(f32)
            return 0

        lax.fori_loop(0, rounds, look_up, 0)

    return kernel


def find_bins(x, slab_rows, groups, tiles):
    n_dp = x.shape[0]
    feats = groups * 8
    smem = pl.BlockSpec(memory_space=pltpu.SMEM)
    vmem = pl.BlockSpec(memory_space=pltpu.VMEM)
    return pl.pallas_call(
        make_bins(n_dp, groups, tiles),
        out_shape=jax.ShapeDtypeStruct((n_dp * tiles + 1, feats, LO), f32),
        in_specs=[smem, vmem],
        out_specs=vmem,
        scratch_shapes=[
            list_shape(n_dp, tiles),
            pltpu.VMEM((n_dp * tiles + 1, 8, LO), f32),
            pltpu.VMEM((feats // 4, LO, LO), f32),
            pltpu.VMEM((feats // 4 * SIDE, LO), f32),
            pltpu.VMEM((feats // 4, 8, LO), i32),
        ],
        compiler_params=params(),
        cost_estimate=cost(2 * 128 * 128 * n_dp * tiles * LO * feats // 4),
        name="bins",
    )(slab_rows, x)


def make_route(n_dp, groups, tiles):
    blocks = n_dp * tiles

    def kernel(slab_rows, split_bin, x_ref, *refs):
        pairs, ch_ref, t_ref = refs[: n_dp // 2], refs[n_dp // 2], refs[n_dp // 2 + 1]
        me = lax.axis_index("dp")
        one, zero = jnp.ones((16, LO), bf16), jnp.zeros((16, LO), bf16)
        counts = jnp.zeros((LO, LO), f32)
        nothing = [zero] * (SIDE // 16)
        for j in range(n_dp):
            s = me ^ j
            row = iota((tiles, LO), 0) * LO + iota((tiles, LO), 1)
            live = row < slab_rows[s]
            t_ref[j, 3] = jnp.where(live, x_ref[s, groups * tiles], 0.0)
            h = jnp.where(live, x_ref[s, groups * tiles + 1], 0.0)
            t_ref[j, 4] = h
            lefts, rights = [], []
            hs = [spread(h, i) for i in range(tiles)]
            for n in range(3):
                t = fine_of(pairs[j // 2][j % 2, n * tiles : (n + 1) * tiles])
                t_ref[j, n] = t
                upper, lower = split_by(t, SIDE)
                left = [jnp.concatenate(hot(spread(upper, i), SIDE, hs[i], zero), 0) for i in range(tiles)]
                right = [jnp.concatenate(hot(spread(lower, i), SIDE, one, zero), 0) for i in range(tiles)]
                lefts.append(jnp.concatenate(left, 1))
                rights.append(jnp.concatenate(right, 1))
            empty = jnp.zeros((SIDE, tiles * LO), bf16)
            counts += dot_nt(jnp.concatenate(lefts + [empty], 0), jnp.concatenate(rights + [empty], 0))
        lane = iota((SIDE, LO), 1)
        mine = counts[:SIDE]
        for n in range(1, 3):
            mine = jnp.where(lane // SIDE == n, counts[n * SIDE : (n + 1) * SIDE], mine)
        mine = jnp.where(lane < 3 * SIDE, (mine * 16384.0).astype(i32), 1)
        cut = coarse_of(mine)
        bound = jnp.where(lane < SIDE, split_bin[0], jnp.where(lane < 2 * SIDE, split_bin[1], split_bin[2]))
        below = jnp.sum(jnp.where(cut <= bound, 1.0, 0.0), axis=0, keepdims=True)
        lane = lane[:1]
        cuts = [jnp.sum(jnp.where(lane // SIDE == n, below, 0.0), axis=1, keepdims=True) for n in range(3)]
        ch_ref[blocks] = jnp.zeros((8, LO), f32)
        at = iota((8, LO), 0)
        for j in range(n_dp):
            s = me ^ j
            l0, l1, l2 = [t_ref[j, n] < cuts[n] for n in range(3)]
            leaf = jnp.where(l0, jnp.where(l1, 0, 1), jnp.where(l2, 2, 3))
            g, h = t_ref[j, 3], t_ref[j, 4]
            for i in range(tiles):
                gh = jnp.where(at < 4, jnp.broadcast_to(g[i : i + 1], (8, LO)), jnp.broadcast_to(h[i : i + 1], (8, LO)))
                here = at % 4 == jnp.broadcast_to(leaf[i : i + 1], (8, LO))
                ch_ref[s * tiles + i] = jnp.where(here, gh, 0.0)

    return kernel


def make_gains(n_dp, feats_all, feats, tiles):
    quads = feats_all // 4
    width = GROUP * LO
    inner = 64

    def kernel(slab_rows, bin_ref, ch_ref, o_ref, list_ref, acc_ref, cum_ref):
        used = list_blocks(slab_rows, list_ref, n_dp, tiles)
        acc_ref[...] = jnp.zeros_like(acc_ref)
        kk = [to_bf16(iota((16, width), 0) // 8 + 2 * j) for j in range(2)]
        one, zero = jnp.ones((16, width), bf16), jnp.zeros((16, width), bf16)
        lane = iota((inner, LO), 1) // SIDE

        def add(q, _):
            bs, chs = [], []
            for i in range(GROUP):
                at = list_ref[q * GROUP + i]
                bs.append(bin_ref[at])
                chs.append(ch_ref[at])
            ch = jnp.concatenate(chs, 1)
            ch = jnp.concatenate([ch, ch], 0).astype(bf16)
            upper, lower = split_by(jnp.concatenate(bs, 1), inner)
            for quad in range(quads):
                left, right = [], []
                for f in range(quad * 4, quad * 4 + 4):
                    left += hot(spread(lower, f), inner, one, zero)
                    u = spread(upper, f)
                    right += [jnp.where(u == k, ch, zero) for k in kk]
                out = dot_nt(jnp.concatenate(left, 0), jnp.concatenate(right, 0))
                mine = out[:inner]
                for i in range(1, 4):
                    mine = jnp.where(lane == i, out[i * inner : (i + 1) * inner], mine)
                acc_ref[quad] += mine
            return 0

        lax.fori_loop(0, (used + GROUP - 1) // GROUP, add, 0)
        r, c = iota((inner, LO), 0), iota((inner, LO), 1)
        upto = to_bf16((r <= c) | (c >= inner))
        pad = jnp.zeros((LO - inner, LO), f32)
        for quad in range(quads):
            acc = jnp.transpose(jnp.concatenate([acc_ref[quad], pad], 0))[:, :inner]
            p0 = acc.astype(bf16)
            r1 = acc - p0.astype(f32)
            p1 = r1.astype(bf16)
            p2 = (r1 - p1.astype(f32)).astype(bf16)
            run = (dot_nn(p0, upto) + dot_nn(p1, upto)) + dot_nn(p2, upto)
            whole = pltpu.roll(run, inner, 1)
            first = iota((8, LO), 1) < inner
            for i in range(4):
                f = quad * 4 + i
                if f >= feats:
                    break
                base = jnp.zeros((8, LO), f32)
                for k in range(0, 4, 2):
                    a = (i * 4 + k) * 8
                    ta = jnp.where(first, whole[a : a + 8], run[a : a + 8])
                    tb = jnp.where(first, whole[a + 8 : a + 16], run[a + 8 : a + 16])
                    gl = base + jnp.where(first, run[a : a + 8], ta + whole[a + 8 : a + 16])
                    base = base + (ta + tb)
                    for c in range(8):
                        cum_ref[c, f : f + 1, k // 2 * LO : k // 2 * LO + LO] = gl[c : c + 1]

        def score(g, h):
            return g * g / (h + 1.0)

        def nodes(at):
            leaves = [cum_ref[at + c] for c in range(4)]
            a, b = leaves[0] + leaves[1], leaves[2] + leaves[3]
            return [a + b, a, b] + leaves

        for i, (gl, hl) in enumerate(zip(nodes(0), nodes(4))):
            g, h = gl[:, BINS - 1 :], hl[:, BINS - 1 :]
            o_ref[i] = score(gl, hl) + score(g - gl, h - hl) - score(g, h)

    return kernel


def route_and_sum(x, pairs, bins, slab_rows, split_bin, feats, groups, tiles):
    n_dp = x.shape[0]
    blocks, feats_all = n_dp * tiles, groups * 8
    smem = pl.BlockSpec(memory_space=pltpu.SMEM)
    vmem = pl.BlockSpec(memory_space=pltpu.VMEM)
    route = make_route(n_dp, groups, tiles)
    sum_up = make_gains(n_dp, feats_all, feats, tiles)

    def kernel(slab_rows, split_bin, x_ref, bin_ref, *refs):
        o_ref, list_ref, ch_ref, t_ref, acc_ref, cum_ref = refs[n_dp // 2 :]
        route(slab_rows, split_bin, x_ref, *refs[: n_dp // 2], ch_ref, t_ref)
        sum_up(slab_rows, bin_ref, ch_ref, o_ref, list_ref, acc_ref, cum_ref)

    return pl.pallas_call(
        kernel,
        out_shape=jax.ShapeDtypeStruct((7, feats, BINS), f32),
        in_specs=[smem, smem] + [vmem] * (2 + len(pairs)),
        out_specs=vmem,
        scratch_shapes=[
            list_shape(n_dp, tiles),
            pltpu.VMEM((blocks + 1, 8, LO), f32),
            pltpu.VMEM((n_dp, 5, tiles, LO), f32),
            pltpu.VMEM((feats_all // 4, 64, LO), f32),
            pltpu.VMEM((8, feats, BINS), f32),
        ],
        compiler_params=params(),
        cost_estimate=cost(2 * 128 * 256 * blocks * LO * feats_all // 4),
        name="gains",
    )(slab_rows, split_bin, x, bins, *pairs)


def make_pick(groups, tiles, feat_dev, feats):
    def kernel(split_feature, x_ref, g_ref, h_ref, o_ref, x_out, sems):
        me = lax.axis_index("feat")
        n_dp = x_ref.shape[0]
        size = groups * tiles
        copies = [pltpu.make_async_copy(x_ref.at[s], x_out.at[s, pl.ds(0, size)], sems.at[s]) for s in range(n_dp)]
        for copy in copies:
            copy.start()
        g, h = g_ref[...].astype(f32), h_ref[...].astype(f32)
        for s in range(n_dp):
            x_out[s, size] = g
            x_out[s, size + 1] = h
        for copy in copies:
            copy.wait()
        at8 = iota((8, LO), 0)
        for n in range(3):
            local = split_feature[n] - me * feat_dev
            owned = (local >= 0) & (local < feat_dev)
            at = jnp.clip(local, 0, feat_dev - 1)
            s, f = at // feats, at % feats
            mine = (at8 == f % 8) & owned
            for i in range(tiles):
                tile = x_out[s, f // 8 * tiles + i]
                o_ref[n * tiles + i : n * tiles + i + 1, :] = jnp.sum(jnp.where(mine, tile, 0.0), axis=0, keepdims=True)

    return kernel


def pick_rows(x, grad, hess, split_feature, groups, tiles, feat_dev):
    n_dp = x.shape[0]
    smem = pl.BlockSpec(memory_space=pltpu.SMEM)
    vmem = pl.BlockSpec(memory_space=pltpu.VMEM)
    return pl.pallas_call(
        make_pick(groups, tiles, feat_dev, feat_dev // n_dp),
        out_shape=[
            jax.ShapeDtypeStruct((3 * tiles, LO), f32),
            jax.ShapeDtypeStruct((n_dp, groups * tiles + 2, 8, LO), f32),
        ],
        in_specs=[smem, pl.BlockSpec(memory_space=pl.ANY), vmem, vmem],
        out_specs=[vmem, vmem],
        scratch_shapes=[pltpu.SemaphoreType.DMA((n_dp,))],
        name="pick",
    )(split_feature, x, grad.reshape(tiles, LO), hess.reshape(tiles, LO))


def swap(value, axis, size, step):
    return lax.ppermute(value, axis, [(s, s ^ step) for s in range(size)])


def make_shards(n_dp, n_feat):
    def shards(fine_values, grad, hess, slab_rows, split_feature, split_bin):
        feat_dev, row_dev = fine_values.shape
        feats, tiles = feat_dev // n_dp, row_dev // LO
        groups = (feats + 7) // 8
        me = lax.axis_index("dp")
        both = ("dp", "feat")
        x = fine_values.reshape(n_dp, feats, tiles, LO)
        x = jnp.pad(x, ((0, 0), (0, groups * 8 - feats), (0, 0), (0, 0)))
        x = x.reshape(n_dp, groups, 8, tiles, LO).swapaxes(2, 3).reshape(n_dp, groups * tiles, 8, LO)
        share, x = pick_rows(x, grad, hess, split_feature, groups, tiles, feat_dev)
        share = share + swap(share, "feat", n_feat, 1)
        got = [swap(share, "dp", n_dp, 1)]
        for i in range(2, n_feat, 2):
            got.append(swap(share, "feat", n_feat, i))
            got.append(swap(share, both, n_dp * n_feat, n_feat + i))
        got = lax.optimization_barrier(got)
        mine, other = share, got[0]
        for i in range(1, len(got), 2):
            mine, other = mine + got[i], other + got[i + 1]
        pair = jnp.stack([mine, other])
        pairs = [pair] + [swap(pair, "dp", n_dp, d) for d in range(2, n_dp, 2)]
        x = lax.all_to_all(x, "dp", 0, 0)
        bins = find_bins(x, slab_rows, groups, tiles)
        gains = route_and_sum(x, pairs, bins, slab_rows, split_bin, feats, groups, tiles)
        pieces = [gains] + [None] * (n_dp - 1)
        for d in [*range(n_dp - 2, 0, -2), 1]:
            pieces[d] = swap(gains, "dp", n_dp, d)
        for d in range(3, n_dp, 2):
            pieces[d] = swap(pieces[d - 1], "dp", n_dp, 1)
        whole = jnp.zeros((7, feat_dev, BINS), f32)
        order = [4, 2, 1] + [*range(6, n_dp, 2)] + [*range(3, n_dp, 2)]
        for d in [0] + [d for d in order if d < n_dp]:
            whole = lax.dynamic_update_slice_in_dim(whole, pieces[d], (me ^ d) * feats, 1)
        return whole

    return shards


def solution(mesh):
    return jax.shard_map(
        make_shards(mesh.shape["dp"], mesh.shape["feat"]),
        mesh=mesh,
        in_specs=(P("feat", "dp"), P("dp"), P("dp"), P(), P(), P()),
        out_specs=P(None, "feat", None),
        check_vma=False,
    )
```

time: 63 us -> 55.6 us (0.88)
  waiting for transfers between devices: 20.5 us -> 13 us
  starting transfers between devices: 23.4 us -> 27.9 us
  Pallas kernels: 16.3 us -> 13.3 us
  local copies, waits for them, and re-layouts: 1.53 us -> 0.84 us
    ppermute x14, waiting for transfers between devices: 20.5 us -> 9.58 us  [swap(): return lax.ppermute(value, axis, [(s, s ^ step) for s in range(size)])]
    ppermute x14, starting transfers between devices: 16.5 us -> 20.6 us  [swap(): return lax.ppermute(value, axis, [(s, s ^ step) for s in range(size)])]
    all_to_all x1, waiting for transfers between devices: 0.01 us -> 3.43 us  [shards(): x = lax.all_to_all(x, 'dp', 0, 0)]
    pallas_call x3, Pallas kernels: 16.3 us -> 13.3 us  [the longest x1 6.14 us: route_and_sum(): pl.pallas_call(kernel, out_shape=jax.ShapeDtypeStruct((7, feats, BINS), f...]
    unnamed x12 -> x8, local copies, waits for them, and re-layouts: 0.7 us -> 0.02 us
  transfers between devices with their start and end apart: 15 -> 15, of which waited for: 8 -> 8; matrix products, arithmetic and copies ran while one was open for 0% -> 0% of each run, Pallas kernels for 3% -> 8%
where the time goes in v4:
time: 55.6 us; the launch traced here: 55.3 us
  starting transfers between devices  27.9 us (50%)
  Pallas kernels  13.3 us (24%)
  waiting for transfers between devices  13 us (23%)
  local copies, waits for them, and re-layouts  0.84 us (2%)
    ppermute x14, starting transfers between devices, swap(): return lax.ppermute(value, axis, [(s, s ^ step) for s in range(size)])  20.6 us
    ppermute x14, waiting for transfers between devices, swap(): return lax.ppermute(value, axis, [(s, s ^ step) for s in range(size)])  9.58 us
    all_to_all x1, starting transfers between devices, shards(): x = lax.all_to_all(x, 'dp', 0, 0)  7.29 us
    pallas_call x1, Pallas kernels, route_and_sum(): pl.pallas_call(kernel, out_shape=jax.ShapeDtypeStruct((7, feats, BINS), f...  6.14 us
    pallas_call x1, Pallas kernels, find_bins(): pl.pallas_call(make_bins(n_dp, groups, tiles), out_shape=jax.ShapeDtypeSt...  4.51 us
    all_to_all x1, waiting for transfers between devices, shards(): x = lax.all_to_all(x, 'dp', 0, 0)  3.43 us
    pallas_call x1, Pallas kernels, pick_rows(): pl.pallas_call(make_pick(groups, tiles, feat_dev, feat_dev // n_dp), out_...  2.65 us
  transfers between devices with their start and end apart: 15, of which 8 were waited for; matrix products, arithmetic and copies ran while one was open for 0% of the time, Pallas kernels for 8%

profile of v4, /device:TPU:0, one launch (start us, length us, event | category | flops | bytes accessed | tf_op | source)
XLA Modules:
  0.0 55.3 jit_solution(7174201874356413672)
XLA Ops:
  0.0 2.7 %pick.1 = (f32[24,128]{1,0:T(8,128)}, f32[8,18,8,128]{3,2,1,0:T(8,128)}) custom-call(s32[3]{0:T(128)} %split_feature.1, f32[8,16,8,128]{3,2,1,0:T(8,128)} %bitcast.11, bf16[8,128]{1,0:T(8,128)(2,1)} %bitcast.12, bf16[8,128]{1,0:T(8,128)(2,1)} %bitcast.13), custom_call_target="tpu_custom_call" | custom-call | tf_op jit(solution)/shard_map/pick/pallas_call | solution.py:407
  2.7 0.0 copy-start.3
  2.7 7.3 %all-to-all-start = ((f32[8,18,8,128]{3,2,1,0:T(8,128)}), f32[8,18,8,128]{3,2,1,0:T(8,128)S(1)}, u32[]{:S(2)}, u32[]{:S(2)}) async-start(f32[8,18,8,128]{3,2,1,0:T(8,128)} %get-tuple-element.10), calls=%async_computation | async-start | bytes 1179648 | tf_op jit(solution)/shard_map/all_to_all | solution.py:446
  10.0 0.0 copy-done.3
  10.0 0.1 collective-permute-start
  10.0 1.2 %collective-permute-done = f32[24,128]{1,0:T(8,128)S(1)} collective-permute-done((f32[24,128]{1,0:T(8,128)S(1)}, f32[24,128]{1,0:T(8,128)S(1)}, u32[]{:S(2)}, u32[]{:S(2)}) %collective-permute-start) | collective-permute-done | bytes 12320 | tf_op jit(solution)/shard_map/ppermute | solution.py:421
  11.2 2.0 %collective-permute-start.1 = (f32[24,128]{1,0:T(8,128)S(1)}, f32[24,128]{1,0:T(8,128)S(1)}, u32[]{:S(2)}, u32[]{:S(2)}) collective-permute-start(f32[24,128]{1,0:T(8,128)S(1)} %add.33), channel_id=1, source_target_pairs={{0,4},{4,0},{8,12},{12,8},{16,20},{20,16},{24,28},{28,24},{1,5},{5... | collective-permute-start | bytes 36872 | tf_op jit(solution)/shard_map/ppermute | solution.py:421
  13.2 1.5 %collective-permute-start.2 = (f32[24,128]{1,0:T(8,128)S(1)}, f32[24,128]{1,0:T(8,128)S(1)}, u32[]{:S(2)}, u32[]{:S(2)}) collective-permute-start(f32[24,128]{1,0:T(8,128)S(1)} %add.33), channel_id=1, source_target_pairs={{0,2},{1,3},{2,0},{3,1},{4,6},{5,7},{6,4},{7,5},{8,10},{9,11},{10,... | collective-permute-start | bytes 36872 | tf_op jit(solution)/shard_map/ppermute | solution.py:421
  14.7 0.0 collective-permute-start.3
  14.7 2.0 %collective-permute-done.1 = f32[24,128]{1,0:T(8,128)S(1)} collective-permute-done((f32[24,128]{1,0:T(8,128)S(1)}, f32[24,128]{1,0:T(8,128)S(1)}, u32[]{:S(2)}, u32[]{:S(2)}) %collective-permute-start.1) | collective-permute-done | bytes 12320 | tf_op jit(solution)/shard_map/ppermute | solution.py:421
  16.7 0.2 collective-permute-done.2
  16.9 2.4 %collective-permute-done.3 = f32[24,128]{1,0:T(8,128)S(1)} collective-permute-done((f32[24,128]{1,0:T(8,128)S(1)}, f32[24,128]{1,0:T(8,128)S(1)}, u32[]{:S(2)}, u32[]{:S(2)}) %collective-permute-start.3) | collective-permute-done | bytes 12320 | tf_op jit(solution)/shard_map/ppermute | solution.py:421
  19.3 0.0 copy-start
  19.3 0.0 copy-start.1
  19.3 1.5 %collective-permute-start.4 = (f32[2,24,128]{2,1,0:T(8,128)S(1)}, f32[2,24,128]{2,1,0:T(8,128)S(1)}, u32[]{:S(2)}, u32[]{:S(2)}) collective-permute-start(f32[2,24,128]{2,1,0:T(8,128)S(1)} %pad_maximum_fusion.refs_0_), channel_id=1, source_target_pairs={{0,8},{4,12},{8,0},{12,4},{16,24},{20,28},{24,16},{28,20},{1,9},{5... | collective-permute-start | bytes 73736 | tf_op jit(solution)/shard_map/ppermute | solution.py:421
  20.8 2.5 %collective-permute-start.5 = (f32[2,24,128]{2,1,0:T(8,128)S(1)}, f32[2,24,128]{2,1,0:T(8,128)S(1)}, u32[]{:S(2)}, u32[]{:S(2)}) collective-permute-start(f32[2,24,128]{2,1,0:T(8,128)S(1)} %pad_maximum_fusion.refs_0_), channel_id=1, source_target_pairs={{0,16},{4,20},{8,24},{12,28},{16,0},{20,4},{24,8},{28,12},{1,17},{... | collective-permute-start | bytes 73736 | tf_op jit(solution)/shard_map/ppermute | solution.py:421
  23.3 0.4 collective-permute-start.6
  23.7 3.4 %all-to-all-done.x_ref = f32[8,18,8,128]{3,2,1,0:T(8,128)S(1)} async-done(((f32[8,18,8,128]{3,2,1,0:T(8,128)}), f32[8,18,8,128]{3,2,1,0:T(8,128)S(1)}, u32[]{:S(2)}, u32[]{:S(2)}) %all-to-all-start) | async-done | bytes 589856 | tf_op jit(solution)/shard_map/all_to_all | solution.py:446
  27.2 0.0 copy-done
  27.2 4.5 %bins.1.bin_ref = f32[65,16,128]{2,1,0:T(8,128)S(1)} custom-call(s32[8]{0:T(128)S(1)} %copy-done, f32[8,18,8,128]{3,2,1,0:T(8,128)S(1)} %all-to-all-done.x_ref), custom_call_target="tpu_custom_call" | custom-call | flops 1073741824 | bytes 1048576 | tf_op jit(solution)/shard_map/bins/pallas_call | solution.py:197
  31.7 0.0 collective-permute-done.4.refs_1_
  31.7 0.0 collective-permute-done.5.refs_2_
  31.7 0.0 collective-permute-done.6.refs_3_
  31.7 0.0 copy-done.1
  31.7 6.1 %gains.1 = f32[7,16,256]{2,1,0:T(8,128)S(1)} custom-call(s32[8]{0:T(128)S(1)} %copy-done, s32[3]{0:T(128)S(1)} %copy-done.1, f32[8,18,8,128]{3,2,1,0:T(8,128)S(1)} %all-to-all-done.x_ref, f32[65,16,128]{2,1,0:T(8,128)S(1)} %bins.1.bin_ref, f32[2,24,128]{2,1,0:T(8,128)S(1)} %pad_maximum_fusion.refs_0_, f32[2,24,128]{2,1,0:T(8,128)S(1)} %collective-permute-done.4.refs_1_, ...), custom_call_target="tpu_custom_call" | custom-call | flops 2147483648 | bytes 1048576 | tf_op jit(solution)/shard_map/gains/pallas_call | solution.py:357
  37.9 0.1 collective-permute-start.7
  38.0 1.5 %collective-permute-start.8 = (f32[7,16,256]{2,1,0:T(8,128)S(1)}, f32[7,16,256]{2,1,0:T(8,128)S(1)}, u32[]{:S(2)}, u32[]{:S(2)}) collective-permute-start(f32[7,16,256]{2,1,0:T(8,128)S(1)} %gains.1), channel_id=1, source_target_pairs={{0,8},{4,12},{8,0},{12,4},{16,24},{20,28},{24,16},{28,20},{1,9},{5... | collective-permute-start | bytes 344072 | tf_op jit(solution)/shard_map/ppermute | solution.py:421
  39.5 1.8 %collective-permute-start.9 = (f32[7,16,256]{2,1,0:T(8,128)S(1)}, f32[7,16,256]{2,1,0:T(8,128)S(1)}, u32[]{:S(2)}, u32[]{:S(2)}) collective-permute-start(f32[7,16,256]{2,1,0:T(8,128)S(1)} %gains.1), channel_id=1, source_target_pairs={{0,4},{4,0},{8,12},{12,8},{16,20},{20,16},{24,28},{28,24},{1,5},{5... | collective-permute-start | bytes 344072 | tf_op jit(solution)/shard_map/ppermute | solution.py:421
  41.3 2.5 %collective-permute-start.10 = (f32[7,16,256]{2,1,0:T(8,128)S(1)}, f32[7,16,256]{2,1,0:T(8,128)S(1)}, u32[]{:S(2)}, u32[]{:S(2)}) collective-permute-start(f32[7,16,256]{2,1,0:T(8,128)S(1)} %gains.1), channel_id=1, source_target_pairs={{0,24},{4,28},{8,16},{12,20},{16,8},{20,12},{24,0},{28,4},{1,25},{... | collective-permute-start | bytes 344072 | tf_op jit(solution)/shard_map/ppermute | solution.py:421
  43.8 0.1 broadcast_in_dim.3
  43.9 0.0 collective-permute-done.8
  43.9 4.7 %collective-permute-start.11 = (f32[7,16,256]{2,1,0:T(8,128)S(1)}, f32[7,16,256]{2,1,0:T(8,128)S(1)}, u32[]{:S(2)}, u32[]{:S(2)}) collective-permute-start(f32[7,16,256]{2,1,0:T(8,128)S(1)} %collective-permute-done.8), channel_id=1, source_target_pairs={{0,4},{4,0},{8,12},{12,8},{16,20},{20,16},{24,28},{28,24},{1,5},{5... | collective-permute-start | bytes 344072 | tf_op jit(solution)/shard_map/ppermute | solution.py:421
  48.6 0.0 collective-permute-done.7
  48.6 0.6 %collective-permute-start.12 = (f32[7,16,256]{2,1,0:T(8,128)S(1)}, f32[7,16,256]{2,1,0:T(8,128)S(1)}, u32[]{:S(2)}, u32[]{:S(2)}) collective-permute-start(f32[7,16,256]{2,1,0:T(8,128)S(1)} %collective-permute-done.7), channel_id=1, source_target_pairs={{0,4},{4,0},{8,12},{12,8},{16,20},{20,16},{24,28},{28,24},{1,5},{5... | collective-permute-start | bytes 344072 | tf_op jit(solution)/shard_map/ppermute | solution.py:421
  49.2 0.0 collective-permute-done.10
  49.2 1.5 %collective-permute-start.13 = (f32[7,16,256]{2,1,0:T(8,128)S(1)}, f32[7,16,256]{2,1,0:T(8,128)S(1)}, u32[]{:S(2)}, u32[]{:S(2)}) collective-permute-start(f32[7,16,256]{2,1,0:T(8,128)S(1)} %collective-permute-done.10), channel_id=1, source_target_pairs={{0,4},{4,0},{8,12},{12,8},{16,20},{20,16},{24,28},{28,24},{1,5},{5... | collective-permute-start | bytes 344072 | tf_op jit(solution)/shard_map/ppermute | solution.py:421
  50.7 0.0 collective-permute-done.9
  50.7 0.6 %collective-permute-done.11 = f32[7,16,256]{2,1,0:T(8,128)S(1)} collective-permute-done((f32[7,16,256]{2,1,0:T(8,128)S(1)}, f32[7,16,256]{2,1,0:T(8,128)S(1)}, u32[]{:S(2)}, u32[]{:S(2)}) %collective-permute-start.11) | collective-permute-done | bytes 114720 | tf_op jit(solution)/shard_map/ppermute | solution.py:421
  51.4 2.0 %collective-permute-done.12 = f32[7,16,256]{2,1,0:T(8,128)S(1)} collective-permute-done((f32[7,16,256]{2,1,0:T(8,128)S(1)}, f32[7,16,256]{2,1,0:T(8,128)S(1)}, u32[]{:S(2)}, u32[]{:S(2)}) %collective-permute-start.12) | collective-permute-done | bytes 114720 | tf_op jit(solution)/shard_map/ppermute | solution.py:421
  53.4 0.0 copy-start.2
  53.4 1.2 %collective-permute-done.13 = f32[7,16,256]{2,1,0:T(8,128)S(1)} collective-permute-done((f32[7,16,256]{2,1,0:T(8,128)S(1)}, f32[7,16,256]{2,1,0:T(8,128)S(1)}, u32[]{:S(2)}, u32[]{:S(2)}) %collective-permute-start.13) | collective-permute-done | bytes 114720 | tf_op jit(solution)/shard_map/ppermute | solution.py:421
  54.6 0.0 copy-done.2
  54.6 0.7 %constant_dynamic-update-slice_fusion = f32[7,128,256]{2,1,0:T(8,128)} fusion(f32[7,128,256]{2,1,0:T(8,128)} %copy-done.2, f32[7,16,256]{2,1,0:T(8,128)S(1)} %collective-permute-done.13, s32[]{:T(128)S(6)} %select_n.31), kind=kLoop, calls=%fused_computation.3 | loop fusion | bytes 229380 | tf_op jit(solution)/shard_map/dynamic_update_slice | solution.py:457
  (10 shorter events, 0.1 us)
Async XLA Ops:
  2.7 7.3 %copy-start.3 = (f32[24,128]{1,0:T(8,128)S(1)}, f32[24,128]{1,0:T(8,128)}, u32[]{:S(2)}) copy-start(f32[24,128]{1,0:T(8,128)} %get-tuple-element.11) | copy-start | bytes 36868
  2.7 24.5 %all-to-all-start = ((f32[8,18,8,128]{3,2,1,0:T(8,128)}), f32[8,18,8,128]{3,2,1,0:T(8,128)S(1)}, u32[]{:S(2)}, u32[]{:S(2)}) async-start(f32[8,18,8,128]{3,2,1,0:T(8,128)} %get-tuple-element.10), calls=%async_computation | async-start | bytes 1179648 | tf_op jit(solution)/shard_map/all_to_all | solution.py:446
  10.0 1.2 %collective-permute-start = (f32[24,128]{1,0:T(8,128)S(1)}, f32[24,128]{1,0:T(8,128)S(1)}, u32[]{:S(2)}, u32[]{:S(2)}) collective-permute-start(f32[24,128]{1,0:T(8,128)S(1)} %copy-done.3), channel_id=1, source_target_pairs={{0,1},{1,0},{2,3},{3,2},{4,5},{5,4},{6,7},{7,6},{8,9},{9,8},{10,11... | collective-permute-start | bytes 36872 | tf_op jit(solution)/shard_map/ppermute | solution.py:421
  11.2 5.5 %collective-permute-start.1 = (f32[24,128]{1,0:T(8,128)S(1)}, f32[24,128]{1,0:T(8,128)S(1)}, u32[]{:S(2)}, u32[]{:S(2)}) collective-permute-start(f32[24,128]{1,0:T(8,128)S(1)} %add.33), channel_id=1, source_target_pairs={{0,4},{4,0},{8,12},{12,8},{16,20},{20,16},{24,28},{28,24},{1,5},{5... | collective-permute-start | bytes 36872 | tf_op jit(solution)/shard_map/ppermute | solution.py:421
  13.2 3.7 %collective-permute-start.2 = (f32[24,128]{1,0:T(8,128)S(1)}, f32[24,128]{1,0:T(8,128)S(1)}, u32[]{:S(2)}, u32[]{:S(2)}) collective-permute-start(f32[24,128]{1,0:T(8,128)S(1)} %add.33), channel_id=1, source_target_pairs={{0,2},{1,3},{2,0},{3,1},{4,6},{5,7},{6,4},{7,5},{8,10},{9,11},{10,... | collective-permute-start | bytes 36872 | tf_op jit(solution)/shard_map/ppermute | solution.py:421
  14.7 4.6 %collective-permute-start.3 = (f32[24,128]{1,0:T(8,128)S(1)}, f32[24,128]{1,0:T(8,128)S(1)}, u32[]{:S(2)}, u32[]{:S(2)}) collective-permute-start(f32[24,128]{1,0:T(8,128)S(1)} %add.33), channel_id=1, source_target_pairs={{0,6},{1,7},{2,4},{3,5},{4,2},{5,3},{6,0},{7,1},{8,14},{9,15},{10,... | collective-permute-start | bytes 36872 | tf_op jit(solution)/shard_map/ppermute | solution.py:421
  19.3 7.9 %copy-start = (s32[8]{0:T(128)S(1)}, s32[8]{0:T(128)}, u32[]{:S(2)}) copy-start(s32[8]{0:T(128)} %slab_rows.3) | copy-start | bytes 100
  19.3 12.4 %copy-start.1 = (s32[3]{0:T(128)S(1)}, s32[3]{0:T(128)}, u32[]{:S(2)}) copy-start(s32[3]{0:T(128)} %split_bin.1) | copy-start | bytes 40
  19.3 12.4 %collective-permute-start.4 = (f32[2,24,128]{2,1,0:T(8,128)S(1)}, f32[2,24,128]{2,1,0:T(8,128)S(1)}, u32[]{:S(2)}, u32[]{:S(2)}) collective-permute-start(f32[2,24,128]{2,1,0:T(8,128)S(1)} %pad_maximum_fusion.refs_0_), channel_id=1, source_target_pairs={{0,8},{4,12},{8,0},{12,4},{16,24},{20,28},{24,16},{28,20},{1,9},{5... | collective-permute-start | bytes 73736 | tf_op jit(solution)/shard_map/ppermute | solution.py:421
  20.8 10.9 %collective-permute-start.5 = (f32[2,24,128]{2,1,0:T(8,128)S(1)}, f32[2,24,128]{2,1,0:T(8,128)S(1)}, u32[]{:S(2)}, u32[]{:S(2)}) collective-permute-start(f32[2,24,128]{2,1,0:T(8,128)S(1)} %pad_maximum_fusion.refs_0_), channel_id=1, source_target_pairs={{0,16},{4,20},{8,24},{12,28},{16,0},{20,4},{24,8},{28,12},{1,17},{... | collective-permute-start | bytes 73736 | tf_op jit(solution)/shard_map/ppermute | solution.py:421
  23.3 8.4 %collective-permute-start.6 = (f32[2,24,128]{2,1,0:T(8,128)S(1)}, f32[2,24,128]{2,1,0:T(8,128)S(1)}, u32[]{:S(2)}, u32[]{:S(2)}) collective-permute-start(f32[2,24,128]{2,1,0:T(8,128)S(1)} %pad_maximum_fusion.refs_0_), channel_id=1, source_target_pairs={{0,24},{4,28},{8,16},{12,20},{16,8},{20,12},{24,0},{28,4},{1,25},{... | collective-permute-start | bytes 73736 | tf_op jit(solution)/shard_map/ppermute | solution.py:421
  37.9 10.7 %collective-permute-start.7 = (f32[7,16,256]{2,1,0:T(8,128)S(1)}, f32[7,16,256]{2,1,0:T(8,128)S(1)}, u32[]{:S(2)}, u32[]{:S(2)}) collective-permute-start(f32[7,16,256]{2,1,0:T(8,128)S(1)} %gains.1), channel_id=1, source_target_pairs={{0,16},{4,20},{8,24},{12,28},{16,0},{20,4},{24,8},{28,12},{1,17},{... | collective-permute-start | bytes 344072 | tf_op jit(solution)/shard_map/ppermute | solution.py:421
  38.0 5.9 %collective-permute-start.8 = (f32[7,16,256]{2,1,0:T(8,128)S(1)}, f32[7,16,256]{2,1,0:T(8,128)S(1)}, u32[]{:S(2)}, u32[]{:S(2)}) collective-permute-start(f32[7,16,256]{2,1,0:T(8,128)S(1)} %gains.1), channel_id=1, source_target_pairs={{0,8},{4,12},{8,0},{12,4},{16,24},{20,28},{24,16},{28,20},{1,9},{5... | collective-permute-start | bytes 344072 | tf_op jit(solution)/shard_map/ppermute | solution.py:421
  39.5 11.2 %collective-permute-start.9 = (f32[7,16,256]{2,1,0:T(8,128)S(1)}, f32[7,16,256]{2,1,0:T(8,128)S(1)}, u32[]{:S(2)}, u32[]{:S(2)}) collective-permute-start(f32[7,16,256]{2,1,0:T(8,128)S(1)} %gains.1), channel_id=1, source_target_pairs={{0,4},{4,0},{8,12},{12,8},{16,20},{20,16},{24,28},{28,24},{1,5},{5... | collective-permute-start | bytes 344072 | tf_op jit(solution)/shard_map/ppermute | solution.py:421
  41.3 7.9 %collective-permute-start.10 = (f32[7,16,256]{2,1,0:T(8,128)S(1)}, f32[7,16,256]{2,1,0:T(8,128)S(1)}, u32[]{:S(2)}, u32[]{:S(2)}) collective-permute-start(f32[7,16,256]{2,1,0:T(8,128)S(1)} %gains.1), channel_id=1, source_target_pairs={{0,24},{4,28},{8,16},{12,20},{16,8},{20,12},{24,0},{28,4},{1,25},{... | collective-permute-start | bytes 344072 | tf_op jit(solution)/shard_map/ppermute | solution.py:421
  43.9 7.5 %collective-permute-start.11 = (f32[7,16,256]{2,1,0:T(8,128)S(1)}, f32[7,16,256]{2,1,0:T(8,128)S(1)}, u32[]{:S(2)}, u32[]{:S(2)}) collective-permute-start(f32[7,16,256]{2,1,0:T(8,128)S(1)} %collective-permute-done.8), channel_id=1, source_target_pairs={{0,4},{4,0},{8,12},{12,8},{16,20},{20,16},{24,28},{28,24},{1,5},{5... | collective-permute-start | bytes 344072 | tf_op jit(solution)/shard_map/ppermute | solution.py:421
  48.6 4.8 %collective-permute-start.12 = (f32[7,16,256]{2,1,0:T(8,128)S(1)}, f32[7,16,256]{2,1,0:T(8,128)S(1)}, u32[]{:S(2)}, u32[]{:S(2)}) collective-permute-start(f32[7,16,256]{2,1,0:T(8,128)S(1)} %collective-permute-done.7), channel_id=1, source_target_pairs={{0,4},{4,0},{8,12},{12,8},{16,20},{20,16},{24,28},{28,24},{1,5},{5... | collective-permute-start | bytes 344072 | tf_op jit(solution)/shard_map/ppermute | solution.py:421
  49.2 5.5 %collective-permute-start.13 = (f32[7,16,256]{2,1,0:T(8,128)S(1)}, f32[7,16,256]{2,1,0:T(8,128)S(1)}, u32[]{:S(2)}, u32[]{:S(2)}) collective-permute-start(f32[7,16,256]{2,1,0:T(8,128)S(1)} %collective-permute-done.10), channel_id=1, source_target_pairs={{0,4},{4,0},{8,12},{12,8},{16,20},{20,16},{24,28},{28,24},{1,5},{5... | collective-permute-start | bytes 344072 | tf_op jit(solution)/shard_map/ppermute | solution.py:421
  53.4 1.2 %copy-start.2 = (f32[7,128,256]{2,1,0:T(8,128)}, f32[7,128,256]{2,1,0:T(8,128)S(1)}, u32[]{:S(2)}) copy-start(f32[7,128,256]{2,1,0:T(8,128)S(1)} %constant_dynamic-update-slice_fusion.1) | copy-start | bytes 2752516

commit v5 on v4

--- a/solution.py
+++ b/solution.py
@@ -9,6 +9,8 @@
 BINS = 256
 LO = 128
 SIDE = 32
+UPPER = 6
+INNER = 48
 GROUP = 16
 f32 = jnp.float32
 bf16 = jnp.bfloat16
@@ -108,7 +110,7 @@
         used = list_blocks(slab_rows, list_ref, n_dp, tiles)
         row = iota((tiles, LO), 0) * LO + iota((tiles, LO), 1)
         for s in range(n_dp):
-            h = jnp.where(row < slab_rows[s], x_ref[s, groups * tiles + 1], 0.0)
+            h = jnp.where(row < slab_rows[s], x_ref[s, groups * tiles], 0.0)
             for i in range(tiles):
                 h_ref[s * tiles + i] = jnp.broadcast_to(h[i : i + 1], (8, LO))
         h_ref[blocks] = jnp.zeros((8, LO), f32)
@@ -225,8 +227,8 @@
             s = me ^ j
             row = iota((tiles, LO), 0) * LO + iota((tiles, LO), 1)
             live = row < slab_rows[s]
-            t_ref[j, 3] = jnp.where(live, x_ref[s, groups * tiles], 0.0)
-            h = jnp.where(live, x_ref[s, groups * tiles + 1], 0.0)
+            t_ref[j, 3] = jnp.where(live, pairs[j // 2][j % 2, 3 * tiles :], 0.0)
+            h = jnp.where(live, x_ref[s, groups * tiles], 0.0)
             t_ref[j, 4] = h
             lefts, rights = [], []
             hs = [spread(h, i) for i in range(tiles)]
@@ -268,14 +270,14 @@
 def make_gains(n_dp, feats_all, feats, tiles):
     quads = feats_all // 4
     width = GROUP * LO
-    inner = 64
+    lanes = 4 * UPPER * 8
 
     def kernel(slab_rows, bin_ref, ch_ref, o_ref, list_ref, acc_ref, cum_ref):
         used = list_blocks(slab_rows, list_ref, n_dp, tiles)
         acc_ref[...] = jnp.zeros_like(acc_ref)
-        kk = [to_bf16(iota((16, width), 0) // 8 + 2 * j) for j in range(2)]
+        kk = [to_bf16(iota((16, width), 0) // 8 + 2 * j) for j in range(UPPER // 2)]
         one, zero = jnp.ones((16, width), bf16), jnp.zeros((16, width), bf16)
-        lane = iota((inner, LO), 1) // SIDE
+        lane = iota((INNER, lanes), 1) // (UPPER * 8)
 
         def add(q, _):
             bs, chs = [], []
@@ -285,46 +287,54 @@
                 chs.append(ch_ref[at])
             ch = jnp.concatenate(chs, 1)
             ch = jnp.concatenate([ch, ch], 0).astype(bf16)
-            upper, lower = split_by(jnp.concatenate(bs, 1), inner)
+            bins = jnp.concatenate(bs, 1)
+            upper = jnp.floor((bins + 0.5) * (1.0 / INNER))
+            lower = bins - upper * INNER
             for quad in range(quads):
                 left, right = [], []
                 for f in range(quad * 4, quad * 4 + 4):
-                    left += hot(spread(lower, f), inner, one, zero)
+                    left += hot(spread(lower, f), INNER, one, zero)
                     u = spread(upper, f)
                     right += [jnp.where(u == k, ch, zero) for k in kk]
                 out = dot_nt(jnp.concatenate(left, 0), jnp.concatenate(right, 0))
-                mine = out[:inner]
+                mine = out[:INNER]
                 for i in range(1, 4):
-                    mine = jnp.where(lane == i, out[i * inner : (i + 1) * inner], mine)
-                acc_ref[quad] += mine
+                    mine = jnp.where(lane == i, out[i * INNER : (i + 1) * INNER], mine)
+                acc_ref[quad, :INNER, :lanes] += mine
             return 0
 
         lax.fori_loop(0, (used + GROUP - 1) // GROUP, add, 0)
-        r, c = iota((inner, LO), 0), iota((inner, LO), 1)
-        upto = to_bf16((r <= c) | (c >= inner))
-        pad = jnp.zeros((LO - inner, LO), f32)
+        r, c = iota((LO, 2 * LO), 0), iota((LO, 2 * LO), 1)
+        upto = to_bf16(r <= c)
+        at = iota((8, LO), 1)
         for quad in range(quads):
-            acc = jnp.transpose(jnp.concatenate([acc_ref[quad], pad], 0))[:, :inner]
+            acc = jnp.concatenate([jnp.transpose(acc_ref[quad, :, :LO]), jnp.transpose(acc_ref[quad, :, LO:])], 0)[:lanes]
             p0 = acc.astype(bf16)
             r1 = acc - p0.astype(f32)
             p1 = r1.astype(bf16)
             p2 = (r1 - p1.astype(f32)).astype(bf16)
             run = (dot_nn(p0, upto) + dot_nn(p1, upto)) + dot_nn(p2, upto)
-            whole = pltpu.roll(run, inner, 1)
-            first = iota((8, LO), 1) < inner
             for i in range(4):
                 f = quad * 4 + i
                 if f >= feats:
                     break
-                base = jnp.zeros((8, LO), f32)
-                for k in range(0, 4, 2):
-                    a = (i * 4 + k) * 8
-                    ta = jnp.where(first, whole[a : a + 8], run[a : a + 8])
-                    tb = jnp.where(first, whole[a + 8 : a + 16], run[a + 8 : a + 16])
-                    gl = base + jnp.where(first, run[a : a + 8], ta + whole[a + 8 : a + 16])
-                    base = base + (ta + tb)
+                for t in range(BINS // LO):
+                    gl = jnp.zeros((8, LO), f32)
+                    for k in range(UPPER):
+                        row = (i * UPPER + k) * 8
+                        part, total = run[row : row + 8, :LO], run[row : row + 8, LO:]
+                        s = INNER * k - LO * t
+                        if s >= LO:
+                            continue
+                        if s <= -INNER:
+                            part = total
+                        elif s < 0:
+                            part = jnp.where(at < LO + s, pltpu.roll(part, LO + s, 1), total)
+                        elif s > 0:
+                            part = jnp.where(at >= s, pltpu.roll(part, s, 1), 0.0)
+                        gl = gl + part
                     for c in range(8):
-                        cum_ref[c, f : f + 1, k // 2 * LO : k // 2 * LO + LO] = gl[c : c + 1]
+                        cum_ref[c, f : f + 1, t * LO : t * LO + LO] = gl[c : c + 1]
 
         def score(g, h):
             return g * g / (h + 1.0)
@@ -363,7 +373,7 @@
             list_shape(n_dp, tiles),
             pltpu.VMEM((blocks + 1, 8, LO), f32),
             pltpu.VMEM((n_dp, 5, tiles, LO), f32),
-            pltpu.VMEM((feats_all // 4, 64, LO), f32),
+            pltpu.VMEM((feats_all // 4, LO, 2 * LO), f32),
             pltpu.VMEM((8, feats, BINS), f32),
         ],
         compiler_params=params(),
@@ -373,17 +383,22 @@
 
 
 def make_pick(groups, tiles, feat_dev, feats):
-    def kernel(split_feature, x_ref, g_ref, h_ref, o_ref, x_out, sems):
+    def kernel(split_ref, x_ref, h_ref, o_ref, x_out, split_feature, h_in, sems):
         me = lax.axis_index("feat")
         n_dp = x_ref.shape[0]
         size = groups * tiles
+        split_copy = pltpu.make_async_copy(split_ref, split_feature, sems.at[n_dp + 1])
+        split_copy.start()
+        h_copy = pltpu.make_async_copy(h_ref, h_in, sems.at[n_dp])
+        h_copy.start()
         copies = [pltpu.make_async_copy(x_ref.at[s], x_out.at[s, pl.ds(0, size)], sems.at[s]) for s in range(n_dp)]
         for copy in copies:
             copy.start()
-        g, h = g_ref[...].astype(f32), h_ref[...].astype(f32)
+        h_copy.wait()
+        h = h_in[...].astype(f32)
         for s in range(n_dp):
-            x_out[s, size] = g
-            x_out[s, size + 1] = h
+            x_out[s, size] = h
+        split_copy.wait()
         for copy in copies:
             copy.wait()
         at8 = iota((8, LO), 0)
@@ -400,21 +415,21 @@
     return kernel
 
 
-def pick_rows(x, grad, hess, split_feature, groups, tiles, feat_dev):
+def pick_rows(x, hess, split_feature, groups, tiles, feat_dev):
     n_dp = x.shape[0]
-    smem = pl.BlockSpec(memory_space=pltpu.SMEM)
+    anywhere = pl.BlockSpec(memory_space=pl.ANY)
     vmem = pl.BlockSpec(memory_space=pltpu.VMEM)
     return pl.pallas_call(
         make_pick(groups, tiles, feat_dev, feat_dev // n_dp),
         out_shape=[
             jax.ShapeDtypeStruct((3 * tiles, LO), f32),
-            jax.ShapeDtypeStruct((n_dp, groups * tiles + 2, 8, LO), f32),
+            jax.ShapeDtypeStruct((n_dp, groups * tiles + 1, 8, LO), f32),
         ],
-        in_specs=[smem, pl.BlockSpec(memory_space=pl.ANY), vmem, vmem],
+        in_specs=[anywhere, anywhere, anywhere],
         out_specs=[vmem, vmem],
-        scratch_shapes=[pltpu.SemaphoreType.DMA((n_dp,))],
+        scratch_shapes=[pltpu.SMEM((3,), i32), pltpu.VMEM((tiles, LO), bf16), pltpu.SemaphoreType.DMA((n_dp + 2,))],
         name="pick",
-    )(split_feature, x, grad.reshape(tiles, LO), hess.reshape(tiles, LO))
+    )(split_feature, x, hess.reshape(tiles, LO))
 
 
 def swap(value, axis, size, step):
@@ -431,17 +446,19 @@
         x = fine_values.reshape(n_dp, feats, tiles, LO)
         x = jnp.pad(x, ((0, 0), (0, groups * 8 - feats), (0, 0), (0, 0)))
         x = x.reshape(n_dp, groups, 8, tiles, LO).swapaxes(2, 3).reshape(n_dp, groups * tiles, 8, LO)
-        share, x = pick_rows(x, grad, hess, split_feature, groups, tiles, feat_dev)
+        share, x = pick_rows(x, hess, split_feature, groups, tiles, feat_dev)
         share = share + swap(share, "feat", n_feat, 1)
-        got = [swap(share, "dp", n_dp, 1)]
+        g = grad.astype(f32).reshape(tiles, LO)
+        share, g, block = lax.optimization_barrier((share, g, jnp.concatenate([share, g])))
+        got = [swap(block, "dp", n_dp, 1)]
         for i in range(2, n_feat, 2):
             got.append(swap(share, "feat", n_feat, i))
             got.append(swap(share, both, n_dp * n_feat, n_feat + i))
         got = lax.optimization_barrier(got)
-        mine, other = share, got[0]
+        mine, other, other_g = share, got[0][: 3 * tiles], got[0][3 * tiles :]
         for i in range(1, len(got), 2):
             mine, other = mine + got[i], other + got[i + 1]
-        pair = jnp.stack([mine, other])
+        pair = jnp.stack([jnp.concatenate([mine, g]), jnp.concatenate([other, other_g])])
         pairs = [pair] + [swap(pair, "dp", n_dp, d) for d in range(2, n_dp, 2)]
         x = lax.all_to_all(x, "dp", 0, 0)
         bins = find_bins(x, slab_rows, groups, tiles)

time: 55.6 us -> 54.3 us (0.977)
  Pallas kernels: 13.3 us -> 12 us
    pallas_call x1, Pallas kernels: 2.65 us -> 1.97 us  [pick_rows(): pl.pallas_call(make_pick(groups, tiles, feat_dev, feat_dev // n_dp), out_...]
    pallas_call x1, Pallas kernels: 6.14 us -> 5.56 us  [route_and_sum(): pl.pallas_call(kernel, out_shape=jax.ShapeDtypeStruct((7, feats, BINS), f...]
  transfers between devices with their start and end apart: 15 -> 15, of which waited for: 8 -> 7; matrix products, arithmetic and copies ran while one was open for 0% -> 0% of each run, Pallas kernels for 8% -> 8%
where the time goes in v5:
time: 54.3 us; the launch traced here: 54 us
  starting transfers between devices  28.2 us (52%)
  waiting for transfers between devices  12.7 us (23%)
  Pallas kernels  12 us (22%)
  local copies, waits for them, and re-layouts  0.85 us (2%)
    ppermute x14, starting transfers between devices, swap(): return lax.ppermute(value, axis, [(s, s ^ step) for s in range(size)])  20.9 us
    ppermute x14, waiting for transfers between devices, swap(): return lax.ppermute(value, axis, [(s, s ^ step) for s in range(size)])  9.57 us
    all_to_all x1, starting transfers between devices, shards(): x = lax.all_to_all(x, 'dp', 0, 0)  7.29 us
    pallas_call x1, Pallas kernels, route_and_sum(): pl.pallas_call(kernel, out_shape=jax.ShapeDtypeStruct((7, feats, BINS), f...  5.56 us
    pallas_call x1, Pallas kernels, find_bins(): pl.pallas_call(make_bins(n_dp, groups, tiles), out_shape=jax.ShapeDtypeSt...  4.51 us
    all_to_all x1, waiting for transfers between devices, shards(): x = lax.all_to_all(x, 'dp', 0, 0)  3.12 us
    pallas_call x1, Pallas kernels, pick_rows(): pl.pallas_call(make_pick(groups, tiles, feat_dev, feat_dev // n_dp), out_...  1.97 us
  transfers between devices with their start and end apart: 15, of which 7 were waited for; matrix products, arithmetic and copies ran while one was open for 0% of the time, Pallas kernels for 8%

profile of v5, /device:TPU:0, one launch (start us, length us, event | category | flops | bytes accessed | tf_op | source)
XLA Modules:
  0.0 54.0 jit_solution(3858701478571298897)
XLA Ops:
  0.0 2.0 %pick.1 = (f32[24,128]{1,0:T(8,128)}, f32[8,17,8,128]{3,2,1,0:T(8,128)}) custom-call(s32[3]{0:T(128)} %split_ref.1, f32[8,16,8,128]{3,2,1,0:T(8,128)} %bitcast.13, bf16[8,128]{1,0:T(8,128)(2,1)} %bitcast.14), custom_call_target="tpu_custom_call" | custom-call | tf_op jit(solution)/shard_map/pick/pallas_call | solution.py:422
  2.0 0.0 copy-start.3
  2.0 0.0 copy-start.4
  2.0 7.3 %all-to-all-start = ((f32[8,17,8,128]{3,2,1,0:T(8,128)}), f32[8,17,8,128]{3,2,1,0:T(8,128)S(1)}, u32[]{:S(2)}, u32[]{:S(2)}) async-start(f32[8,17,8,128]{3,2,1,0:T(8,128)} %get-tuple-element.13), calls=%async_computation | async-start | bytes 1114112 | tf_op jit(solution)/shard_map/all_to_all | solution.py:463
  9.3 0.0 copy-done.3
  9.3 0.1 collective-permute-start
  9.4 0.0 copy-done.4
  9.4 1.1 %collective-permute-done = f32[24,128]{1,0:T(8,128)S(1)} collective-permute-done((f32[24,128]{1,0:T(8,128)S(1)}, f32[24,128]{1,0:T(8,128)S(1)}, u32[]{:S(2)}, u32[]{:S(2)}) %collective-permute-start) | collective-permute-done | bytes 12320 | tf_op jit(solution)/shard_map/ppermute | solution.py:436
  10.6 2.0 %collective-permute-start.1 = (f32[32,128]{1,0:T(8,128)S(1)}, f32[32,128]{1,0:T(8,128)S(1)}, u32[]{:S(2)}, u32[]{:S(2)}) collective-permute-start(f32[32,128]{1,0:T(8,128)S(1)} %pad_maximum_fusion.1), channel_id=1, source_target_pairs={{0,4},{4,0},{8,12},{12,8},{16,20},{20,16},{24,28},{28,24},{1,5},{5... | collective-permute-start | bytes 49160 | tf_op jit(solution)/shard_map/ppermute | solution.py:436
  12.5 1.5 %collective-permute-start.2 = (f32[24,128]{1,0:T(8,128)S(1)}, f32[24,128]{1,0:T(8,128)S(1)}, u32[]{:S(2)}, u32[]{:S(2)}) collective-permute-start(f32[24,128]{1,0:T(8,128)S(1)} %add.33), channel_id=1, source_target_pairs={{0,2},{1,3},{2,0},{3,1},{4,6},{5,7},{6,4},{7,5},{8,10},{9,11},{10,... | collective-permute-start | bytes 36872 | tf_op jit(solution)/shard_map/ppermute | solution.py:436
  14.0 0.0 collective-permute-start.3
  14.0 2.2 %collective-permute-done.2 = f32[24,128]{1,0:T(8,128)S(1)} collective-permute-done((f32[24,128]{1,0:T(8,128)S(1)}, f32[24,128]{1,0:T(8,128)S(1)}, u32[]{:S(2)}, u32[]{:S(2)}) %collective-permute-start.2) | collective-permute-done | bytes 12320 | tf_op jit(solution)/shard_map/ppermute | solution.py:436
  16.2 2.3 %collective-permute-done.3 = f32[24,128]{1,0:T(8,128)S(1)} collective-permute-done((f32[24,128]{1,0:T(8,128)S(1)}, f32[24,128]{1,0:T(8,128)S(1)}, u32[]{:S(2)}, u32[]{:S(2)}) %collective-permute-start.3) | collective-permute-done | bytes 12320 | tf_op jit(solution)/shard_map/ppermute | solution.py:436
  18.6 0.0 collective-permute-done.1
  18.6 0.0 copy-start
  18.7 0.0 copy-start.1
  18.7 1.5 %collective-permute-start.4 = (f32[2,32,128]{2,1,0:T(8,128)S(1)}, f32[2,32,128]{2,1,0:T(8,128)S(1)}, u32[]{:S(2)}, u32[]{:S(2)}) collective-permute-start(f32[2,32,128]{2,1,0:T(8,128)S(1)} %pad_maximum_fusion.refs_0_), channel_id=1, source_target_pairs={{0,8},{4,12},{8,0},{12,4},{16,24},{20,28},{24,16},{28,20},{1,9},{5... | collective-permute-start | bytes 98312 | tf_op jit(solution)/shard_map/ppermute | solution.py:436
  20.2 2.5 %collective-permute-start.5 = (f32[2,32,128]{2,1,0:T(8,128)S(1)}, f32[2,32,128]{2,1,0:T(8,128)S(1)}, u32[]{:S(2)}, u32[]{:S(2)}) collective-permute-start(f32[2,32,128]{2,1,0:T(8,128)S(1)} %pad_maximum_fusion.refs_0_), channel_id=1, source_target_pairs={{0,16},{4,20},{8,24},{12,28},{16,0},{20,4},{24,8},{28,12},{1,17},{... | collective-permute-start | bytes 98312 | tf_op jit(solution)/shard_map/ppermute | solution.py:436
  22.7 0.4 collective-permute-start.6
  23.1 3.1 %all-to-all-done.x_ref = f32[8,17,8,128]{3,2,1,0:T(8,128)S(1)} async-done(((f32[8,17,8,128]{3,2,1,0:T(8,128)}), f32[8,17,8,128]{3,2,1,0:T(8,128)S(1)}, u32[]{:S(2)}, u32[]{:S(2)}) %all-to-all-start) | async-done | bytes 557088 | tf_op jit(solution)/shard_map/all_to_all | solution.py:463
  26.2 0.0 copy-done
  26.2 4.5 %bins.1.bin_ref = f32[65,16,128]{2,1,0:T(8,128)S(1)} custom-call(s32[8]{0:T(128)S(1)} %copy-done, f32[8,17,8,128]{3,2,1,0:T(8,128)S(1)} %all-to-all-done.x_ref), custom_call_target="tpu_custom_call" | custom-call | flops 1073741824 | bytes 1048576 | tf_op jit(solution)/shard_map/bins/pallas_call | solution.py:199
  30.7 0.0 collective-permute-done.4.refs_1_
  30.8 0.0 collective-permute-done.5.refs_2_
  30.8 0.0 collective-permute-done.6.refs_3_
  30.8 0.0 copy-done.1
  30.8 5.6 %gains.1 = f32[7,16,256]{2,1,0:T(8,128)S(1)} custom-call(s32[8]{0:T(128)S(1)} %copy-done, s32[3]{0:T(128)S(1)} %copy-done.1, f32[8,17,8,128]{3,2,1,0:T(8,128)S(1)} %all-to-all-done.x_ref, f32[65,16,128]{2,1,0:T(8,128)S(1)} %bins.1.bin_ref, f32[2,32,128]{2,1,0:T(8,128)S(1)} %pad_maximum_fusion.refs_0_, f32[2,32,128]{2,1,0:T(8,128)S(1)} %collective-permute-done.4.refs_1_, ...), custom_call_target="tpu_custom_call" | custom-call | flops 2147483648 | bytes 1048576 | tf_op jit(solution)/shard_map/gains/pallas_call | solution.py:367
  36.4 0.1 collective-permute-start.7
  36.4 1.4 %collective-permute-start.8 = (f32[7,16,256]{2,1,0:T(8,128)S(1)}, f32[7,16,256]{2,1,0:T(8,128)S(1)}, u32[]{:S(2)}, u32[]{:S(2)}) collective-permute-start(f32[7,16,256]{2,1,0:T(8,128)S(1)} %gains.1), channel_id=1, source_target_pairs={{0,8},{4,12},{8,0},{12,4},{16,24},{20,28},{24,16},{28,20},{1,9},{5... | collective-permute-start | bytes 344072 | tf_op jit(solution)/shard_map/ppermute | solution.py:436
  37.9 1.1 %collective-permute-start.9 = (f32[7,16,256]{2,1,0:T(8,128)S(1)}, f32[7,16,256]{2,1,0:T(8,128)S(1)}, u32[]{:S(2)}, u32[]{:S(2)}) collective-permute-start(f32[7,16,256]{2,1,0:T(8,128)S(1)} %gains.1), channel_id=1, source_target_pairs={{0,4},{4,0},{8,12},{12,8},{16,20},{20,16},{24,28},{28,24},{1,5},{5... | collective-permute-start | bytes 344072 | tf_op jit(solution)/shard_map/ppermute | solution.py:436
  39.0 3.3 %collective-permute-start.10 = (f32[7,16,256]{2,1,0:T(8,128)S(1)}, f32[7,16,256]{2,1,0:T(8,128)S(1)}, u32[]{:S(2)}, u32[]{:S(2)}) collective-permute-start(f32[7,16,256]{2,1,0:T(8,128)S(1)} %gains.1), channel_id=1, source_target_pairs={{0,24},{4,28},{8,16},{12,20},{16,8},{20,12},{24,0},{28,4},{1,25},{... | collective-permute-start | bytes 344072 | tf_op jit(solution)/shard_map/ppermute | solution.py:436
  42.3 0.1 broadcast_in_dim.3
  42.4 0.0 collective-permute-done.8
  42.4 5.0 %collective-permute-start.11 = (f32[7,16,256]{2,1,0:T(8,128)S(1)}, f32[7,16,256]{2,1,0:T(8,128)S(1)}, u32[]{:S(2)}, u32[]{:S(2)}) collective-permute-start(f32[7,16,256]{2,1,0:T(8,128)S(1)} %collective-permute-done.8), channel_id=1, source_target_pairs={{0,4},{4,0},{8,12},{12,8},{16,20},{20,16},{24,28},{28,24},{1,5},{5... | collective-permute-start | bytes 344072 | tf_op jit(solution)/shard_map/ppermute | solution.py:436
  47.3 0.0 collective-permute-done.7
  47.3 0.0 collective-permute-start.12
  47.4 0.0 collective-permute-done.10
  47.4 2.0 %collective-permute-start.13 = (f32[7,16,256]{2,1,0:T(8,128)S(1)}, f32[7,16,256]{2,1,0:T(8,128)S(1)}, u32[]{:S(2)}, u32[]{:S(2)}) collective-permute-start(f32[7,16,256]{2,1,0:T(8,128)S(1)} %collective-permute-done.10), channel_id=1, source_target_pairs={{0,4},{4,0},{8,12},{12,8},{16,20},{20,16},{24,28},{28,24},{1,5},{5... | collective-permute-start | bytes 344072 | tf_op jit(solution)/shard_map/ppermute | solution.py:436
  49.4 0.0 collective-permute-done.9
  49.5 0.6 %collective-permute-done.11 = f32[7,16,256]{2,1,0:T(8,128)S(1)} collective-permute-done((f32[7,16,256]{2,1,0:T(8,128)S(1)}, f32[7,16,256]{2,1,0:T(8,128)S(1)}, u32[]{:S(2)}, u32[]{:S(2)}) %collective-permute-start.11) | collective-permute-done | bytes 114720 | tf_op jit(solution)/shard_map/ppermute | solution.py:436
  50.1 2.0 %collective-permute-done.12 = f32[7,16,256]{2,1,0:T(8,128)S(1)} collective-permute-done((f32[7,16,256]{2,1,0:T(8,128)S(1)}, f32[7,16,256]{2,1,0:T(8,128)S(1)}, u32[]{:S(2)}, u32[]{:S(2)}) %collective-permute-start.12) | collective-permute-done | bytes 114720 | tf_op jit(solution)/shard_map/ppermute | solution.py:436
  52.1 0.0 copy-start.2
  52.2 1.2 %collective-permute-done.13 = f32[7,16,256]{2,1,0:T(8,128)S(1)} collective-permute-done((f32[7,16,256]{2,1,0:T(8,128)S(1)}, f32[7,16,256]{2,1,0:T(8,128)S(1)}, u32[]{:S(2)}, u32[]{:S(2)}) %collective-permute-start.13) | collective-permute-done | bytes 114720 | tf_op jit(solution)/shard_map/ppermute | solution.py:436
  53.4 0.0 copy-done.2
  53.4 0.7 %constant_dynamic-update-slice_fusion = f32[7,128,256]{2,1,0:T(8,128)} fusion(f32[7,128,256]{2,1,0:T(8,128)} %copy-done.2, f32[7,16,256]{2,1,0:T(8,128)S(1)} %collective-permute-done.13, s32[]{:T(128)S(6)} %select_n.31), kind=kLoop, calls=%fused_computation.6 | loop fusion | bytes 229380 | tf_op jit(solution)/shard_map/dynamic_update_slice | solution.py:474
  (15 shorter events, 0.1 us)
Async XLA Ops:
  2.0 7.3 %copy-start.3 = (f32[24,128]{1,0:T(8,128)S(1)}, f32[24,128]{1,0:T(8,128)}, u32[]{:S(2)}) copy-start(f32[24,128]{1,0:T(8,128)} %get-tuple-element.14) | copy-start | bytes 36868
  2.0 7.4 %copy-start.4 = (bf16[1024]{0:T(1024)(128)(2,1)S(1)}, bf16[1024]{0:T(1024)(128)(2,1)}, u32[]{:S(2)}) copy-start(bf16[1024]{0:T(1024)(128)(2,1)} %param.7) | copy-start | bytes 6148
  2.0 24.2 %all-to-all-start = ((f32[8,17,8,128]{3,2,1,0:T(8,128)}), f32[8,17,8,128]{3,2,1,0:T(8,128)S(1)}, u32[]{:S(2)}, u32[]{:S(2)}) async-start(f32[8,17,8,128]{3,2,1,0:T(8,128)} %get-tuple-element.13), calls=%async_computation | async-start | bytes 1114112 | tf_op jit(solution)/shard_map/all_to_all | solution.py:463
  9.3 1.2 %collective-permute-start = (f32[24,128]{1,0:T(8,128)S(1)}, f32[24,128]{1,0:T(8,128)S(1)}, u32[]{:S(2)}, u32[]{:S(2)}) collective-permute-start(f32[24,128]{1,0:T(8,128)S(1)} %copy-done.3), channel_id=1, source_target_pairs={{0,1},{1,0},{2,3},{3,2},{4,5},{5,4},{6,7},{7,6},{8,9},{9,8},{10,11... | collective-permute-start | bytes 36872 | tf_op jit(solution)/shard_map/ppermute | solution.py:436
  10.6 8.0 %collective-permute-start.1 = (f32[32,128]{1,0:T(8,128)S(1)}, f32[32,128]{1,0:T(8,128)S(1)}, u32[]{:S(2)}, u32[]{:S(2)}) collective-permute-start(f32[32,128]{1,0:T(8,128)S(1)} %pad_maximum_fusion.1), channel_id=1, source_target_pairs={{0,4},{4,0},{8,12},{12,8},{16,20},{20,16},{24,28},{28,24},{1,5},{5... | collective-permute-start | bytes 49160 | tf_op jit(solution)/shard_map/ppermute | solution.py:436
  12.5 3.7 %collective-permute-start.2 = (f32[24,128]{1,0:T(8,128)S(1)}, f32[24,128]{1,0:T(8,128)S(1)}, u32[]{:S(2)}, u32[]{:S(2)}) collective-permute-start(f32[24,128]{1,0:T(8,128)S(1)} %add.33), channel_id=1, source_target_pairs={{0,2},{1,3},{2,0},{3,1},{4,6},{5,7},{6,4},{7,5},{8,10},{9,11},{10,... | collective-permute-start | bytes 36872 | tf_op jit(solution)/shard_map/ppermute | solution.py:436
  14.0 4.6 %collective-permute-start.3 = (f32[24,128]{1,0:T(8,128)S(1)}, f32[24,128]{1,0:T(8,128)S(1)}, u32[]{:S(2)}, u32[]{:S(2)}) collective-permute-start(f32[24,128]{1,0:T(8,128)S(1)} %add.33), channel_id=1, source_target_pairs={{0,6},{1,7},{2,4},{3,5},{4,2},{5,3},{6,0},{7,1},{8,14},{9,15},{10,... | collective-permute-start | bytes 36872 | tf_op jit(solution)/shard_map/ppermute | solution.py:436
  18.6 7.6 %copy-start = (s32[8]{0:T(128)S(1)}, s32[8]{0:T(128)}, u32[]{:S(2)}) copy-start(s32[8]{0:T(128)} %slab_rows.3) | copy-start | bytes 100
  18.7 12.1 %copy-start.1 = (s32[3]{0:T(128)S(1)}, s32[3]{0:T(128)}, u32[]{:S(2)}) copy-start(s32[3]{0:T(128)} %split_bin.1) | copy-start | bytes 40
  18.7 12.1 %collective-permute-start.4 = (f32[2,32,128]{2,1,0:T(8,128)S(1)}, f32[2,32,128]{2,1,0:T(8,128)S(1)}, u32[]{:S(2)}, u32[]{:S(2)}) collective-permute-start(f32[2,32,128]{2,1,0:T(8,128)S(1)} %pad_maximum_fusion.refs_0_), channel_id=1, source_target_pairs={{0,8},{4,12},{8,0},{12,4},{16,24},{20,28},{24,16},{28,20},{1,9},{5... | collective-permute-start | bytes 98312 | tf_op jit(solution)/shard_map/ppermute | solution.py:436
  20.2 10.6 %collective-permute-start.5 = (f32[2,32,128]{2,1,0:T(8,128)S(1)}, f32[2,32,128]{2,1,0:T(8,128)S(1)}, u32[]{:S(2)}, u32[]{:S(2)}) collective-permute-start(f32[2,32,128]{2,1,0:T(8,128)S(1)} %pad_maximum_fusion.refs_0_), channel_id=1, source_target_pairs={{0,16},{4,20},{8,24},{12,28},{16,0},{20,4},{24,8},{28,12},{1,17},{... | collective-permute-start | bytes 98312 | tf_op jit(solution)/shard_map/ppermute | solution.py:436
  22.7 8.1 %collective-permute-start.6 = (f32[2,32,128]{2,1,0:T(8,128)S(1)}, f32[2,32,128]{2,1,0:T(8,128)S(1)}, u32[]{:S(2)}, u32[]{:S(2)}) collective-permute-start(f32[2,32,128]{2,1,0:T(8,128)S(1)} %pad_maximum_fusion.refs_0_), channel_id=1, source_target_pairs={{0,24},{4,28},{8,16},{12,20},{16,8},{20,12},{24,0},{28,4},{1,25},{... | collective-permute-start | bytes 98312 | tf_op jit(solution)/shard_map/ppermute | solution.py:436
  36.4 11.0 %collective-permute-start.7 = (f32[7,16,256]{2,1,0:T(8,128)S(1)}, f32[7,16,256]{2,1,0:T(8,128)S(1)}, u32[]{:S(2)}, u32[]{:S(2)}) collective-permute-start(f32[7,16,256]{2,1,0:T(8,128)S(1)} %gains.1), channel_id=1, source_target_pairs={{0,16},{4,20},{8,24},{12,28},{16,0},{20,4},{24,8},{28,12},{1,17},{... | collective-permute-start | bytes 344072 | tf_op jit(solution)/shard_map/ppermute | solution.py:436
  36.4 5.9 %collective-permute-start.8 = (f32[7,16,256]{2,1,0:T(8,128)S(1)}, f32[7,16,256]{2,1,0:T(8,128)S(1)}, u32[]{:S(2)}, u32[]{:S(2)}) collective-permute-start(f32[7,16,256]{2,1,0:T(8,128)S(1)} %gains.1), channel_id=1, source_target_pairs={{0,8},{4,12},{8,0},{12,4},{16,24},{20,28},{24,16},{28,20},{1,9},{5... | collective-permute-start | bytes 344072 | tf_op jit(solution)/shard_map/ppermute | solution.py:436
  37.9 11.5 %collective-permute-start.9 = (f32[7,16,256]{2,1,0:T(8,128)S(1)}, f32[7,16,256]{2,1,0:T(8,128)S(1)}, u32[]{:S(2)}, u32[]{:S(2)}) collective-permute-start(f32[7,16,256]{2,1,0:T(8,128)S(1)} %gains.1), channel_id=1, source_target_pairs={{0,4},{4,0},{8,12},{12,8},{16,20},{20,16},{24,28},{28,24},{1,5},{5... | collective-permute-start | bytes 344072 | tf_op jit(solution)/shard_map/ppermute | solution.py:436
  39.0 8.4 %collective-permute-start.10 = (f32[7,16,256]{2,1,0:T(8,128)S(1)}, f32[7,16,256]{2,1,0:T(8,128)S(1)}, u32[]{:S(2)}, u32[]{:S(2)}) collective-permute-start(f32[7,16,256]{2,1,0:T(8,128)S(1)} %gains.1), channel_id=1, source_target_pairs={{0,24},{4,28},{8,16},{12,20},{16,8},{20,12},{24,0},{28,4},{1,25},{... | collective-permute-start | bytes 344072 | tf_op jit(solution)/shard_map/ppermute | solution.py:436
  42.4 7.7 %collective-permute-start.11 = (f32[7,16,256]{2,1,0:T(8,128)S(1)}, f32[7,16,256]{2,1,0:T(8,128)S(1)}, u32[]{:S(2)}, u32[]{:S(2)}) collective-permute-start(f32[7,16,256]{2,1,0:T(8,128)S(1)} %collective-permute-done.8), channel_id=1, source_target_pairs={{0,4},{4,0},{8,12},{12,8},{16,20},{20,16},{24,28},{28,24},{1,5},{5... | collective-permute-start | bytes 344072 | tf_op jit(solution)/shard_map/ppermute | solution.py:436
  47.3 4.8 %collective-permute-start.12 = (f32[7,16,256]{2,1,0:T(8,128)S(1)}, f32[7,16,256]{2,1,0:T(8,128)S(1)}, u32[]{:S(2)}, u32[]{:S(2)}) collective-permute-start(f32[7,16,256]{2,1,0:T(8,128)S(1)} %collective-permute-done.7), channel_id=1, source_target_pairs={{0,4},{4,0},{8,12},{12,8},{16,20},{20,16},{24,28},{28,24},{1,5},{5... | collective-permute-start | bytes 344072 | tf_op jit(solution)/shard_map/ppermute | solution.py:436
  47.4 6.0 %collective-permute-start.13 = (f32[7,16,256]{2,1,0:T(8,128)S(1)}, f32[7,16,256]{2,1,0:T(8,128)S(1)}, u32[]{:S(2)}, u32[]{:S(2)}) collective-permute-start(f32[7,16,256]{2,1,0:T(8,128)S(1)} %collective-permute-done.10), channel_id=1, source_target_pairs={{0,4},{4,0},{8,12},{12,8},{16,20},{20,16},{24,28},{28,24},{1,5},{5... | collective-permute-start | bytes 344072 | tf_op jit(solution)/shard_map/ppermute | solution.py:436
  52.1 1.2 %copy-start.2 = (f32[7,128,256]{2,1,0:T(8,128)}, f32[7,128,256]{2,1,0:T(8,128)S(1)}, u32[]{:S(2)}) copy-start(f32[7,128,256]{2,1,0:T(8,128)S(1)} %constant_dynamic-update-slice_fusion.1) | copy-start | bytes 2752516

commit v6 on v5

--- a/solution.py
+++ b/solution.py
@@ -106,11 +106,15 @@
     quads = feats // 4
     width = GROUP * LO
 
-    def kernel(slab_rows, x_ref, o_ref, list_ref, h_ref, cnt_ref, cut_ref, map_ref):
+    def kernel(slab_rows, _, x_ref, *refs):
+        hs, (o_ref, h_out, list_ref, h_ref, cnt_ref, cut_ref, map_ref) = refs[: n_dp // 2], refs[n_dp // 2 :]
+        me = lax.axis_index("dp")
         used = list_blocks(slab_rows, list_ref, n_dp, tiles)
         row = iota((tiles, LO), 0) * LO + iota((tiles, LO), 1)
-        for s in range(n_dp):
-            h = jnp.where(row < slab_rows[s], x_ref[s, groups * tiles], 0.0)
+        for j in range(n_dp):
+            s = me ^ j
+            h = jnp.where(row < slab_rows[s], hs[j // 2][j % 2], 0.0)
+            h_out[s] = h
             for i in range(tiles):
                 h_ref[s * tiles + i] = jnp.broadcast_to(h[i : i + 1], (8, LO))
         h_ref[blocks] = jnp.zeros((8, LO), f32)
@@ -191,16 +195,19 @@
     return kernel
 
 
-def find_bins(x, slab_rows, groups, tiles):
+def find_bins(x, hs, slab_rows, split_bin, groups, tiles):
     n_dp = x.shape[0]
     feats = groups * 8
     smem = pl.BlockSpec(memory_space=pltpu.SMEM)
     vmem = pl.BlockSpec(memory_space=pltpu.VMEM)
     return pl.pallas_call(
         make_bins(n_dp, groups, tiles),
-        out_shape=jax.ShapeDtypeStruct((n_dp * tiles + 1, feats, LO), f32),
-        in_specs=[smem, vmem],
-        out_specs=vmem,
+        out_shape=[
+            jax.ShapeDtypeStruct((n_dp * tiles + 1, feats, LO), f32),
+            jax.ShapeDtypeStruct((n_dp, tiles, LO), f32),
+        ],
+        in_specs=[smem, smem] + [vmem] * (1 + len(hs)),
+        out_specs=[vmem, vmem],
         scratch_shapes=[
             list_shape(n_dp, tiles),
             pltpu.VMEM((n_dp * tiles + 1, 8, LO), f32),
@@ -211,7 +218,7 @@
         compiler_params=params(),
         cost_estimate=cost(2 * 128 * 128 * n_dp * tiles * LO * feats // 4),
         name="bins",
-    )(slab_rows, x)
+    )(slab_rows, split_bin, x, *hs)
 
 
 def make_route(n_dp, groups, tiles):
@@ -228,7 +235,7 @@
             row = iota((tiles, LO), 0) * LO + iota((tiles, LO), 1)
             live = row < slab_rows[s]
             t_ref[j, 3] = jnp.where(live, pairs[j // 2][j % 2, 3 * tiles :], 0.0)
-            h = jnp.where(live, x_ref[s, groups * tiles], 0.0)
+            h = jnp.where(live, x_ref[s], 0.0)
             t_ref[j, 4] = h
             lefts, rights = [], []
             hs = [spread(h, i) for i in range(tiles)]
@@ -383,53 +390,55 @@
 
 
 def make_pick(groups, tiles, feat_dev, feats):
-    def kernel(split_ref, x_ref, h_ref, o_ref, x_out, split_feature, h_in, sems):
+    def kernel(split_ref, x_ref, g_ref, h_ref, o_ref, g_out, h_out, split_feature, rows_ref, gh_ref, sems):
         me = lax.axis_index("feat")
-        n_dp = x_ref.shape[0]
-        size = groups * tiles
-        split_copy = pltpu.make_async_copy(split_ref, split_feature, sems.at[n_dp + 1])
+        split_copy = pltpu.make_async_copy(split_ref, split_feature, sems.at[3])
+        g_copy = pltpu.make_async_copy(g_ref, gh_ref.at[0], sems.at[4])
+        h_copy = pltpu.make_async_copy(h_ref, gh_ref.at[1], sems.at[5])
         split_copy.start()
-        h_copy = pltpu.make_async_copy(h_ref, h_in, sems.at[n_dp])
+        g_copy.start()
         h_copy.start()
-        copies = [pltpu.make_async_copy(x_ref.at[s], x_out.at[s, pl.ds(0, size)], sems.at[s]) for s in range(n_dp)]
-        for copy in copies:
-            copy.start()
-        h_copy.wait()
-        h = h_in[...].astype(f32)
-        for s in range(n_dp):
-            x_out[s, size] = h
         split_copy.wait()
-        for copy in copies:
-            copy.wait()
         at8 = iota((8, LO), 0)
+        work = []
         for n in range(3):
             local = split_feature[n] - me * feat_dev
             owned = (local >= 0) & (local < feat_dev)
             at = jnp.clip(local, 0, feat_dev - 1)
             s, f = at // feats, at % feats
-            mine = (at8 == f % 8) & owned
+            copy = pltpu.make_async_copy(x_ref.at[s, pl.ds(f // 8 * tiles, tiles)], rows_ref.at[n], sems.at[n])
+            copy.start()
+            work.append((copy, (at8 == f % 8) & owned))
+        g_copy.wait()
+        h_copy.wait()
+        g_out[...] = gh_ref[0].astype(f32)
+        h_out[...] = gh_ref[1].astype(f32)
+        for n, (copy, mine) in enumerate(work):
+            copy.wait()
             for i in range(tiles):
-                tile = x_out[s, f // 8 * tiles + i]
-                o_ref[n * tiles + i : n * tiles + i + 1, :] = jnp.sum(jnp.where(mine, tile, 0.0), axis=0, keepdims=True)
+                row = jnp.sum(jnp.where(mine, rows_ref[n, i], 0.0), axis=0, keepdims=True)
+                o_ref[n * tiles + i : n * tiles + i + 1, :] = row
 
     return kernel
 
 
-def pick_rows(x, hess, split_feature, groups, tiles, feat_dev):
+def pick_rows(x, grad, hess, split_feature, groups, tiles, feat_dev):
     n_dp = x.shape[0]
     anywhere = pl.BlockSpec(memory_space=pl.ANY)
     vmem = pl.BlockSpec(memory_space=pltpu.VMEM)
     return pl.pallas_call(
         make_pick(groups, tiles, feat_dev, feat_dev // n_dp),
-        out_shape=[
-            jax.ShapeDtypeStruct((3 * tiles, LO), f32),
-            jax.ShapeDtypeStruct((n_dp, groups * tiles + 1, 8, LO), f32),
+        out_shape=[pltpu.VMEM((rows * tiles, LO), f32) for rows in (3, 1, 1)],
+        in_specs=[anywhere] * 4,
+        out_specs=[vmem] * 3,
+        scratch_shapes=[
+            pltpu.SMEM((3,), i32),
+            pltpu.VMEM((3, tiles, 8, LO), f32),
+            pltpu.VMEM((2, tiles, LO), bf16),
+            pltpu.SemaphoreType.DMA((6,)),
         ],
-        in_specs=[anywhere, anywhere, anywhere],
-        out_specs=[vmem, vmem],
-        scratch_shapes=[pltpu.SMEM((3,), i32), pltpu.VMEM((tiles, LO), bf16), pltpu.SemaphoreType.DMA((n_dp + 2,))],
         name="pick",
-    )(split_feature, x, hess.reshape(tiles, LO))
+    )(split_feature, x, grad.reshape(tiles, LO), hess.reshape(tiles, LO))
 
 
 def swap(value, axis, size, step):
@@ -446,9 +455,8 @@
         x = fine_values.reshape(n_dp, feats, tiles, LO)
         x = jnp.pad(x, ((0, 0), (0, groups * 8 - feats), (0, 0), (0, 0)))
         x = x.reshape(n_dp, groups, 8, tiles, LO).swapaxes(2, 3).reshape(n_dp, groups * tiles, 8, LO)
-        share, x = pick_rows(x, hess, split_feature, groups, tiles, feat_dev)
+        share, g, h = pick_rows(x, grad, hess, split_feature, groups, tiles, feat_dev)
         share = share + swap(share, "feat", n_feat, 1)
-        g = grad.astype(f32).reshape(tiles, LO)
         share, g, block = lax.optimization_barrier((share, g, jnp.concatenate([share, g])))
         got = [swap(block, "dp", n_dp, 1)]
         for i in range(2, n_feat, 2):
@@ -461,8 +469,10 @@
         pair = jnp.stack([jnp.concatenate([mine, g]), jnp.concatenate([other, other_g])])
         pairs = [pair] + [swap(pair, "dp", n_dp, d) for d in range(2, n_dp, 2)]
         x = lax.all_to_all(x, "dp", 0, 0)
-        bins = find_bins(x, slab_rows, groups, tiles)
-        gains = route_and_sum(x, pairs, bins, slab_rows, split_bin, feats, groups, tiles)
+        h = jnp.stack([h, swap(h, "dp", n_dp, 1)])
+        hs = [h] + [swap(h, "dp", n_dp, d) for d in range(2, n_dp, 2)]
+        bins, h = find_bins(x, hs, slab_rows, split_bin, groups, tiles)
+        gains = route_and_sum(h, pairs, bins, slab_rows, split_bin, feats, groups, tiles)
         pieces = [gains] + [None] * (n_dp - 1)
         for d in [*range(n_dp - 2, 0, -2), 1]:
             pieces[d] = swap(gains, "dp", n_dp, d)

time: 54.3 us -> 51 us (0.939)
  waiting for transfers between devices: 12.7 us -> 7.32 us
  starting transfers between devices: 28.2 us -> 30.6 us
    all_to_all x1, waiting for transfers between devices: 3.12 us -> 0.01 us  [shards(): x = lax.all_to_all(x, 'dp', 0, 0)]
    ppermute x14 -> x18, starting transfers between devices: 20.9 us -> 23.3 us  [swap(): return lax.ppermute(value, axis, [(s, s ^ step) for s in range(size)])]
    ppermute x14 -> x18, waiting for transfers between devices: 9.57 us -> 7.32 us  [swap(): return lax.ppermute(value, axis, [(s, s ^ step) for s in range(size)])]
  transfers between devices with their start and end apart: 15 -> 19, of which waited for: 7 -> 7; matrix products, arithmetic and copies ran while one was open for 0% -> 0% of each run, Pallas kernels for 8% -> 12%
where the time goes in v6:
time: 51 us; the launch traced here: 50.7 us
  starting transfers between devices  30.6 us (60%)
  Pallas kernels  11.7 us (23%)
  waiting for transfers between devices  7.32 us (14%)
  local copies, waits for them, and re-layouts  0.84 us (2%)
    ppermute x18, starting transfers between devices, swap(): return lax.ppermute(value, axis, [(s, s ^ step) for s in range(size)])  23.3 us
    ppermute x18, waiting for transfers between devices, swap(): return lax.ppermute(value, axis, [(s, s ^ step) for s in range(size)])  7.32 us
    all_to_all x1, starting transfers between devices, shards(): x = lax.all_to_all(x, 'dp', 0, 0)  7.28 us
    pallas_call x1, Pallas kernels, route_and_sum(): pl.pallas_call(kernel, out_shape=jax.ShapeDtypeStruct((7, feats, BINS), f...  5.56 us
    pallas_call x1, Pallas kernels, find_bins(): pl.pallas_call(make_bins(n_dp, groups, tiles), out_shape=[jax.ShapeDtypeS...  4.54 us
    pallas_call x1, Pallas kernels, pick_rows(): pl.pallas_call(make_pick(groups, tiles, feat_dev, feat_dev // n_dp), out_...  1.59 us
  transfers between devices with their start and end apart: 19, of which 7 were waited for; matrix products, arithmetic and copies ran while one was open for 0% of the time, Pallas kernels for 12%

profile of v6, /device:TPU:0, one launch (start us, length us, event | category | flops | bytes accessed | tf_op | source)
XLA Modules:
  0.0 50.7 jit_solution(9322446224914139703)
XLA Ops:
  0.0 7.3 %all-to-all-start = ((f32[8,16,8,128]{3,2,1,0:T(8,128)}), f32[8,16,8,128]{3,2,1,0:T(8,128)S(1)}, u32[]{:S(2)}, u32[]{:S(2)}) async-start(f32[8,16,8,128]{3,2,1,0:T(8,128)} %bitcast.14), calls=%async_computation | async-start | bytes 1048576 | tf_op jit(solution)/shard_map/all_to_all | solution.py:471
  7.3 1.6 %pick.1 = (f32[24,128]{1,0:T(8,128)S(1)}, f32[8,128]{1,0:T(8,128)S(1)}, f32[8,128]{1,0:T(8,128)S(1)}) custom-call(s32[3]{0:T(128)} %split_ref.1, f32[8,16,8,128]{3,2,1,0:T(8,128)} %bitcast.15, bf16[8,128]{1,0:T(8,128)(2,1)} %bitcast.17, bf16[8,128]{1,0:T(8,128)(2,1)} %bitcast.18), custom_call_target="tpu_custom_call" | custom-call | tf_op jit(solution)/shard_map/pick/pallas_call | solution.py:429
  8.9 0.1 collective-permute-start.4
  9.0 2.1 %collective-permute-start = (f32[8,128]{1,0:T(8,128)S(1)}, f32[8,128]{1,0:T(8,128)S(1)}, u32[]{:S(2)}, u32[]{:S(2)}) collective-permute-start(f32[8,128]{1,0:T(8,128)S(1)} %get-tuple-element.16), channel_id=1, source_target_pairs={{0,4},{4,0},{8,12},{12,8},{16,20},{20,16},{24,28},{28,24},{1,5},{5... | collective-permute-start | bytes 12296 | tf_op jit(solution)/shard_map/ppermute | solution.py:445
  11.0 0.0 collective-permute-done.4
  11.1 1.5 %collective-permute-start.6 = (f32[24,128]{1,0:T(8,128)S(1)}, f32[24,128]{1,0:T(8,128)S(1)}, u32[]{:S(2)}, u32[]{:S(2)}) collective-permute-start(f32[24,128]{1,0:T(8,128)S(1)} %add.33), channel_id=1, source_target_pairs={{0,2},{1,3},{2,0},{3,1},{4,6},{5,7},{6,4},{7,5},{8,10},{9,11},{10,... | collective-permute-start | bytes 36872 | tf_op jit(solution)/shard_map/ppermute | solution.py:445
  12.6 1.0 %collective-permute-start.7 = (f32[24,128]{1,0:T(8,128)S(1)}, f32[24,128]{1,0:T(8,128)S(1)}, u32[]{:S(2)}, u32[]{:S(2)}) collective-permute-start(f32[24,128]{1,0:T(8,128)S(1)} %add.33), channel_id=1, source_target_pairs={{0,6},{1,7},{2,4},{3,5},{4,2},{5,3},{6,0},{7,1},{8,14},{9,15},{10,... | collective-permute-start | bytes 36872 | tf_op jit(solution)/shard_map/ppermute | solution.py:445
  13.6 1.0 %collective-permute-start.5 = (f32[32,128]{1,0:T(8,128)S(1)}, f32[32,128]{1,0:T(8,128)S(1)}, u32[]{:S(2)}, u32[]{:S(2)}) collective-permute-start(f32[32,128]{1,0:T(8,128)S(1)} %pad_maximum_fusion.1), channel_id=1, source_target_pairs={{0,4},{4,0},{8,12},{12,8},{16,20},{20,16},{24,28},{28,24},{1,5},{5... | collective-permute-start | bytes 49160 | tf_op jit(solution)/shard_map/ppermute | solution.py:445
  14.6 0.0 collective-permute-done
  14.6 1.5 %collective-permute-start.1 = (f32[2,8,128]{2,1,0:T(8,128)S(1)}, f32[2,8,128]{2,1,0:T(8,128)S(1)}, u32[]{:S(2)}, u32[]{:S(2)}) collective-permute-start(f32[2,8,128]{2,1,0:T(8,128)S(1)} %pad_maximum_fusion.2.refs_0_), channel_id=1, source_target_pairs={{0,8},{4,12},{8,0},{12,4},{16,24},{20,28},{24,16},{28,20},{1,9},{5... | collective-permute-start | bytes 24584 | tf_op jit(solution)/shard_map/ppermute | solution.py:445
  16.1 2.4 %collective-permute-start.2 = (f32[2,8,128]{2,1,0:T(8,128)S(1)}, f32[2,8,128]{2,1,0:T(8,128)S(1)}, u32[]{:S(2)}, u32[]{:S(2)}) collective-permute-start(f32[2,8,128]{2,1,0:T(8,128)S(1)} %pad_maximum_fusion.2.refs_0_), channel_id=1, source_target_pairs={{0,16},{4,20},{8,24},{12,28},{16,0},{20,4},{24,8},{28,12},{1,17},{... | collective-permute-start | bytes 24584 | tf_op jit(solution)/shard_map/ppermute | solution.py:445
  18.4 0.0 collective-permute-done.6
  18.4 0.6 %collective-permute-start.3 = (f32[2,8,128]{2,1,0:T(8,128)S(1)}, f32[2,8,128]{2,1,0:T(8,128)S(1)}, u32[]{:S(2)}, u32[]{:S(2)}) collective-permute-start(f32[2,8,128]{2,1,0:T(8,128)S(1)} %pad_maximum_fusion.2.refs_0_), channel_id=1, source_target_pairs={{0,24},{4,28},{8,16},{12,20},{16,8},{20,12},{24,0},{28,4},{1,25},{... | collective-permute-start | bytes 24584 | tf_op jit(solution)/shard_map/ppermute | solution.py:445
  19.0 0.0 collective-permute-done.7
  19.0 0.0 collective-permute-done.5
  19.1 0.0 copy-start
  19.1 0.0 copy-start.1
  19.1 3.3 %collective-permute-start.10 = (f32[2,32,128]{2,1,0:T(8,128)S(1)}, f32[2,32,128]{2,1,0:T(8,128)S(1)}, u32[]{:S(2)}, u32[]{:S(2)}) collective-permute-start(f32[2,32,128]{2,1,0:T(8,128)S(1)} %pad_maximum_fusion.refs_0_), channel_id=1, source_target_pairs={{0,24},{4,28},{8,16},{12,20},{16,8},{20,12},{24,0},{28,4},{1,25},{... | collective-permute-start | bytes 98312 | tf_op jit(solution)/shard_map/ppermute | solution.py:445
  22.4 0.0 collective-permute-start.8
  22.4 0.0 collective-permute-done.1.refs_1_
  22.4 1.1 %collective-permute-start.9 = (f32[2,32,128]{2,1,0:T(8,128)S(1)}, f32[2,32,128]{2,1,0:T(8,128)S(1)}, u32[]{:S(2)}, u32[]{:S(2)}) collective-permute-start(f32[2,32,128]{2,1,0:T(8,128)S(1)} %pad_maximum_fusion.refs_0_), channel_id=1, source_target_pairs={{0,16},{4,20},{8,24},{12,28},{16,0},{20,4},{24,8},{28,12},{1,17},{... | collective-permute-start | bytes 98312 | tf_op jit(solution)/shard_map/ppermute | solution.py:445
  23.6 0.0 collective-permute-done.2.refs_2_
  23.6 0.3 collective-permute-done.3.refs_3_
  23.9 0.0 all-to-all-done.x_ref
  23.9 0.0 copy-done
  23.9 0.0 copy-done.1
  23.9 4.5 %bins.1 = (f32[65,16,128]{2,1,0:T(8,128)S(1)}, f32[8,8,128]{2,1,0:T(8,128)S(1)}) custom-call(s32[8]{0:T(128)S(1)} %copy-done, s32[3]{0:T(128)S(1)} %copy-done.1, f32[8,16,8,128]{3,2,1,0:T(8,128)S(1)} %all-to-all-done.x_ref, f32[2,8,128]{2,1,0:T(8,128)S(1)} %pad_maximum_fusion.2.refs_0_, f32[2,8,128]{2,1,0:T(8,128)S(1)} %collective-permute-done.1.refs_1_, ...), custom_call_target="tpu_custom_call" | custom-call | flops 1073741824 | bytes 1048576 | tf_op jit(solution)/shard_map/bins/pallas_call | solution.py:203
  28.5 0.0 collective-permute-done.10.refs_3_
  28.5 0.0 collective-permute-done.8.refs_1_
  28.5 0.0 collective-permute-done.9.refs_2_
  28.5 5.6 %gains.1 = f32[7,16,256]{2,1,0:T(8,128)S(1)} custom-call(s32[8]{0:T(128)S(1)} %copy-done, s32[3]{0:T(128)S(1)} %copy-done.1, f32[8,8,128]{2,1,0:T(8,128)S(1)} %get-tuple-element.17.x_ref, f32[65,16,128]{2,1,0:T(8,128)S(1)} %get-tuple-element.18.bin_ref, f32[2,32,128]{2,1,0:T(8,128)S(1)} %pad_maximum_fusion.refs_0_, ...), custom_call_target="tpu_custom_call" | custom-call | flops 2147483648 | bytes 1048576 | tf_op jit(solution)/shard_map/gains/pallas_call | solution.py:374
  34.0 1.5 %collective-permute-start.11 = (f32[7,16,256]{2,1,0:T(8,128)S(1)}, f32[7,16,256]{2,1,0:T(8,128)S(1)}, u32[]{:S(2)}, u32[]{:S(2)}) collective-permute-start(f32[7,16,256]{2,1,0:T(8,128)S(1)} %gains.1), channel_id=1, source_target_pairs={{0,16},{4,20},{8,24},{12,28},{16,0},{20,4},{24,8},{28,12},{1,17},{... | collective-permute-start | bytes 344072 | tf_op jit(solution)/shard_map/ppermute | solution.py:445
  35.6 2.0 %collective-permute-start.12 = (f32[7,16,256]{2,1,0:T(8,128)S(1)}, f32[7,16,256]{2,1,0:T(8,128)S(1)}, u32[]{:S(2)}, u32[]{:S(2)}) collective-permute-start(f32[7,16,256]{2,1,0:T(8,128)S(1)} %gains.1), channel_id=1, source_target_pairs={{0,8},{4,12},{8,0},{12,4},{16,24},{20,28},{24,16},{28,20},{1,9},{5... | collective-permute-start | bytes 344072 | tf_op jit(solution)/shard_map/ppermute | solution.py:445
  37.6 1.0 %collective-permute-start.13 = (f32[7,16,256]{2,1,0:T(8,128)S(1)}, f32[7,16,256]{2,1,0:T(8,128)S(1)}, u32[]{:S(2)}, u32[]{:S(2)}) collective-permute-start(f32[7,16,256]{2,1,0:T(8,128)S(1)} %gains.1), channel_id=1, source_target_pairs={{0,4},{4,0},{8,12},{12,8},{16,20},{20,16},{24,28},{28,24},{1,5},{5... | collective-permute-start | bytes 344072 | tf_op jit(solution)/shard_map/ppermute | solution.py:445
  38.6 0.9 %collective-permute-start.14 = (f32[7,16,256]{2,1,0:T(8,128)S(1)}, f32[7,16,256]{2,1,0:T(8,128)S(1)}, u32[]{:S(2)}, u32[]{:S(2)}) collective-permute-start(f32[7,16,256]{2,1,0:T(8,128)S(1)} %gains.1), channel_id=1, source_target_pairs={{0,24},{4,28},{8,16},{12,20},{16,8},{20,12},{24,0},{28,4},{1,25},{... | collective-permute-start | bytes 344072 | tf_op jit(solution)/shard_map/ppermute | solution.py:445
  39.6 0.1 broadcast_in_dim.3
  39.7 1.9 %collective-permute-done.12 = f32[7,16,256]{2,1,0:T(8,128)S(1)} collective-permute-done((f32[7,16,256]{2,1,0:T(8,128)S(1)}, f32[7,16,256]{2,1,0:T(8,128)S(1)}, u32[]{:S(2)}, u32[]{:S(2)}) %collective-permute-start.12) | collective-permute-done | bytes 114720 | tf_op jit(solution)/shard_map/ppermute | solution.py:445
  41.6 0.9 %collective-permute-start.15 = (f32[7,16,256]{2,1,0:T(8,128)S(1)}, f32[7,16,256]{2,1,0:T(8,128)S(1)}, u32[]{:S(2)}, u32[]{:S(2)}) collective-permute-start(f32[7,16,256]{2,1,0:T(8,128)S(1)} %collective-permute-done.12), channel_id=1, source_target_pairs={{0,4},{4,0},{8,12},{12,8},{16,20},{20,16},{24,28},{28,24},{1,5},{5... | collective-permute-start | bytes 344072 | tf_op jit(solution)/shard_map/ppermute | solution.py:445
  42.5 0.2 collective-permute-done.11
  42.7 1.2 %collective-permute-start.16 = (f32[7,16,256]{2,1,0:T(8,128)S(1)}, f32[7,16,256]{2,1,0:T(8,128)S(1)}, u32[]{:S(2)}, u32[]{:S(2)}) collective-permute-start(f32[7,16,256]{2,1,0:T(8,128)S(1)} %collective-permute-done.11), channel_id=1, source_target_pairs={{0,4},{4,0},{8,12},{12,8},{16,20},{20,16},{24,28},{28,24},{1,5},{5... | collective-permute-start | bytes 344072 | tf_op jit(solution)/shard_map/ppermute | solution.py:445
  44.0 1.3 %collective-permute-done.14 = f32[7,16,256]{2,1,0:T(8,128)S(1)} collective-permute-done((f32[7,16,256]{2,1,0:T(8,128)S(1)}, f32[7,16,256]{2,1,0:T(8,128)S(1)}, u32[]{:S(2)}, u32[]{:S(2)}) %collective-permute-start.14) | collective-permute-done | bytes 114720 | tf_op jit(solution)/shard_map/ppermute | solution.py:445
  45.2 1.1 %collective-permute-start.17 = (f32[7,16,256]{2,1,0:T(8,128)S(1)}, f32[7,16,256]{2,1,0:T(8,128)S(1)}, u32[]{:S(2)}, u32[]{:S(2)}) collective-permute-start(f32[7,16,256]{2,1,0:T(8,128)S(1)} %collective-permute-done.14), channel_id=1, source_target_pairs={{0,4},{4,0},{8,12},{12,8},{16,20},{20,16},{24,28},{28,24},{1,5},{5... | collective-permute-start | bytes 344072 | tf_op jit(solution)/shard_map/ppermute | solution.py:445
  46.4 0.0 collective-permute-done.13
  46.4 0.8 %collective-permute-done.15 = f32[7,16,256]{2,1,0:T(8,128)S(1)} collective-permute-done((f32[7,16,256]{2,1,0:T(8,128)S(1)}, f32[7,16,256]{2,1,0:T(8,128)S(1)}, u32[]{:S(2)}, u32[]{:S(2)}) %collective-permute-start.15) | collective-permute-done | bytes 114720 | tf_op jit(solution)/shard_map/ppermute | solution.py:445
  47.2 1.2 %collective-permute-done.16 = f32[7,16,256]{2,1,0:T(8,128)S(1)} collective-permute-done((f32[7,16,256]{2,1,0:T(8,128)S(1)}, f32[7,16,256]{2,1,0:T(8,128)S(1)}, u32[]{:S(2)}, u32[]{:S(2)}) %collective-permute-start.16) | collective-permute-done | bytes 114720 | tf_op jit(solution)/shard_map/ppermute | solution.py:445
  48.4 0.0 copy-start.2
  48.5 1.6 %collective-permute-done.17 = f32[7,16,256]{2,1,0:T(8,128)S(1)} collective-permute-done((f32[7,16,256]{2,1,0:T(8,128)S(1)}, f32[7,16,256]{2,1,0:T(8,128)S(1)}, u32[]{:S(2)}, u32[]{:S(2)}) %collective-permute-start.17) | collective-permute-done | bytes 114720 | tf_op jit(solution)/shard_map/ppermute | solution.py:445
  50.0 0.0 copy-done.2
  50.0 0.7 %constant_dynamic-update-slice_fusion = f32[7,128,256]{2,1,0:T(8,128)} fusion(f32[7,128,256]{2,1,0:T(8,128)} %copy-done.2, f32[7,16,256]{2,1,0:T(8,128)S(1)} %collective-permute-done.17, s32[]{:T(128)S(6)} %select_n.31), kind=kLoop, calls=%fused_computation.6 | loop fusion | bytes 229380 | tf_op jit(solution)/shard_map/dynamic_update_slice | solution.py:484
  (15 shorter events, 0.1 us)
Async XLA Ops:
  0.0 23.9 %all-to-all-start = ((f32[8,16,8,128]{3,2,1,0:T(8,128)}), f32[8,16,8,128]{3,2,1,0:T(8,128)S(1)}, u32[]{:S(2)}, u32[]{:S(2)}) async-start(f32[8,16,8,128]{3,2,1,0:T(8,128)} %bitcast.14), calls=%async_computation | async-start | bytes 1048576 | tf_op jit(solution)/shard_map/all_to_all | solution.py:471
  8.9 2.2 %collective-permute-start.4 = (f32[24,128]{1,0:T(8,128)S(1)}, f32[24,128]{1,0:T(8,128)S(1)}, u32[]{:S(2)}, u32[]{:S(2)}) collective-permute-start(f32[24,128]{1,0:T(8,128)S(1)} %get-tuple-element.19), channel_id=1, source_target_pairs={{0,1},{1,0},{2,3},{3,2},{4,5},{5,4},{6,7},{7,6},{8,9},{9,8},{10,11... | collective-permute-start | bytes 36872 | tf_op jit(solution)/shard_map/ppermute | solution.py:445
  9.0 5.7 %collective-permute-start = (f32[8,128]{1,0:T(8,128)S(1)}, f32[8,128]{1,0:T(8,128)S(1)}, u32[]{:S(2)}, u32[]{:S(2)}) collective-permute-start(f32[8,128]{1,0:T(8,128)S(1)} %get-tuple-element.16), channel_id=1, source_target_pairs={{0,4},{4,0},{8,12},{12,8},{16,20},{20,16},{24,28},{28,24},{1,5},{5... | collective-permute-start | bytes 12296 | tf_op jit(solution)/shard_map/ppermute | solution.py:445
  11.1 7.4 %collective-permute-start.6 = (f32[24,128]{1,0:T(8,128)S(1)}, f32[24,128]{1,0:T(8,128)S(1)}, u32[]{:S(2)}, u32[]{:S(2)}) collective-permute-start(f32[24,128]{1,0:T(8,128)S(1)} %add.33), channel_id=1, source_target_pairs={{0,2},{1,3},{2,0},{3,1},{4,6},{5,7},{6,4},{7,5},{8,10},{9,11},{10,... | collective-permute-start | bytes 36872 | tf_op jit(solution)/shard_map/ppermute | solution.py:445
  12.6 6.4 %collective-permute-start.7 = (f32[24,128]{1,0:T(8,128)S(1)}, f32[24,128]{1,0:T(8,128)S(1)}, u32[]{:S(2)}, u32[]{:S(2)}) collective-permute-start(f32[24,128]{1,0:T(8,128)S(1)} %add.33), channel_id=1, source_target_pairs={{0,6},{1,7},{2,4},{3,5},{4,2},{5,3},{6,0},{7,1},{8,14},{9,15},{10,... | collective-permute-start | bytes 36872 | tf_op jit(solution)/shard_map/ppermute | solution.py:445
  13.6 5.4 %collective-permute-start.5 = (f32[32,128]{1,0:T(8,128)S(1)}, f32[32,128]{1,0:T(8,128)S(1)}, u32[]{:S(2)}, u32[]{:S(2)}) collective-permute-start(f32[32,128]{1,0:T(8,128)S(1)} %pad_maximum_fusion.1), channel_id=1, source_target_pairs={{0,4},{4,0},{8,12},{12,8},{16,20},{20,16},{24,28},{28,24},{1,5},{5... | collective-permute-start | bytes 49160 | tf_op jit(solution)/shard_map/ppermute | solution.py:445
  14.6 7.8 %collective-permute-start.1 = (f32[2,8,128]{2,1,0:T(8,128)S(1)}, f32[2,8,128]{2,1,0:T(8,128)S(1)}, u32[]{:S(2)}, u32[]{:S(2)}) collective-permute-start(f32[2,8,128]{2,1,0:T(8,128)S(1)} %pad_maximum_fusion.2.refs_0_), channel_id=1, source_target_pairs={{0,8},{4,12},{8,0},{12,4},{16,24},{20,28},{24,16},{28,20},{1,9},{5... | collective-permute-start | bytes 24584 | tf_op jit(solution)/shard_map/ppermute | solution.py:445
  16.1 7.5 %collective-permute-start.2 = (f32[2,8,128]{2,1,0:T(8,128)S(1)}, f32[2,8,128]{2,1,0:T(8,128)S(1)}, u32[]{:S(2)}, u32[]{:S(2)}) collective-permute-start(f32[2,8,128]{2,1,0:T(8,128)S(1)} %pad_maximum_fusion.2.refs_0_), channel_id=1, source_target_pairs={{0,16},{4,20},{8,24},{12,28},{16,0},{20,4},{24,8},{28,12},{1,17},{... | collective-permute-start | bytes 24584 | tf_op jit(solution)/shard_map/ppermute | solution.py:445
  18.4 5.4 %collective-permute-start.3 = (f32[2,8,128]{2,1,0:T(8,128)S(1)}, f32[2,8,128]{2,1,0:T(8,128)S(1)}, u32[]{:S(2)}, u32[]{:S(2)}) collective-permute-start(f32[2,8,128]{2,1,0:T(8,128)S(1)} %pad_maximum_fusion.2.refs_0_), channel_id=1, source_target_pairs={{0,24},{4,28},{8,16},{12,20},{16,8},{20,12},{24,0},{28,4},{1,25},{... | collective-permute-start | bytes 24584 | tf_op jit(solution)/shard_map/ppermute | solution.py:445
  19.1 4.8 %copy-start = (s32[8]{0:T(128)S(1)}, s32[8]{0:T(128)}, u32[]{:S(2)}) copy-start(s32[8]{0:T(128)} %slab_rows.3) | copy-start | bytes 100
  19.1 4.8 %copy-start.1 = (s32[3]{0:T(128)S(1)}, s32[3]{0:T(128)}, u32[]{:S(2)}) copy-start(s32[3]{0:T(128)} %split_bin.1) | copy-start | bytes 40
  19.1 9.4 %collective-permute-start.10 = (f32[2,32,128]{2,1,0:T(8,128)S(1)}, f32[2,32,128]{2,1,0:T(8,128)S(1)}, u32[]{:S(2)}, u32[]{:S(2)}) collective-permute-start(f32[2,32,128]{2,1,0:T(8,128)S(1)} %pad_maximum_fusion.refs_0_), channel_id=1, source_target_pairs={{0,24},{4,28},{8,16},{12,20},{16,8},{20,12},{24,0},{28,4},{1,25},{... | collective-permute-start | bytes 98312 | tf_op jit(solution)/shard_map/ppermute | solution.py:445
  22.4 6.0 %collective-permute-start.8 = (f32[2,32,128]{2,1,0:T(8,128)S(1)}, f32[2,32,128]{2,1,0:T(8,128)S(1)}, u32[]{:S(2)}, u32[]{:S(2)}) collective-permute-start(f32[2,32,128]{2,1,0:T(8,128)S(1)} %pad_maximum_fusion.refs_0_), channel_id=1, source_target_pairs={{0,8},{4,12},{8,0},{12,4},{16,24},{20,28},{24,16},{28,20},{1,9},{5... | collective-permute-start | bytes 98312 | tf_op jit(solution)/shard_map/ppermute | solution.py:445
  22.4 6.0 %collective-permute-start.9 = (f32[2,32,128]{2,1,0:T(8,128)S(1)}, f32[2,32,128]{2,1,0:T(8,128)S(1)}, u32[]{:S(2)}, u32[]{:S(2)}) collective-permute-start(f32[2,32,128]{2,1,0:T(8,128)S(1)} %pad_maximum_fusion.refs_0_), channel_id=1, source_target_pairs={{0,16},{4,20},{8,24},{12,28},{16,0},{20,4},{24,8},{28,12},{1,17},{... | collective-permute-start | bytes 98312 | tf_op jit(solution)/shard_map/ppermute | solution.py:445
  34.0 8.7 %collective-permute-start.11 = (f32[7,16,256]{2,1,0:T(8,128)S(1)}, f32[7,16,256]{2,1,0:T(8,128)S(1)}, u32[]{:S(2)}, u32[]{:S(2)}) collective-permute-start(f32[7,16,256]{2,1,0:T(8,128)S(1)} %gains.1), channel_id=1, source_target_pairs={{0,16},{4,20},{8,24},{12,28},{16,0},{20,4},{24,8},{28,12},{1,17},{... | collective-permute-start | bytes 344072 | tf_op jit(solution)/shard_map/ppermute | solution.py:445
  35.6 6.0 %collective-permute-start.12 = (f32[7,16,256]{2,1,0:T(8,128)S(1)}, f32[7,16,256]{2,1,0:T(8,128)S(1)}, u32[]{:S(2)}, u32[]{:S(2)}) collective-permute-start(f32[7,16,256]{2,1,0:T(8,128)S(1)} %gains.1), channel_id=1, source_target_pairs={{0,8},{4,12},{8,0},{12,4},{16,24},{20,28},{24,16},{28,20},{1,9},{5... | collective-permute-start | bytes 344072 | tf_op jit(solution)/shard_map/ppermute | solution.py:445
  37.6 8.8 %collective-permute-start.13 = (f32[7,16,256]{2,1,0:T(8,128)S(1)}, f32[7,16,256]{2,1,0:T(8,128)S(1)}, u32[]{:S(2)}, u32[]{:S(2)}) collective-permute-start(f32[7,16,256]{2,1,0:T(8,128)S(1)} %gains.1), channel_id=1, source_target_pairs={{0,4},{4,0},{8,12},{12,8},{16,20},{20,16},{24,28},{28,24},{1,5},{5... | collective-permute-start | bytes 344072 | tf_op jit(solution)/shard_map/ppermute | solution.py:445
  38.6 6.6 %collective-permute-start.14 = (f32[7,16,256]{2,1,0:T(8,128)S(1)}, f32[7,16,256]{2,1,0:T(8,128)S(1)}, u32[]{:S(2)}, u32[]{:S(2)}) collective-permute-start(f32[7,16,256]{2,1,0:T(8,128)S(1)} %gains.1), channel_id=1, source_target_pairs={{0,24},{4,28},{8,16},{12,20},{16,8},{20,12},{24,0},{28,4},{1,25},{... | collective-permute-start | bytes 344072 | tf_op jit(solution)/shard_map/ppermute | solution.py:445
  41.6 5.6 %collective-permute-start.15 = (f32[7,16,256]{2,1,0:T(8,128)S(1)}, f32[7,16,256]{2,1,0:T(8,128)S(1)}, u32[]{:S(2)}, u32[]{:S(2)}) collective-permute-start(f32[7,16,256]{2,1,0:T(8,128)S(1)} %collective-permute-done.12), channel_id=1, source_target_pairs={{0,4},{4,0},{8,12},{12,8},{16,20},{20,16},{24,28},{28,24},{1,5},{5... | collective-permute-start | bytes 344072 | tf_op jit(solution)/shard_map/ppermute | solution.py:445
  42.7 5.7 %collective-permute-start.16 = (f32[7,16,256]{2,1,0:T(8,128)S(1)}, f32[7,16,256]{2,1,0:T(8,128)S(1)}, u32[]{:S(2)}, u32[]{:S(2)}) collective-permute-start(f32[7,16,256]{2,1,0:T(8,128)S(1)} %collective-permute-done.11), channel_id=1, source_target_pairs={{0,4},{4,0},{8,12},{12,8},{16,20},{20,16},{24,28},{28,24},{1,5},{5... | collective-permute-start | bytes 344072 | tf_op jit(solution)/shard_map/ppermute | solution.py:445
  45.2 4.8 %collective-permute-start.17 = (f32[7,16,256]{2,1,0:T(8,128)S(1)}, f32[7,16,256]{2,1,0:T(8,128)S(1)}, u32[]{:S(2)}, u32[]{:S(2)}) collective-permute-start(f32[7,16,256]{2,1,0:T(8,128)S(1)} %collective-permute-done.14), channel_id=1, source_target_pairs={{0,4},{4,0},{8,12},{12,8},{16,20},{20,16},{24,28},{28,24},{1,5},{5... | collective-permute-start | bytes 344072 | tf_op jit(solution)/shard_map/ppermute | solution.py:445
  48.4 1.6 %copy-start.2 = (f32[7,128,256]{2,1,0:T(8,128)}, f32[7,128,256]{2,1,0:T(8,128)S(1)}, u32[]{:S(2)}) copy-start(f32[7,128,256]{2,1,0:T(8,128)S(1)} %constant_dynamic-update-slice_fusion.1) | copy-start | bytes 2752516

commit v7 on v6

--- a/solution.py
+++ b/solution.py
@@ -88,6 +88,21 @@
     return used
 
 
+def over_blocks(used, body):
+    whole = (used + GROUP // 2 - 1) // GROUP
+
+    def long(q, _):
+        body(q * GROUP, GROUP)
+        return 0
+
+    def short(q, _):
+        body(whole * GROUP, GROUP // 2)
+        return 0
+
+    lax.fori_loop(0, whole, long, 0)
+    lax.fori_loop(0, (used > whole * GROUP).astype(i32), short, 0)
+
+
 def list_shape(n_dp, tiles):
     return pltpu.SMEM((n_dp * tiles + GROUP,), i32)
 
@@ -104,7 +119,6 @@
     blocks = n_dp * tiles
     feats = groups * 8
     quads = feats // 4
-    width = GROUP * LO
 
     def kernel(slab_rows, _, x_ref, *refs):
         hs, (o_ref, h_out, list_ref, h_ref, cnt_ref, cut_ref, map_ref) = refs[: n_dp // 2], refs[n_dp // 2 :]
@@ -119,16 +133,16 @@
                 h_ref[s * tiles + i] = jnp.broadcast_to(h[i : i + 1], (8, LO))
         h_ref[blocks] = jnp.zeros((8, LO), f32)
         cnt_ref[...] = jnp.zeros_like(cnt_ref)
-        one, zero = jnp.ones((16, width), bf16), jnp.zeros((16, width), bf16)
 
         def fine_block(at):
             s, i = jnp.minimum(at // tiles, n_dp - 1), at % tiles
             return fine_of(jnp.concatenate([x_ref[s, g * tiles + i] for g in range(groups)], 0))
 
-        def count(q, _):
+        def count(start, length):
+            one, zero = jnp.ones((16, length * LO), bf16), jnp.zeros((16, length * LO), bf16)
             ts, hs = [], []
-            for i in range(GROUP):
-                at = list_ref[q * GROUP + i]
+            for i in range(length):
+                at = list_ref[start + i]
                 ts.append(fine_block(at))
                 hs.append(h_ref[at])
             h = jnp.concatenate(hs, 1)
@@ -140,10 +154,8 @@
                     left += hot(spread(upper, f), SIDE, h, zero)
                     right += hot(spread(lower, f), SIDE, one, zero)
                 cnt_ref[quad] += dot_nt(jnp.concatenate(left, 0), jnp.concatenate(right, 0))
-            return 0
-
-        rounds = (used + GROUP - 1) // GROUP
-        lax.fori_loop(0, rounds, count, 0)
+
+        over_blocks(used, count)
         counts = []
         for quad in range(quads):
             lane = iota((SIDE, LO), 1) // SIDE
@@ -173,9 +185,9 @@
             map_ref[quad] = words[quad]
         upper_half = sub >= 4
 
-        def look_up(q, _):
-            for i in range(GROUP):
-                at = list_ref[q * GROUP + i]
+        def look_up(start, length):
+            for i in range(length):
+                at = list_ref[start + i]
                 fine = fine_block(at).astype(i32)
                 for g in range(groups):
                     here = fine[g * 8 : g * 8 + 8]
@@ -188,9 +200,8 @@
                         value = jnp.where((t >= FINE_BINS // 2) == upper_half, value, 0)
                         found.append(value + pltpu.roll(value, 4, 0))
                     o_ref[at, g * 8 : g * 8 + 8, :] = jnp.where(upper_half, found[1], found[0]).astype(f32)
-            return 0
-
-        lax.fori_loop(0, rounds, look_up, 0)
+
+        over_blocks(used, look_up)
 
     return kernel
 
@@ -228,8 +239,7 @@
         pairs, ch_ref, t_ref = refs[: n_dp // 2], refs[n_dp // 2], refs[n_dp // 2 + 1]
         me = lax.axis_index("dp")
         one, zero = jnp.ones((16, LO), bf16), jnp.zeros((16, LO), bf16)
-        counts = jnp.zeros((LO, LO), f32)
-        nothing = [zero] * (SIDE // 16)
+        counts = jnp.zeros((3 * SIDE, 3 * SIDE), f32)
         for j in range(n_dp):
             s = me ^ j
             row = iota((tiles, LO), 0) * LO + iota((tiles, LO), 1)
@@ -247,9 +257,9 @@
                 right = [jnp.concatenate(hot(spread(lower, i), SIDE, one, zero), 0) for i in range(tiles)]
                 lefts.append(jnp.concatenate(left, 1))
                 rights.append(jnp.concatenate(right, 1))
-            empty = jnp.zeros((SIDE, tiles * LO), bf16)
-            counts += dot_nt(jnp.concatenate(lefts + [empty], 0), jnp.concatenate(rights + [empty], 0))
+            counts += dot_nt(jnp.concatenate(lefts, 0), jnp.concatenate(rights, 0))
         lane = iota((SIDE, LO), 1)
+        counts = jnp.concatenate([counts, jnp.zeros((3 * SIDE, LO - 3 * SIDE), f32)], 1)
         mine = counts[:SIDE]
         for n in range(1, 3):
             mine = jnp.where(lane // SIDE == n, counts[n * SIDE : (n + 1) * SIDE], mine)
@@ -276,20 +286,20 @@
 
 def make_gains(n_dp, feats_all, feats, tiles):
     quads = feats_all // 4
-    width = GROUP * LO
     lanes = 4 * UPPER * 8
 
     def kernel(slab_rows, bin_ref, ch_ref, o_ref, list_ref, acc_ref, cum_ref):
         used = list_blocks(slab_rows, list_ref, n_dp, tiles)
         acc_ref[...] = jnp.zeros_like(acc_ref)
-        kk = [to_bf16(iota((16, width), 0) // 8 + 2 * j) for j in range(UPPER // 2)]
-        one, zero = jnp.ones((16, width), bf16), jnp.zeros((16, width), bf16)
         lane = iota((INNER, lanes), 1) // (UPPER * 8)
 
-        def add(q, _):
+        def add(start, length):
+            width = length * LO
+            kk = [to_bf16(iota((16, width), 0) // 8 + 2 * j) for j in range(UPPER // 2)]
+            one, zero = jnp.ones((16, width), bf16), jnp.zeros((16, width), bf16)
             bs, chs = [], []
-            for i in range(GROUP):
-                at = list_ref[q * GROUP + i]
+            for i in range(length):
+                at = list_ref[start + i]
                 bs.append(bin_ref[at])
                 chs.append(ch_ref[at])
             ch = jnp.concatenate(chs, 1)
@@ -308,9 +318,8 @@
                 for i in range(1, 4):
                     mine = jnp.where(lane == i, out[i * INNER : (i + 1) * INNER], mine)
                 acc_ref[quad, :INNER, :lanes] += mine
-            return 0
-
-        lax.fori_loop(0, (used + GROUP - 1) // GROUP, add, 0)
+
+        over_blocks(used, add)
         r, c = iota((LO, 2 * LO), 0), iota((LO, 2 * LO), 1)
         upto = to_bf16(r <= c)
         at = iota((8, LO), 1)
@@ -479,7 +488,7 @@
         for d in range(3, n_dp, 2):
             pieces[d] = swap(pieces[d - 1], "dp", n_dp, 1)
         whole = jnp.zeros((7, feat_dev, BINS), f32)
-        order = [4, 2, 1] + [*range(6, n_dp, 2)] + [*range(3, n_dp, 2)]
+        order = [4, 2] + [*range(6, n_dp, 2)] + [1] + [*range(3, n_dp, 2)]
         for d in [0] + [d for d in order if d < n_dp]:
             whole = lax.dynamic_update_slice_in_dim(whole, pieces[d], (me ^ d) * feats, 1)
         return whole

time: 51 us -> 50.3 us (0.986)
  transfers between devices with their start and end apart: 19 -> 19, of which waited for: 7 -> 6; matrix products, arithmetic and copies ran while one was open for 0% -> 0% of each run, Pallas kernels for 12% -> 12%
where the time goes in v7:
time: 50.3 us; the launch traced here: 50 us
  starting transfers between devices  30.4 us (60%)
  Pallas kernels  11.6 us (23%)
  waiting for transfers between devices  6.88 us (14%)
  local copies, waits for them, and re-layouts  0.84 us (2%)
    ppermute x18, starting transfers between devices, swap(): return lax.ppermute(value, axis, [(s, s ^ step) for s in range(size)])  23.2 us
    all_to_all x1, starting transfers between devices, shards(): x = lax.all_to_all(x, 'dp', 0, 0)  7.28 us
    ppermute x18, waiting for transfers between devices, swap(): return lax.ppermute(value, axis, [(s, s ^ step) for s in range(size)])  6.88 us
    pallas_call x1, Pallas kernels, route_and_sum(): pl.pallas_call(kernel, out_shape=jax.ShapeDtypeStruct((7, feats, BINS), f...  5.44 us
    pallas_call x1, Pallas kernels, find_bins(): pl.pallas_call(make_bins(n_dp, groups, tiles), out_shape=[jax.ShapeDtypeS...  4.55 us
    pallas_call x1, Pallas kernels, pick_rows(): pl.pallas_call(make_pick(groups, tiles, feat_dev, feat_dev // n_dp), out_...  1.59 us
  transfers between devices with their start and end apart: 19, of which 6 were waited for; matrix products, arithmetic and copies ran while one was open for 0% of the time, Pallas kernels for 12%

profile of v7, /device:TPU:0, one launch (start us, length us, event | category | flops | bytes accessed | tf_op | source)
XLA Modules:
  0.0 50.0 jit_solution(3056623896807825914)
XLA Ops:
  0.0 7.3 %all-to-all-start = ((f32[8,16,8,128]{3,2,1,0:T(8,128)}), f32[8,16,8,128]{3,2,1,0:T(8,128)S(1)}, u32[]{:S(2)}, u32[]{:S(2)}) async-start(f32[8,16,8,128]{3,2,1,0:T(8,128)} %bitcast.14), calls=%async_computation | async-start | bytes 1048576 | tf_op jit(solution)/shard_map/all_to_all | solution.py:480
  7.3 1.6 %pick.1 = (f32[24,128]{1,0:T(8,128)S(1)}, f32[8,128]{1,0:T(8,128)S(1)}, f32[8,128]{1,0:T(8,128)S(1)}) custom-call(s32[3]{0:T(128)} %split_ref.1, f32[8,16,8,128]{3,2,1,0:T(8,128)} %bitcast.15, bf16[8,128]{1,0:T(8,128)(2,1)} %bitcast.17, bf16[8,128]{1,0:T(8,128)(2,1)} %bitcast.18), custom_call_target="tpu_custom_call" | custom-call | tf_op jit(solution)/shard_map/pick/pallas_call | solution.py:438
  8.9 0.1 collective-permute-start.4
  9.0 2.1 %collective-permute-start = (f32[8,128]{1,0:T(8,128)S(1)}, f32[8,128]{1,0:T(8,128)S(1)}, u32[]{:S(2)}, u32[]{:S(2)}) collective-permute-start(f32[8,128]{1,0:T(8,128)S(1)} %get-tuple-element.16), channel_id=1, source_target_pairs={{0,4},{4,0},{8,12},{12,8},{16,20},{20,16},{24,28},{28,24},{1,5},{5... | collective-permute-start | bytes 12296 | tf_op jit(solution)/shard_map/ppermute | solution.py:454
  11.0 0.0 collective-permute-done.4
  11.1 1.5 %collective-permute-start.6 = (f32[24,128]{1,0:T(8,128)S(1)}, f32[24,128]{1,0:T(8,128)S(1)}, u32[]{:S(2)}, u32[]{:S(2)}) collective-permute-start(f32[24,128]{1,0:T(8,128)S(1)} %add.33), channel_id=1, source_target_pairs={{0,2},{1,3},{2,0},{3,1},{4,6},{5,7},{6,4},{7,5},{8,10},{9,11},{10,... | collective-permute-start | bytes 36872 | tf_op jit(solution)/shard_map/ppermute | solution.py:454
  12.6 1.0 %collective-permute-start.7 = (f32[24,128]{1,0:T(8,128)S(1)}, f32[24,128]{1,0:T(8,128)S(1)}, u32[]{:S(2)}, u32[]{:S(2)}) collective-permute-start(f32[24,128]{1,0:T(8,128)S(1)} %add.33), channel_id=1, source_target_pairs={{0,6},{1,7},{2,4},{3,5},{4,2},{5,3},{6,0},{7,1},{8,14},{9,15},{10,... | collective-permute-start | bytes 36872 | tf_op jit(solution)/shard_map/ppermute | solution.py:454
  13.6 1.0 %collective-permute-start.5 = (f32[32,128]{1,0:T(8,128)S(1)}, f32[32,128]{1,0:T(8,128)S(1)}, u32[]{:S(2)}, u32[]{:S(2)}) collective-permute-start(f32[32,128]{1,0:T(8,128)S(1)} %pad_maximum_fusion.1), channel_id=1, source_target_pairs={{0,4},{4,0},{8,12},{12,8},{16,20},{20,16},{24,28},{28,24},{1,5},{5... | collective-permute-start | bytes 49160 | tf_op jit(solution)/shard_map/ppermute | solution.py:454
  14.6 0.0 collective-permute-done
  14.6 1.5 %collective-permute-start.1 = (f32[2,8,128]{2,1,0:T(8,128)S(1)}, f32[2,8,128]{2,1,0:T(8,128)S(1)}, u32[]{:S(2)}, u32[]{:S(2)}) collective-permute-start(f32[2,8,128]{2,1,0:T(8,128)S(1)} %pad_maximum_fusion.2.refs_0_), channel_id=1, source_target_pairs={{0,8},{4,12},{8,0},{12,4},{16,24},{20,28},{24,16},{28,20},{1,9},{5... | collective-permute-start | bytes 24584 | tf_op jit(solution)/shard_map/ppermute | solution.py:454
  16.1 2.4 %collective-permute-start.2 = (f32[2,8,128]{2,1,0:T(8,128)S(1)}, f32[2,8,128]{2,1,0:T(8,128)S(1)}, u32[]{:S(2)}, u32[]{:S(2)}) collective-permute-start(f32[2,8,128]{2,1,0:T(8,128)S(1)} %pad_maximum_fusion.2.refs_0_), channel_id=1, source_target_pairs={{0,16},{4,20},{8,24},{12,28},{16,0},{20,4},{24,8},{28,12},{1,17},{... | collective-permute-start | bytes 24584 | tf_op jit(solution)/shard_map/ppermute | solution.py:454
  18.4 0.0 collective-permute-done.6
  18.4 0.6 %collective-permute-start.3 = (f32[2,8,128]{2,1,0:T(8,128)S(1)}, f32[2,8,128]{2,1,0:T(8,128)S(1)}, u32[]{:S(2)}, u32[]{:S(2)}) collective-permute-start(f32[2,8,128]{2,1,0:T(8,128)S(1)} %pad_maximum_fusion.2.refs_0_), channel_id=1, source_target_pairs={{0,24},{4,28},{8,16},{12,20},{16,8},{20,12},{24,0},{28,4},{1,25},{... | collective-permute-start | bytes 24584 | tf_op jit(solution)/shard_map/ppermute | solution.py:454
  19.0 0.0 collective-permute-done.7
  19.0 0.0 collective-permute-done.5
  19.1 0.0 copy-start
  19.1 0.0 copy-start.1
  19.1 3.3 %collective-permute-start.10 = (f32[2,32,128]{2,1,0:T(8,128)S(1)}, f32[2,32,128]{2,1,0:T(8,128)S(1)}, u32[]{:S(2)}, u32[]{:S(2)}) collective-permute-start(f32[2,32,128]{2,1,0:T(8,128)S(1)} %pad_maximum_fusion.refs_0_), channel_id=1, source_target_pairs={{0,24},{4,28},{8,16},{12,20},{16,8},{20,12},{24,0},{28,4},{1,25},{... | collective-permute-start | bytes 98312 | tf_op jit(solution)/shard_map/ppermute | solution.py:454
  22.4 0.0 collective-permute-start.8
  22.4 0.0 collective-permute-done.1.refs_1_
  22.4 1.1 %collective-permute-start.9 = (f32[2,32,128]{2,1,0:T(8,128)S(1)}, f32[2,32,128]{2,1,0:T(8,128)S(1)}, u32[]{:S(2)}, u32[]{:S(2)}) collective-permute-start(f32[2,32,128]{2,1,0:T(8,128)S(1)} %pad_maximum_fusion.refs_0_), channel_id=1, source_target_pairs={{0,16},{4,20},{8,24},{12,28},{16,0},{20,4},{24,8},{28,12},{1,17},{... | collective-permute-start | bytes 98312 | tf_op jit(solution)/shard_map/ppermute | solution.py:454
  23.6 0.0 collective-permute-done.2.refs_2_
  23.6 0.3 collective-permute-done.3.refs_3_
  23.9 0.0 all-to-all-done.x_ref
  23.9 0.0 copy-done
  23.9 0.0 copy-done.1
  23.9 4.5 %bins.1 = (f32[65,16,128]{2,1,0:T(8,128)S(1)}, f32[8,8,128]{2,1,0:T(8,128)S(1)}) custom-call(s32[8]{0:T(128)S(1)} %copy-done, s32[3]{0:T(128)S(1)} %copy-done.1, f32[8,16,8,128]{3,2,1,0:T(8,128)S(1)} %all-to-all-done.x_ref, f32[2,8,128]{2,1,0:T(8,128)S(1)} %pad_maximum_fusion.2.refs_0_, f32[2,8,128]{2,1,0:T(8,128)S(1)} %collective-permute-done.1.refs_1_, ...), custom_call_target="tpu_custom_call" | custom-call | flops 1073741824 | bytes 1048576 | tf_op jit(solution)/shard_map/bins/pallas_call | solution.py:214
  28.5 0.0 collective-permute-done.10.refs_3_
  28.5 0.0 collective-permute-done.8.refs_1_
  28.5 0.0 collective-permute-done.9.refs_2_
  28.5 5.4 %gains.1 = f32[7,16,256]{2,1,0:T(8,128)S(1)} custom-call(s32[8]{0:T(128)S(1)} %copy-done, s32[3]{0:T(128)S(1)} %copy-done.1, f32[8,8,128]{2,1,0:T(8,128)S(1)} %get-tuple-element.17.x_ref, f32[65,16,128]{2,1,0:T(8,128)S(1)} %get-tuple-element.18.bin_ref, f32[2,32,128]{2,1,0:T(8,128)S(1)} %pad_maximum_fusion.refs_0_, ...), custom_call_target="tpu_custom_call" | custom-call | flops 2147483648 | bytes 1048576 | tf_op jit(solution)/shard_map/gains/pallas_call | solution.py:383
  33.9 1.6 %collective-permute-start.11 = (f32[7,16,256]{2,1,0:T(8,128)S(1)}, f32[7,16,256]{2,1,0:T(8,128)S(1)}, u32[]{:S(2)}, u32[]{:S(2)}) collective-permute-start(f32[7,16,256]{2,1,0:T(8,128)S(1)} %gains.1), channel_id=1, source_target_pairs={{0,16},{4,20},{8,24},{12,28},{16,0},{20,4},{24,8},{28,12},{1,17},{... | collective-permute-start | bytes 344072 | tf_op jit(solution)/shard_map/ppermute | solution.py:454
  35.5 2.0 %collective-permute-start.12 = (f32[7,16,256]{2,1,0:T(8,128)S(1)}, f32[7,16,256]{2,1,0:T(8,128)S(1)}, u32[]{:S(2)}, u32[]{:S(2)}) collective-permute-start(f32[7,16,256]{2,1,0:T(8,128)S(1)} %gains.1), channel_id=1, source_target_pairs={{0,8},{4,12},{8,0},{12,4},{16,24},{20,28},{24,16},{28,20},{1,9},{5... | collective-permute-start | bytes 344072 | tf_op jit(solution)/shard_map/ppermute | solution.py:454
  37.5 0.9 %collective-permute-start.13 = (f32[7,16,256]{2,1,0:T(8,128)S(1)}, f32[7,16,256]{2,1,0:T(8,128)S(1)}, u32[]{:S(2)}, u32[]{:S(2)}) collective-permute-start(f32[7,16,256]{2,1,0:T(8,128)S(1)} %gains.1), channel_id=1, source_target_pairs={{0,24},{4,28},{8,16},{12,20},{16,8},{20,12},{24,0},{28,4},{1,25},{... | collective-permute-start | bytes 344072 | tf_op jit(solution)/shard_map/ppermute | solution.py:454
  38.4 1.1 %collective-permute-start.14 = (f32[7,16,256]{2,1,0:T(8,128)S(1)}, f32[7,16,256]{2,1,0:T(8,128)S(1)}, u32[]{:S(2)}, u32[]{:S(2)}) collective-permute-start(f32[7,16,256]{2,1,0:T(8,128)S(1)} %gains.1), channel_id=1, source_target_pairs={{0,4},{4,0},{8,12},{12,8},{16,20},{20,16},{24,28},{28,24},{1,5},{5... | collective-permute-start | bytes 344072 | tf_op jit(solution)/shard_map/ppermute | solution.py:454
  39.5 0.1 broadcast_in_dim.3
  39.6 2.5 %collective-permute-done.12 = f32[7,16,256]{2,1,0:T(8,128)S(1)} collective-permute-done((f32[7,16,256]{2,1,0:T(8,128)S(1)}, f32[7,16,256]{2,1,0:T(8,128)S(1)}, u32[]{:S(2)}, u32[]{:S(2)}) %collective-permute-start.12) | collective-permute-done | bytes 114720 | tf_op jit(solution)/shard_map/ppermute | solution.py:454
  42.1 0.8 %collective-permute-start.15 = (f32[7,16,256]{2,1,0:T(8,128)S(1)}, f32[7,16,256]{2,1,0:T(8,128)S(1)}, u32[]{:S(2)}, u32[]{:S(2)}) collective-permute-start(f32[7,16,256]{2,1,0:T(8,128)S(1)} %collective-permute-done.12), channel_id=1, source_target_pairs={{0,4},{4,0},{8,12},{12,8},{16,20},{20,16},{24,28},{28,24},{1,5},{5... | collective-permute-start | bytes 344072 | tf_op jit(solution)/shard_map/ppermute | solution.py:454
  42.8 0.0 collective-permute-done.11
  42.8 1.3 %collective-permute-start.16 = (f32[7,16,256]{2,1,0:T(8,128)S(1)}, f32[7,16,256]{2,1,0:T(8,128)S(1)}, u32[]{:S(2)}, u32[]{:S(2)}) collective-permute-start(f32[7,16,256]{2,1,0:T(8,128)S(1)} %collective-permute-done.11), channel_id=1, source_target_pairs={{0,4},{4,0},{8,12},{12,8},{16,20},{20,16},{24,28},{28,24},{1,5},{5... | collective-permute-start | bytes 344072 | tf_op jit(solution)/shard_map/ppermute | solution.py:454
  44.1 0.1 collective-permute-done.13
  44.2 1.0 %collective-permute-start.17 = (f32[7,16,256]{2,1,0:T(8,128)S(1)}, f32[7,16,256]{2,1,0:T(8,128)S(1)}, u32[]{:S(2)}, u32[]{:S(2)}) collective-permute-start(f32[7,16,256]{2,1,0:T(8,128)S(1)} %collective-permute-done.13), channel_id=1, source_target_pairs={{0,4},{4,0},{8,12},{12,8},{16,20},{20,16},{24,28},{28,24},{1,5},{5... | collective-permute-start | bytes 344072 | tf_op jit(solution)/shard_map/ppermute | solution.py:454
  45.3 0.0 collective-permute-done.14
  45.4 1.5 %collective-permute-done.15 = f32[7,16,256]{2,1,0:T(8,128)S(1)} collective-permute-done((f32[7,16,256]{2,1,0:T(8,128)S(1)}, f32[7,16,256]{2,1,0:T(8,128)S(1)}, u32[]{:S(2)}, u32[]{:S(2)}) %collective-permute-start.15) | collective-permute-done | bytes 114720 | tf_op jit(solution)/shard_map/ppermute | solution.py:454
  46.9 1.2 %collective-permute-done.16 = f32[7,16,256]{2,1,0:T(8,128)S(1)} collective-permute-done((f32[7,16,256]{2,1,0:T(8,128)S(1)}, f32[7,16,256]{2,1,0:T(8,128)S(1)}, u32[]{:S(2)}, u32[]{:S(2)}) %collective-permute-start.16) | collective-permute-done | bytes 114720 | tf_op jit(solution)/shard_map/ppermute | solution.py:454
  48.1 0.0 copy-start.2
  48.1 1.2 %collective-permute-done.17 = f32[7,16,256]{2,1,0:T(8,128)S(1)} collective-permute-done((f32[7,16,256]{2,1,0:T(8,128)S(1)}, f32[7,16,256]{2,1,0:T(8,128)S(1)}, u32[]{:S(2)}, u32[]{:S(2)}) %collective-permute-start.17) | collective-permute-done | bytes 114720 | tf_op jit(solution)/shard_map/ppermute | solution.py:454
  49.3 0.0 copy-done.2
  49.3 0.7 %constant_dynamic-update-slice_fusion = f32[7,128,256]{2,1,0:T(8,128)} fusion(f32[7,128,256]{2,1,0:T(8,128)} %copy-done.2, f32[7,16,256]{2,1,0:T(8,128)S(1)} %collective-permute-done.17, s32[]{:T(128)S(6)} %select_n.31), kind=kLoop, calls=%fused_computation.6 | loop fusion | bytes 229380 | tf_op jit(solution)/shard_map/dynamic_update_slice | solution.py:493
  (15 shorter events, 0.1 us)
Async XLA Ops:
  0.0 23.9 %all-to-all-start = ((f32[8,16,8,128]{3,2,1,0:T(8,128)}), f32[8,16,8,128]{3,2,1,0:T(8,128)S(1)}, u32[]{:S(2)}, u32[]{:S(2)}) async-start(f32[8,16,8,128]{3,2,1,0:T(8,128)} %bitcast.14), calls=%async_computation | async-start | bytes 1048576 | tf_op jit(solution)/shard_map/all_to_all | solution.py:480
  8.9 2.2 %collective-permute-start.4 = (f32[24,128]{1,0:T(8,128)S(1)}, f32[24,128]{1,0:T(8,128)S(1)}, u32[]{:S(2)}, u32[]{:S(2)}) collective-permute-start(f32[24,128]{1,0:T(8,128)S(1)} %get-tuple-element.19), channel_id=1, source_target_pairs={{0,1},{1,0},{2,3},{3,2},{4,5},{5,4},{6,7},{7,6},{8,9},{9,8},{10,11... | collective-permute-start | bytes 36872 | tf_op jit(solution)/shard_map/ppermute | solution.py:454
  9.0 5.7 %collective-permute-start = (f32[8,128]{1,0:T(8,128)S(1)}, f32[8,128]{1,0:T(8,128)S(1)}, u32[]{:S(2)}, u32[]{:S(2)}) collective-permute-start(f32[8,128]{1,0:T(8,128)S(1)} %get-tuple-element.16), channel_id=1, source_target_pairs={{0,4},{4,0},{8,12},{12,8},{16,20},{20,16},{24,28},{28,24},{1,5},{5... | collective-permute-start | bytes 12296 | tf_op jit(solution)/shard_map/ppermute | solution.py:454
  11.1 7.4 %collective-permute-start.6 = (f32[24,128]{1,0:T(8,128)S(1)}, f32[24,128]{1,0:T(8,128)S(1)}, u32[]{:S(2)}, u32[]{:S(2)}) collective-permute-start(f32[24,128]{1,0:T(8,128)S(1)} %add.33), channel_id=1, source_target_pairs={{0,2},{1,3},{2,0},{3,1},{4,6},{5,7},{6,4},{7,5},{8,10},{9,11},{10,... | collective-permute-start | bytes 36872 | tf_op jit(solution)/shard_map/ppermute | solution.py:454
  12.6 6.4 %collective-permute-start.7 = (f32[24,128]{1,0:T(8,128)S(1)}, f32[24,128]{1,0:T(8,128)S(1)}, u32[]{:S(2)}, u32[]{:S(2)}) collective-permute-start(f32[24,128]{1,0:T(8,128)S(1)} %add.33), channel_id=1, source_target_pairs={{0,6},{1,7},{2,4},{3,5},{4,2},{5,3},{6,0},{7,1},{8,14},{9,15},{10,... | collective-permute-start | bytes 36872 | tf_op jit(solution)/shard_map/ppermute | solution.py:454
  13.6 5.4 %collective-permute-start.5 = (f32[32,128]{1,0:T(8,128)S(1)}, f32[32,128]{1,0:T(8,128)S(1)}, u32[]{:S(2)}, u32[]{:S(2)}) collective-permute-start(f32[32,128]{1,0:T(8,128)S(1)} %pad_maximum_fusion.1), channel_id=1, source_target_pairs={{0,4},{4,0},{8,12},{12,8},{16,20},{20,16},{24,28},{28,24},{1,5},{5... | collective-permute-start | bytes 49160 | tf_op jit(solution)/shard_map/ppermute | solution.py:454
  14.6 7.8 %collective-permute-start.1 = (f32[2,8,128]{2,1,0:T(8,128)S(1)}, f32[2,8,128]{2,1,0:T(8,128)S(1)}, u32[]{:S(2)}, u32[]{:S(2)}) collective-permute-start(f32[2,8,128]{2,1,0:T(8,128)S(1)} %pad_maximum_fusion.2.refs_0_), channel_id=1, source_target_pairs={{0,8},{4,12},{8,0},{12,4},{16,24},{20,28},{24,16},{28,20},{1,9},{5... | collective-permute-start | bytes 24584 | tf_op jit(solution)/shard_map/ppermute | solution.py:454
  16.1 7.5 %collective-permute-start.2 = (f32[2,8,128]{2,1,0:T(8,128)S(1)}, f32[2,8,128]{2,1,0:T(8,128)S(1)}, u32[]{:S(2)}, u32[]{:S(2)}) collective-permute-start(f32[2,8,128]{2,1,0:T(8,128)S(1)} %pad_maximum_fusion.2.refs_0_), channel_id=1, source_target_pairs={{0,16},{4,20},{8,24},{12,28},{16,0},{20,4},{24,8},{28,12},{1,17},{... | collective-permute-start | bytes 24584 | tf_op jit(solution)/shard_map/ppermute | solution.py:454
  18.4 5.4 %collective-permute-start.3 = (f32[2,8,128]{2,1,0:T(8,128)S(1)}, f32[2,8,128]{2,1,0:T(8,128)S(1)}, u32[]{:S(2)}, u32[]{:S(2)}) collective-permute-start(f32[2,8,128]{2,1,0:T(8,128)S(1)} %pad_maximum_fusion.2.refs_0_), channel_id=1, source_target_pairs={{0,24},{4,28},{8,16},{12,20},{16,8},{20,12},{24,0},{28,4},{1,25},{... | collective-permute-start | bytes 24584 | tf_op jit(solution)/shard_map/ppermute | solution.py:454
  19.1 4.8 %copy-start = (s32[8]{0:T(128)S(1)}, s32[8]{0:T(128)}, u32[]{:S(2)}) copy-start(s32[8]{0:T(128)} %slab_rows.3) | copy-start | bytes 100
  19.1 4.8 %copy-start.1 = (s32[3]{0:T(128)S(1)}, s32[3]{0:T(128)}, u32[]{:S(2)}) copy-start(s32[3]{0:T(128)} %split_bin.1) | copy-start | bytes 40
  19.1 9.4 %collective-permute-start.10 = (f32[2,32,128]{2,1,0:T(8,128)S(1)}, f32[2,32,128]{2,1,0:T(8,128)S(1)}, u32[]{:S(2)}, u32[]{:S(2)}) collective-permute-start(f32[2,32,128]{2,1,0:T(8,128)S(1)} %pad_maximum_fusion.refs_0_), channel_id=1, source_target_pairs={{0,24},{4,28},{8,16},{12,20},{16,8},{20,12},{24,0},{28,4},{1,25},{... | collective-permute-start | bytes 98312 | tf_op jit(solution)/shard_map/ppermute | solution.py:454
  22.4 6.1 %collective-permute-start.8 = (f32[2,32,128]{2,1,0:T(8,128)S(1)}, f32[2,32,128]{2,1,0:T(8,128)S(1)}, u32[]{:S(2)}, u32[]{:S(2)}) collective-permute-start(f32[2,32,128]{2,1,0:T(8,128)S(1)} %pad_maximum_fusion.refs_0_), channel_id=1, source_target_pairs={{0,8},{4,12},{8,0},{12,4},{16,24},{20,28},{24,16},{28,20},{1,9},{5... | collective-permute-start | bytes 98312 | tf_op jit(solution)/shard_map/ppermute | solution.py:454
  22.4 6.1 %collective-permute-start.9 = (f32[2,32,128]{2,1,0:T(8,128)S(1)}, f32[2,32,128]{2,1,0:T(8,128)S(1)}, u32[]{:S(2)}, u32[]{:S(2)}) collective-permute-start(f32[2,32,128]{2,1,0:T(8,128)S(1)} %pad_maximum_fusion.refs_0_), channel_id=1, source_target_pairs={{0,16},{4,20},{8,24},{12,28},{16,0},{20,4},{24,8},{28,12},{1,17},{... | collective-permute-start | bytes 98312 | tf_op jit(solution)/shard_map/ppermute | solution.py:454
  33.9 8.9 %collective-permute-start.11 = (f32[7,16,256]{2,1,0:T(8,128)S(1)}, f32[7,16,256]{2,1,0:T(8,128)S(1)}, u32[]{:S(2)}, u32[]{:S(2)}) collective-permute-start(f32[7,16,256]{2,1,0:T(8,128)S(1)} %gains.1), channel_id=1, source_target_pairs={{0,16},{4,20},{8,24},{12,28},{16,0},{20,4},{24,8},{28,12},{1,17},{... | collective-permute-start | bytes 344072 | tf_op jit(solution)/shard_map/ppermute | solution.py:454
  35.5 6.6 %collective-permute-start.12 = (f32[7,16,256]{2,1,0:T(8,128)S(1)}, f32[7,16,256]{2,1,0:T(8,128)S(1)}, u32[]{:S(2)}, u32[]{:S(2)}) collective-permute-start(f32[7,16,256]{2,1,0:T(8,128)S(1)} %gains.1), channel_id=1, source_target_pairs={{0,8},{4,12},{8,0},{12,4},{16,24},{20,28},{24,16},{28,20},{1,9},{5... | collective-permute-start | bytes 344072 | tf_op jit(solution)/shard_map/ppermute | solution.py:454
  37.5 6.7 %collective-permute-start.13 = (f32[7,16,256]{2,1,0:T(8,128)S(1)}, f32[7,16,256]{2,1,0:T(8,128)S(1)}, u32[]{:S(2)}, u32[]{:S(2)}) collective-permute-start(f32[7,16,256]{2,1,0:T(8,128)S(1)} %gains.1), channel_id=1, source_target_pairs={{0,24},{4,28},{8,16},{12,20},{16,8},{20,12},{24,0},{28,4},{1,25},{... | collective-permute-start | bytes 344072 | tf_op jit(solution)/shard_map/ppermute | solution.py:454
  38.4 6.9 %collective-permute-start.14 = (f32[7,16,256]{2,1,0:T(8,128)S(1)}, f32[7,16,256]{2,1,0:T(8,128)S(1)}, u32[]{:S(2)}, u32[]{:S(2)}) collective-permute-start(f32[7,16,256]{2,1,0:T(8,128)S(1)} %gains.1), channel_id=1, source_target_pairs={{0,4},{4,0},{8,12},{12,8},{16,20},{20,16},{24,28},{28,24},{1,5},{5... | collective-permute-start | bytes 344072 | tf_op jit(solution)/shard_map/ppermute | solution.py:454
  42.1 4.8 %collective-permute-start.15 = (f32[7,16,256]{2,1,0:T(8,128)S(1)}, f32[7,16,256]{2,1,0:T(8,128)S(1)}, u32[]{:S(2)}, u32[]{:S(2)}) collective-permute-start(f32[7,16,256]{2,1,0:T(8,128)S(1)} %collective-permute-done.12), channel_id=1, source_target_pairs={{0,4},{4,0},{8,12},{12,8},{16,20},{20,16},{24,28},{28,24},{1,5},{5... | collective-permute-start | bytes 344072 | tf_op jit(solution)/shard_map/ppermute | solution.py:454
  42.8 5.3 %collective-permute-start.16 = (f32[7,16,256]{2,1,0:T(8,128)S(1)}, f32[7,16,256]{2,1,0:T(8,128)S(1)}, u32[]{:S(2)}, u32[]{:S(2)}) collective-permute-start(f32[7,16,256]{2,1,0:T(8,128)S(1)} %collective-permute-done.11), channel_id=1, source_target_pairs={{0,4},{4,0},{8,12},{12,8},{16,20},{20,16},{24,28},{28,24},{1,5},{5... | collective-permute-start | bytes 344072 | tf_op jit(solution)/shard_map/ppermute | solution.py:454
  44.2 5.1 %collective-permute-start.17 = (f32[7,16,256]{2,1,0:T(8,128)S(1)}, f32[7,16,256]{2,1,0:T(8,128)S(1)}, u32[]{:S(2)}, u32[]{:S(2)}) collective-permute-start(f32[7,16,256]{2,1,0:T(8,128)S(1)} %collective-permute-done.13), channel_id=1, source_target_pairs={{0,4},{4,0},{8,12},{12,8},{16,20},{20,16},{24,28},{28,24},{1,5},{5... | collective-permute-start | bytes 344072 | tf_op jit(solution)/shard_map/ppermute | solution.py:454
  48.1 1.2 %copy-start.2 = (f32[7,128,256]{2,1,0:T(8,128)}, f32[7,128,256]{2,1,0:T(8,128)S(1)}, u32[]{:S(2)}) copy-start(f32[7,128,256]{2,1,0:T(8,128)S(1)} %constant_dynamic-update-slice_fusion.1) | copy-start | bytes 2752516
